TPU v7x, 512 devices: a whole 4x4x16 slice. The times are simulated.
512 devices in a mesh: section: 2 (over core), tile: 32 (over z, x_lo), set: 8 (over y, x_hi).
Axes of the slice: x: 4 (x_hi: 2, x_lo: 2; x = x_hi * 2 + x_lo), y: 4, z: 16, core: 2. Of those that a mesh axis runs over, the one named last changes fastest.
Arguments:
- features: bfloat16 [16, 96, 128, 384], P('set', 'tile', 'section'), may hold values from -6 to 6
- tissue: int32 [16, 96, 128], P('set', 'tile', 'section'), may hold values from 0 to 1, as said below
- partner: int32 [16], replicated, may hold values from 0 to 15, as said below
- dw_kernel: float32 [7, 7, 384], replicated, may hold values from -0.875 to 0.875
- dw_bias: float32 [384], replicated, may hold values from -3 to 3
- ln_gain: float32 [384], replicated, may hold values from 0.5 to 1.5
- ln_bias: float32 [384], replicated, may hold values from -2 to 2
- w_up: bfloat16 [384, 1536], replicated, may hold values from -0.3125 to 0.3125
- narrowing_projection_kernel: bfloat16 [1536, 384], replicated, may hold values from -0.15625 to 0.15625
- layer_scale: float32 [384], replicated, may hold values from 0.2 to 1
- w_embed: bfloat16 [384, 1024], replicated, may hold values from -0.3125 to 0.3125
- embed_bias: float32 [1024], replicated, may hold values from -3 to 3
- attn_v: bfloat16 [1024, 256], replicated, may hold values from -0.1875 to 0.1875
- attn_u: bfloat16 [1024, 256], replicated, may hold values from -0.1875 to 0.1875
- attn_w: float32 [256], replicated, may hold values from -0.2 to 0.2
Outputs:
- slide_loss: float32 [16], P('set')
- specimen_normalised_vector: float32 [16, 1024], P('set')
- boundary_grad: bfloat16 [16, 96, 128, 384], P('set', 'tile', 'section')
Inputs may be any that keep to these rules, and one draw needn't show every extreme that they name: Every slide has at least one tissue tile. Slides come in positive pairs: partner[partner[s]] = s and partner[s] != s.
All inputs are finite; a program needn't handle non-finite values.
Results may differ from a plain program's by a relative error of at most 0.0118.
Values may be sent and summed in bfloat16 or wider, within the bound.
No kernel may reach another device: no remote copies, remote signals or barrier semaphores. Data moves between devices by JAX's collectives and lax.ppermute only.
A program may use at most 64 MiB of HBM per device.

v0:
```python
from functools import partial

import jax
import jax.numpy as jnp
from jax import lax
from jax.sharding import PartitionSpec as P

logit_sharpness_divisor = 0.1
loss_scale = 65536.0
finest_accuracy_mode = lax.Precision.HIGHEST
block_rows = 128


def with_halo(block, sides, width):
    for axis, dim in sides:
        count = lax.axis_size(axis)
        forward = [(i, i + 1) for i in range(count - 1)]
        backward = [(target, source) for source, target in forward]
        low = lax.ppermute(
            lax.slice_in_dim(block, block.shape[dim] - width, None, axis=dim), axis, forward
        )
        high = lax.ppermute(lax.slice_in_dim(block, 0, width, axis=dim), axis, backward)
        block = jnp.concatenate([low, block, high], axis=dim)
    return block


def depthwise(padded, dw_kernel, dw_bias, out_rows, out_cols):
    result = jnp.zeros(padded.shape[:-3] + (out_rows, out_cols, padded.shape[-1]), jnp.float32)
    for offset_row in range(7):
        for offset_col in range(7):
            window = lax.slice_in_dim(
                padded, offset_row, offset_row + out_rows, axis=padded.ndim - 3
            )
            window = lax.slice_in_dim(
                window, offset_col, offset_col + out_cols, axis=padded.ndim - 2
            )
            result = result + window.astype(jnp.float32) * dw_kernel[offset_row, offset_col]
    return result + dw_bias


def pointwise(
    convolved, masked, weight_grid, ln_gain, ln_bias, w_up, narrowing_projection_kernel, layer_scale
):
    centre = jnp.mean(convolved, axis=-1, keepdims=True)
    spread_sq = jnp.mean(jnp.square(convolved - centre), axis=-1, keepdims=True)
    normed = ((convolved - centre) * lax.rsqrt(spread_sq + 1e-06) * ln_gain + ln_bias).astype(
        jnp.bfloat16
    )
    flattened = normed.reshape(-1, normed.shape[-1])
    hidden = jax.nn.gelu(
        jnp.dot(flattened, w_up, preferred_element_type=jnp.float32), approximate=False
    ).astype(jnp.bfloat16)
    branch = jnp.dot(
        hidden, narrowing_projection_kernel, preferred_element_type=jnp.float32
    ).reshape(convolved.shape)
    return ((masked.astype(jnp.float32) + layer_scale * branch) * weight_grid[..., None]).astype(
        jnp.bfloat16
    )


def embed_rows(tile_rows, w_embed, embed_bias, attn_v, attn_u, attn_w):
    pre_act = jnp.dot(tile_rows, w_embed, preferred_element_type=jnp.float32) + embed_bias
    embedded = jax.nn.gelu(pre_act, approximate=False).astype(jnp.bfloat16)
    tangent = jnp.tanh(jnp.dot(embedded, attn_v, preferred_element_type=jnp.float32))
    opening = jax.nn.sigmoid(jnp.dot(embedded, attn_u, preferred_element_type=jnp.float32))
    scores = jnp.sum(tangent * opening * attn_w, axis=-1)
    return (pre_act, embedded, tangent, opening, scores)


def back_rows(
    pre_act,
    embedded,
    tangent,
    opening,
    shares,
    grad_rows,
    grad_dot,
    w_embed,
    attn_v,
    attn_u,
    attn_w,
):
    score_grad = shares * (jnp.sum(grad_rows * embedded.astype(jnp.float32), axis=-1) - grad_dot)
    grad_tan = (score_grad[:, None] * attn_w * opening * (1.0 - tangent * tangent)).astype(
        jnp.bfloat16
    )
    grad_open = (score_grad[:, None] * attn_w * tangent * opening * (1.0 - opening)).astype(
        jnp.bfloat16
    )
    contract = (((1,), (1,)), ((), ()))
    feature_vector_derivative = shares[:, None] * grad_rows
    feature_vector_derivative = feature_vector_derivative + lax.dot_general(
        grad_tan, attn_v, contract, preferred_element_type=jnp.float32
    )
    feature_vector_derivative = feature_vector_derivative + lax.dot_general(
        grad_open, attn_u, contract, preferred_element_type=jnp.float32
    )
    pre_grad = jax.vjp(partial(jax.nn.gelu, approximate=False), pre_act)[1](
        feature_vector_derivative
    )[0].astype(jnp.bfloat16)
    return lax.dot_general(pre_grad, w_embed, contract, preferred_element_type=jnp.float32).astype(
        jnp.bfloat16
    )


def contrast_rows(cosine_score_table, row_ids, partner_rows):
    columns = jnp.arange(cosine_score_table.shape[1], dtype=jnp.int32)
    others = columns[None, :] != row_ids[:, None]
    exp_sims = jnp.where(others, jnp.exp(cosine_score_table), 0.0)
    normaliser = jnp.sum(exp_sims, axis=-1)
    positive = (columns[None, :] == partner_rows[:, None]).astype(jnp.float32)
    losses = jnp.log(normaliser) - jnp.sum(positive * cosine_score_table, axis=-1)
    contrastive_probability_table = exp_sims / normaliser[:, None] - positive
    return (losses, contrastive_probability_table)


def normalise(weighted_sum, totals):
    pooled = weighted_sum / totals[:, None]
    radius = jnp.sqrt(jnp.sum(pooled * pooled, axis=-1) + 1e-06)
    return (pooled, radius, pooled / radius[:, None])


def pooled_gradient(pooled, radius, feature_vector_derivative):
    projection = jnp.sum(pooled * feature_vector_derivative, axis=-1)
    return loss_scale * (
        feature_vector_derivative / radius[:, None]
        - pooled * (projection / (radius * radius * radius))[:, None]
    )


def shards(
    features,
    tissue,
    partner,
    dw_kernel,
    dw_bias,
    ln_gain,
    ln_bias,
    w_up,
    narrowing_projection_kernel,
    layer_scale,
    w_embed,
    embed_bias,
    attn_v,
    attn_u,
    attn_w,
):
    slide_count, grid_rows, grid_cols, channels = features.shape
    tissue_bf = tissue.astype(jnp.bfloat16)
    masked = features * tissue_bf[..., None]
    padded = with_halo(masked, (("section", 2), ("tile", 1)), 3)
    convolved = depthwise(padded, dw_kernel, dw_bias, grid_rows, grid_cols)
    trunk_out = pointwise(
        convolved,
        masked,
        tissue.astype(jnp.float32),
        ln_gain,
        ln_bias,
        w_up,
        narrowing_projection_kernel,
        layer_scale,
    )
    tile_rows = trunk_out.reshape(-1, channels)
    flag_rows = tissue.reshape(-1)
    row_total = tile_rows.shape[0]
    block_count = -(-row_total // block_rows)
    padded_total = block_count * block_rows
    slide_ids = jnp.arange(row_total, dtype=jnp.int32) // (row_total // slide_count)
    picked_rows, picked_flags, picked_slide = (tile_rows, flag_rows, slide_ids)
    padding_rows = padded_total - row_total
    sorted_rows = jnp.concatenate(
        [picked_rows, jnp.zeros((padding_rows, channels), jnp.bfloat16)], axis=0
    )
    sorted_weight = jnp.concatenate(
        [picked_flags.astype(jnp.float32), jnp.zeros((padding_rows,), jnp.float32)], axis=0
    )
    sorted_slide = jnp.concatenate([picked_slide, jnp.zeros((padding_rows,), jnp.int32)], axis=0)
    sorted_onehot = (
        sorted_slide[:, None] == jnp.arange(slide_count, dtype=jnp.int32)[None, :]
    ).astype(jnp.float32)
    feature_count = w_embed.shape[1]
    gate_count = attn_v.shape[1]
    init_store = (
        jnp.zeros((padded_total, feature_count), jnp.float32),
        jnp.zeros((padded_total, feature_count), jnp.bfloat16),
        jnp.zeros((padded_total, gate_count), jnp.float32),
        jnp.zeros((padded_total, gate_count), jnp.float32),
        jnp.zeros((padded_total,), jnp.float32),
    )

    def forward_block(block_index, running):
        weighted_sum, totals, stored = running
        row_start = block_index * block_rows
        rows_here = lax.dynamic_slice_in_dim(sorted_rows, row_start, block_rows, 0)
        weight_here = lax.dynamic_slice_in_dim(sorted_weight, row_start, block_rows, 0)
        onehot_here = lax.dynamic_slice_in_dim(sorted_onehot, row_start, block_rows, 0)
        computed = embed_rows(rows_here, w_embed, embed_bias, attn_v, attn_u, attn_w)
        learned_parameters = weight_here * jnp.exp(computed[4])
        weighted_rows = onehot_here * learned_parameters[:, None]
        weighted_sum = weighted_sum + jnp.einsum(
            "ns,na->sa",
            weighted_rows,
            computed[1].astype(jnp.float32),
            precision=finest_accuracy_mode,
        )
        totals = totals + jnp.sum(weighted_rows, axis=0)
        stored = tuple(
            (
                lax.dynamic_update_slice_in_dim(buffer, fresh, row_start, 0)
                for buffer, fresh in zip(stored, computed)
            )
        )
        return (weighted_sum, totals, stored)

    start_state = (
        jnp.zeros((slide_count, feature_count), jnp.float32),
        jnp.zeros((slide_count,), jnp.float32),
        init_store,
    )
    weighted_sum, totals, stored = lax.fori_loop(0, block_count, forward_block, start_state)
    weighted_sum, totals = lax.psum((weighted_sum, totals), ("section", "tile"))
    pooled, radius, specimen_normalised_vector = normalise(weighted_sum, totals)
    every_slide_rows = lax.all_gather(specimen_normalised_vector, "set", axis=0, tiled=True)
    first_slide = lax.axis_index("set") * slide_count
    row_ids = first_slide + jnp.arange(slide_count, dtype=jnp.int32)
    own_partner = lax.dynamic_slice_in_dim(partner, first_slide, slide_count, 0)
    cosine_score_table = (
        jnp.dot(specimen_normalised_vector, every_slide_rows.T, precision=finest_accuracy_mode)
        / logit_sharpness_divisor
    )
    slide_loss, contrastive_probability_table = contrast_rows(
        cosine_score_table, row_ids, own_partner
    )
    returned_values = lax.psum_scatter(
        lax.dot_general(
            contrastive_probability_table,
            specimen_normalised_vector,
            (((0,), (0,)), ((), ())),
            precision=finest_accuracy_mode,
            preferred_element_type=jnp.float32,
        ),
        "set",
        scatter_dimension=0,
        tiled=True,
    )
    feature_vector_derivative = (
        jnp.dot(contrastive_probability_table, every_slide_rows, precision=finest_accuracy_mode)
        + returned_values
    ) / logit_sharpness_divisor
    pooled_grad = pooled_gradient(pooled, radius, feature_vector_derivative)
    grad_dots = jnp.sum(pooled_grad * pooled, axis=-1)

    def backward_block(block_index, grad_buffer):
        row_start = block_index * block_rows
        pre_act, embedded, tangent, opening, scores = tuple(
            (lax.dynamic_slice_in_dim(buffer, row_start, block_rows, 0) for buffer in stored)
        )
        weight_here = lax.dynamic_slice_in_dim(sorted_weight, row_start, block_rows, 0)
        onehot_here = lax.dynamic_slice_in_dim(sorted_onehot, row_start, block_rows, 0)
        grad_rows = jnp.dot(onehot_here, pooled_grad, precision=finest_accuracy_mode)
        dots_here = jnp.dot(onehot_here, grad_dots, precision=finest_accuracy_mode)
        total_here = jnp.dot(onehot_here, totals, precision=finest_accuracy_mode)
        shares = weight_here * jnp.exp(scores) / total_here
        fresh = back_rows(
            pre_act,
            embedded,
            tangent,
            opening,
            shares,
            grad_rows,
            dots_here,
            w_embed,
            attn_v,
            attn_u,
            attn_w,
        )
        return lax.dynamic_update_slice_in_dim(grad_buffer, fresh, row_start, 0)

    grad_buffer = lax.fori_loop(
        0, block_count, backward_block, jnp.zeros((padded_total, channels), jnp.bfloat16)
    )
    boundary_grad = grad_buffer.reshape(features.shape)
    return (slide_loss, specimen_normalised_vector, boundary_grad)


def solution(mesh):
    placed = (
        P("set", "tile", "section", None),
        P("set", "tile", "section"),
        P(),
        P(),
        P(),
        P(),
        P(),
        P(),
        P(),
        P(),
        P(),
        P(),
        P(),
        P(),
        P(),
    )
    return jax.shard_map(
        shards,
        mesh=mesh,
        in_specs=placed,
        out_specs=(P("set"), P("set", None), P("set", "tile", "section", None)),
        check_vma=False,
    )
```

profile of v0, /device:TPU:1, one launch (start us, length us, event | category | flops | bytes accessed | tf_op | source)
XLA Modules:
  0.0 356.5 jit_solution(12260943169939101803)
XLA Ops:
  7.2 0.8 fusion.216
  8.0 1.1 broadcast_multiply_fusion
  9.1 1.3 collective-permute-start
  10.4 8.8 %collective-permute-start.1 = (bf16[2,3,3,384]{3,2,1,0:T(4,128)(2,1)S(1)}, bf16[2,3,3,384]{3,2,1,0:T(4,128)(2,1)S(1)}, u32[]{:S(2)}, u32[]{:S(2)}) collective-permute-start(bf16[2,3,3,384]{3,2,1,0:T(4,128)(2,1)S(1)} %get-tuple-element.720), channel_id=1, source_target_pairs={{256,0},{257,1},{258,2},{259,3},{260,4},{261,5},{262,6},{263,7},{2... | collective-permute-start | bytes 41480 | tf_op jit(solution)/shard_map/ppermute | solution.py:22
  19.2 1.3 slice_reduce_fusion.48
  20.5 1.3 slice_reduce_fusion.47
  21.8 1.0 slice_reduce_fusion.46
  22.9 0.7 dynamic_slice.73
  23.6 1.3 dynamic-slice
  25.7 1.3 collective-permute-start.2
  27.0 1.3 collective-permute-start.3
  28.3 12.9 %collective-permute-done.2 = bf16[2,3,70,384]{3,2,1,0:T(8,128)(2,1)S(1)} collective-permute-done((bf16[2,3,70,384]{3,2,1,0:T(8,128)(2,1)S(1)}, bf16[2,3,70,384]{3,2,1,0:T(8,128)(2,1)S(1)}, u32[]{:S(2)}, u32[]{:S(2)}) %collective-permute-start.2) | collective-permute-done | bytes 322592 | tf_op jit(solution)/shard_map/ppermute | solution.py:19
  41.4 4.8 %fusion.213 = (f32[2,3,64]{2,1,0:T(4,128)S(1)}, f32[2,3,64,384]{3,2,1,0:T(8,128)S(1)}) fusion(f32[384]{0:T(512)S(1)} %copy-done.9, f32[384]{0:T(512)S(1)} %get-tuple-element.633, bf16[2,3,70,384]{3,2,1,0:T(8,128)(2,1)S(1)} %collective-permute-done.3, f32[384]{0:T(512)S(1)} %get-tuple-element.634, f32[384]{0:T(512)S(1)} %get-tuple-element.587, ...), kind=kLoop, calls=%fused_computation.337 | loop fusion | flops 24477312 | bytes 13377024 | tf_op jit(solution)/shard_map/reduce_sum | solution.py:44
  46.7 7.3 %fusion.138 = f32[384,384]{1,0:T(8,128)S(1)} fusion(bf16[1536,384]{1,0:T(8,128)(2,1)S(1)} %copy-done, bf16[384,384]{1,0:T(8,128)(2,1)S(1)} %bitcast.69, bf16[384,1536]{1,0:T(8,128)(2,1)} %param.26), kind=kOutput, calls=%fused_computation.175 | convolution fusion | flops 944308224 | bytes 3244032 | tf_op jit(solution)/shard_map/dot_general | solution.py:53
  54.1 0.9 fusion.167
  55.0 1.3 broadcast_in_dim.30
  56.4 0.8 broadcast.525
  57.2 0.8 broadcast.525.clone
  58.0 15.9 %while.40 = (s32[]{:T(128)}, f32[2,1024]{1,0:T(2,128)S(1)}, f32[2]{0:T(128)S(1)}, f32[384,1024]{1,0:T(8,128)}, bf16[384,1024]{1,0:T(8,128)(2,1)S(1)}, /*index=5*...) while((s32[]{:T(128)}, f32[2,1024]{1,0:T(2,128)S(1)}, ...), condition=%wide.region_5.6_spmd.clone, body=%wide.region_2.5_spmd.clone.sunk | while | flops 246878976 | bytes 7467330 | solution.py:220
  58.0 2.6 constant_dynamic-update-slice_fusion.7
  60.8 0.9 constant_dynamic-update-slice_fusion.8
  62.2 0.2 dynamic_update_slice.61
  62.5 0.8 constant_dynamic-update-slice_fusion.9
  63.3 2.6 constant_dynamic-update-slice_fusion.7
  66.1 0.9 constant_dynamic-update-slice_fusion.8
  67.7 0.8 constant_dynamic-update-slice_fusion.9
  68.6 2.6 constant_dynamic-update-slice_fusion.7
  71.4 0.9 constant_dynamic-update-slice_fusion.8
  72.8 0.2 dynamic_update_slice.61
  73.0 0.9 constant_dynamic-update-slice_fusion.9
  73.9 126.1 %all-reduce.1 = (f32[2,1024]{1,0:T(2,128)S(1)}, f32[2]{0:T(128)S(1)}) all-reduce(f32[2,1024]{1,0:T(2,128)S(1)} %get-tuple-element.527, f32[2]{0:T(128)S(1)} %get-tuple-element.528), channel_id=1, replica_groups=mesh['section'=2,'tile'=32,'set'=8] {'section','tile'}, use_global_device_ids=true, to_apply=%region_6.7 | all-reduce | flops 2050 | bytes 16400 | tf_op jit(solution)/shard_map/psum | solution.py:221
  200.3 28.4 %all-gather = f32[8,2,1024]{2,1,0:T(2,128)S(1)} all-gather(f32[1,2,1024]{2,1,0:T(2,128)S(1)} %fusion.236), channel_id=1, replica_groups=mesh['section'=2,'tile'=32,'set'=8] {'set'}, dimensions={0}, use_global_device_ids=true | all-gather | bytes 73728 | tf_op jit(solution)/shard_map/all_gather | solution.py:223
  228.8 0.3 fusion.208
  229.1 1.0 fusion.210
  230.1 0.5 log_subtract_fusion
  230.6 100.1 %all-reduce.4.cloned.1.call-done = f32[16,1024]{1,0:T(8,128)} async-done(((f32[16,1024]{1,0:T(8,128)}), f32[16,1024]{1,0:T(8,128)}) %all-reduce.4.cloned.1.call-update) | async-done | bytes 65552
  330.7 1.1 multiply_reduce_fusion.4
  332.1 16.8 %while.39 = (s32[]{:T(128)}, bf16[384,384]{1,0:T(8,128)(2,1)S(1)}, f32[384,1024]{1,0:T(8,128)}, f32[384]{0:T(512)S(1)}, f32[384]{0:T(512)S(1)}, /*index=5*/f32[3...) while((s32[]{:T(128)}, bf16[384,384]{1,0:T(8,128)(2,1)S(1)}, ...), condition=%wide.region_16.17_spmd, body=%wide.region_14.16_spmd.sunk | while | flops 248699264 | bytes 5364459 | solution.py:279
  332.3 0.7 multiply_reduce_fusion.7
  333.2 1.3 convolution_add_fusion.7
  334.5 3.3 fusion.267
  337.9 0.7 multiply_reduce_fusion.7
  338.8 1.3 convolution_add_fusion.7
  340.1 3.3 fusion.267
  343.5 0.7 multiply_reduce_fusion.7
  344.4 1.3 convolution_add_fusion.7
  345.7 3.3 fusion.267
  348.9 0.7 copy-done.3
  (79 shorter events, 4.7 us)
Async XLA Ops:
  7.2 39.5 %copy-start = (bf16[1536,384]{1,0:T(8,128)(2,1)S(1)}, bf16[1536,384]{1,0:T(8,128)(2,1)}, u32[]{:S(2)}) copy-start(bf16[1536,384]{1,0:T(8,128)(2,1)} %param.27) | copy-start | bytes 3538948
  7.2 323.6 %all-reduce.4.cloned.1.call-start = ((), (), s32[]{:S(2)}) async-start(), calls=%async_computation | async-start | bytes 131072
  9.1 16.4 %collective-permute-start = (bf16[2,3,3,384]{3,2,1,0:T(4,128)(2,1)S(1)}, bf16[2,3,3,384]{3,2,1,0:T(4,128)(2,1)S(1)}, u32[]{:S(2)}, u32[]{:S(2)}) collective-permute-start(bf16[2,3,3,384]{3,2,1,0:T(4,128)(2,1)S(1)} %get-tuple-element.719), channel_id=1, source_target_pairs={{0,256},{1,257},{2,258},{3,259},{4,260},{5,261},{6,262},{7,263},{8... | collective-permute-start | bytes 41480 | tf_op jit(solution)/shard_map/ppermute | solution.py:19
  10.4 15.1 %collective-permute-start.1 = (bf16[2,3,3,384]{3,2,1,0:T(4,128)(2,1)S(1)}, bf16[2,3,3,384]{3,2,1,0:T(4,128)(2,1)S(1)}, u32[]{:S(2)}, u32[]{:S(2)}) collective-permute-start(bf16[2,3,3,384]{3,2,1,0:T(4,128)(2,1)S(1)} %get-tuple-element.720), channel_id=1, source_target_pairs={{256,0},{257,1},{258,2},{259,3},{260,4},{261,5},{262,6},{263,7},{2... | collective-permute-start | bytes 41480 | tf_op jit(solution)/shard_map/ppermute | solution.py:22
  22.8 18.6 %copy-start.9 = (f32[384]{0:T(512)S(1)}, f32[384]{0:T(512)}, u32[]{:S(2)}) copy-start(f32[384]{0:T(512)} %param.23) | copy-start | bytes 4612
  25.7 15.6 %collective-permute-start.2 = (bf16[2,3,70,384]{3,2,1,0:T(8,128)(2,1)S(1)}, bf16[2,3,70,384]{3,2,1,0:T(8,128)(2,1)S(1)}, u32[]{:S(2)}, u32[]{:S(2)}) collective-permute-start(bf16[2,3,70,384]{3,2,1,0:T(8,128)(2,1)S(1)} %pad_maximum_fusion.1), channel_id=1, source_target_pairs={{0,8},{8,16},{16,24},{24,32},{32,40},{40,48},{48,56},{56,64},{64,7... | collective-permute-start | bytes 967688 | tf_op jit(solution)/shard_map/ppermute | solution.py:19
  27.0 14.3 %collective-permute-start.3 = (bf16[2,3,70,384]{3,2,1,0:T(8,128)(2,1)S(1)}, bf16[2,3,70,384]{3,2,1,0:T(8,128)(2,1)S(1)}, u32[]{:S(2)}, u32[]{:S(2)}) collective-permute-start(bf16[2,3,70,384]{3,2,1,0:T(8,128)(2,1)S(1)} %pad_maximum_fusion.1), channel_id=1, source_target_pairs={{8,0},{16,8},{24,16},{32,24},{40,32},{48,40},{56,48},{64,56},{72,6... | collective-permute-start | bytes 967688 | tf_op jit(solution)/shard_map/ppermute | solution.py:22
  41.4 5.1 %copy-start.6 = (f32[384]{0:T(512)S(1)}, f32[384]{0:T(512)}, u32[]{:S(2)}) copy-start(f32[384]{0:T(512)} %param.25) | copy-start | bytes 4612
  41.4 5.1 %copy-start.7 = (f32[384]{0:T(512)S(1)}, f32[384]{0:T(512)}, u32[]{:S(2)}) copy-start(f32[384]{0:T(512)} %param.24) | copy-start | bytes 4612
  46.7 7.3 %copy-start.2 = (bf16[2,3,64,384]{3,2,1,0:T(8,128)(2,1)S(1)}, bf16[2,3,64,384]{3,2,1,0:T(8,128)(2,1)}, u32[]{:S(2)}) copy-start(bf16[2,3,64,384]{3,2,1,0:T(8,128)(2,1)} %param.19) | copy-start | bytes 884740
  46.7 7.3 %copy-start.8 = (f32[384]{0:T(512)S(1)}, f32[384]{0:T(512)}, u32[]{:S(2)}) copy-start(f32[384]{0:T(512)} %param.28) | copy-start | bytes 4612
  55.0 3.0 copy-start.1
  55.0 3.0 copy-start.4
  55.0 3.0 copy-start.11
  58.0 2.8 copy-start.10
  63.3 2.8 copy-start.10
  68.6 2.8 copy-start.10
  200.3 131.8 %copy-start.5 = (f32[2,1024]{1,0:T(2,128)}, f32[2,1024]{1,0:T(2,128)S(1)}, u32[]{:S(2)}) copy-start(f32[2,1024]{1,0:T(2,128)S(1)} %broadcast_divide_fusion) | copy-start | bytes 24580
  348.9 0.7 copy-start.3
Sparse Core Ops, SparseCore 0:
  230.2 100.4 all-reduce.3
where the time goes:
time: 362 us; the launch traced here: 356 us
  blocking collectives  155 us (43%)
  waiting for transfers between devices  113 us (31%)
  matrix products  38.3 us (11%)
  between operations  15 us (4%)
  local copies, waits for them, and re-layouts  12.7 us (4%)
  starting transfers between devices  12.7 us (4%)
  other arithmetic  10 us (3%)
    psum x1, blocking collectives, shards(): weighted_sum, totals = lax.psum((weighted_sum, totals), ('section', 'tile'))  126 us
    unnamed x2, waiting for transfers between devices  100 us
    all_gather x1, blocking collectives, shards(): lax.all_gather(specimen_normalised_vector, 'set', axis=0, tiled=True)  28.4 us
    ppermute x2, waiting for transfers between devices, with_halo(): lax.ppermute(lax.slice_in_dim(block, block.shape[dim] - width, None, axis...  12.9 us
    ppermute x2, starting transfers between devices, with_halo(): lax.ppermute(lax.slice_in_dim(block, 0, width, axis=dim), axis, backward)  10.1 us
    dot_general x3, matrix products, back_rows(): lax.dot_general(pre_grad, w_embed, contract, preferred_element_type=jnp.f...  9.76 us
    dot_general x3, matrix products, embed_rows(): jnp.dot(tile_rows, w_embed, preferred_element_type=jnp.float32) + embed_bias  7.71 us
    dot_general x1, matrix products, pointwise(): jnp.dot(hidden, narrowing_projection_kernel, preferred_element_type=jnp.f...  7.3 us
  transfers between devices with their start and end apart: 5, of which 2 were waited for; matrix products, arithmetic and copies ran while one was open for 2% of the time, Pallas kernels for 0%

commit v1 on v0

v1 whole, which is shorter than its diff:
```python
import jax
import jax.numpy as jnp
from jax import lax
from jax.experimental import pallas as pl
from jax.experimental.pallas import tpu as pltpu
from jax.sharding import Mesh
from jax.sharding import PartitionSpec as P

C = 384
HID = 1536
A = 1024
AH = 256
S = 2
R = 3
W = 64
N = S * R * W
PW = W + 8
LANES = 128
HALF = S * R * W // S
INV_T = 10.0
SCALE = 65536.0
RSQRT2 = 0.7071067811865476
RSQRT2PI = 0.3989422804014327
NT = (((1,), (1,)), ((), ()))
HI = lax.Precision.HIGHEST
F32 = jnp.float32
BF = jnp.bfloat16


def copies_between(pairs, sems, first=0):
    return [
        pltpu.make_async_copy(src, dst, sems.at[first + i]) for i, (src, dst) in enumerate(pairs)
    ]


def mask_kernel(
    features_hbm, tissue, masked_hbm, edge_hbm, flags_hbm, features, masked, edge, flags, sems
):
    where = [(s, r) for s in range(S) for r in range(R)]
    arrive = copies_between([(features_hbm.at[p], features.at[p]) for p in where], sems)
    leave = copies_between([(masked.at[p], masked_hbm.at[p]) for p in where], sems, S * R)
    last_out = copies_between([(edge, edge_hbm), (flags, flags_hbm)], sems, 2 * S * R)
    for c in arrive:
        c.start()
    side = lax.axis_index("section")
    place = lax.broadcasted_iota(jnp.int32, (8, C), 0)
    first = jnp.where((place < 3) & (side == 1), 1.0, 0.0)
    last = jnp.where((place >= 5) & (side == 0), 1.0, 0.0)
    for i, (s, r) in enumerate(where):
        row = tissue[r, s : s + 1, :].astype(F32)
        here = jnp.broadcast_to(row, (LANES, W)).T
        flags[i * W : i * W + W, :] = here
        wide = jnp.concatenate([here] * (C // LANES), axis=1)
        arrive[i].wait()
        values = features[s, r].astype(F32) * wide
        masked[s, r] = values.astype(BF)
        leave[i].start()
        edge[s, r] = (values[:8] * first + values[W - 8 :] * last).astype(BF)
    for c in last_out:
        c.start()
    for c in leave + last_out:
        c.wait()


def forward_kernel(
    own_hbm, above_hbm, below_hbm, edge_own_hbm, edge_above_hbm, edge_below_hbm, flags_hbm,
    dw_k_hbm, dw_b_hbm, ln_g_hbm, ln_b_hbm, scale_hbm, e_bias_hbm, a_w_hbm,
    up_hbm, down_hbm, emb_hbm, v_hbm, u_hbm,
    payload_hbm, embedded_hbm, slope_hbm, weight_hbm, gate_v_hbm, gate_u_hbm,
    own, above, below, edge_own, edge_above, edge_below, flags,
    dw_k, dw_b, ln_g, ln_b, scale, e_bias, a_w, up, down, emb, att_v, att_u,
    payload, embedded_out, slope_out, weight_out, gate_v_out, gate_u_out,
    grid_ref, acc_ref, conv_ref, sums_ref, sems,
):
    blocks = copies_between(
        (
            (own_hbm, own), (edge_own_hbm, edge_own), (above_hbm, above),
            (edge_above_hbm, edge_above), (below_hbm, below), (edge_below_hbm, edge_below),
        ),
        sems,
    )
    small = copies_between(
        (
            (dw_k_hbm, dw_k), (dw_b_hbm, dw_b), (ln_g_hbm, ln_g), (ln_b_hbm, ln_b),
            (scale_hbm, scale), (e_bias_hbm, e_bias), (a_w_hbm, a_w), (flags_hbm, flags),
        ),
        sems,
        6,
    )
    copies = copies_between(
        ((up_hbm, up), (down_hbm, down), (emb_hbm, emb), (v_hbm, att_v), (u_hbm, att_u)), sems, 14
    )
    results = copies_between(
        (
            (embedded_out, embedded_hbm), (slope_out, slope_hbm), (payload, payload_hbm),
            (weight_out, weight_hbm), (gate_v_out, gate_v_hbm), (gate_u_out, gate_u_hbm),
        ),
        sems,
        19,
    )
    for c in blocks + small + copies:
        c.start()
    for c in blocks + small:
        c.wait()
    for s in range(S):
        for r in range(R):
            for base, (block, edge) in enumerate(
                ((above, edge_above), (own, edge_own), (below, edge_below))
            ):
                grid_ref[s, base * R + r, 0:W, :] = block[s, r].astype(F32)
                grid_ref[s, base * R + r, W:PW, :] = edge[s, r].astype(F32)

    def conv_lane(step, carry):
        s = step // (C // LANES)
        lane = pl.multiple_of(lax.rem(step, C // LANES) * LANES, LANES)
        for col in range(PW // 8):
            cols = slice(col * 8, col * 8 + 8)
            rows = [grid_ref[s, r, cols, pl.ds(lane, LANES)] for r in range(3 * R)]
            for b in range(7):
                sums = [None] * R
                for a in range(7):
                    k = dw_k[a, b, pl.ds(lane, LANES)].reshape(1, LANES)
                    for i in range(R):
                        term = rows[i + a] * k
                        sums[i] = term if sums[i] is None else sums[i] + term
                for i in range(R):
                    acc_ref[i, b, cols, :] = sums[i]
        for i in range(R):
            total = acc_ref[i, 3]
            for b in (0, 1, 2, 4, 5, 6):
                total = total + pltpu.roll(acc_ref[i, b], (3 - b) % PW, 0)
            at = pl.multiple_of(s * R * W + i * W, W)
            conv_ref[pl.ds(at, W), pl.ds(lane, LANES)] = total[0:W]
        return carry

    lax.fori_loop(0, S * (C // LANES), conv_lane, 0)
    conv = conv_ref[...] + dw_b[...].reshape(1, -1)
    centre = jnp.mean(conv, axis=-1, keepdims=True)
    moved = conv - centre
    spread = jnp.mean(moved * moved, axis=-1, keepdims=True)
    normed = (moved * lax.rsqrt(spread + 1e-06) * ln_g[...].reshape(1, -1) + ln_b[...].reshape(1, -1)).astype(BF)
    copies[0].wait()
    copies[1].wait()
    branch = jnp.zeros((N, C), F32)
    step = 384
    for h in range(0, HID, step):
        raised = jnp.dot(normed, up[:, h : h + step], preferred_element_type=F32)
        hidden = (0.5 * raised * (1.0 + lax.erf(raised * RSQRT2))).astype(BF)
        branch = branch + jnp.dot(hidden, down[h : h + step, :], preferred_element_type=F32)
    tissue = flags[...]
    wide = jnp.concatenate([tissue] * (C // LANES), axis=1)
    masked = own[...].reshape(N, C).astype(F32)
    trunk = ((masked + scale[...].reshape(1, -1) * branch) * wide).astype(BF)
    copies[2].wait()
    copies[3].wait()
    copies[4].wait()
    logits_v = jnp.zeros((N, AH), F32)
    logits_u = jnp.zeros((N, AH), F32)
    step = 256
    for h in range(0, A, step):
        cols = slice(h, h + step)
        pre = jnp.dot(trunk, emb[:, cols], preferred_element_type=F32) + e_bias[cols].reshape(1, -1)
        cdf = 0.5 * (1.0 + lax.erf(pre * RSQRT2))
        slope = cdf + pre * (RSQRT2PI * jnp.exp(-0.5 * pre * pre))
        out = (pre * cdf).astype(BF)
        embedded_out[:, cols] = out
        slope_out[:, cols] = slope.astype(BF)
        logits_v = logits_v + jnp.dot(out, att_v[cols, :], preferred_element_type=F32)
        logits_u = logits_u + jnp.dot(out, att_u[cols, :], preferred_element_type=F32)
    results[0].start()
    results[1].start()
    tangent = jnp.tanh(logits_v)
    opening = jax.nn.sigmoid(logits_u)
    aw = a_w[...].reshape(1, -1)
    product = tangent * opening * aw
    scores = jnp.sum(product, axis=-1, keepdims=True)
    weight = tissue * jnp.exp(scores)
    weight_out[...] = weight
    results[3].start()
    for s in range(S):
        rows = slice(s * HALF, s * HALF + HALF)
        w_here = weight[rows, :]
        for k in range(A // LANES):
            cols = slice(k * LANES, k * LANES + LANES)
            part = jnp.sum(w_here * embedded_out[rows, cols].astype(F32), axis=0, keepdims=True)
            sums_ref[s : s + 1, cols] = part
        sums_ref[s : s + 1, A:] = jnp.sum(w_here, axis=0, keepdims=True)
    payload[...] = jnp.broadcast_to(sums_ref[...][None], payload.shape)
    results[2].start()
    gate_v_out[...] = (aw * opening * (1.0 - tangent * tangent)).astype(BF)
    gate_u_out[...] = (product * (1.0 - opening)).astype(BF)
    results[4].start()
    results[5].start()
    for c in results:
        c.wait()


def slope_kernel(
    gate_v, gate_u, slope, emb_hbm, v_hbm, u_hbm, out, emb, att_v, att_u, sems
):
    copies = [
        pltpu.make_async_copy(src, dst, sems.at[i])
        for i, (src, dst) in enumerate(((v_hbm, att_v), (u_hbm, att_u), (emb_hbm, emb)))
    ]
    for c in copies:
        c.start()
    for c in copies:
        c.wait()
    total = jnp.zeros((N, C), F32)
    step = 256
    for h in range(0, A, step):
        cols = slice(h, h + step)
        back = lax.dot_general(gate_v[...], att_v[cols, :], NT, preferred_element_type=F32)
        back = back + lax.dot_general(gate_u[...], att_u[cols, :], NT, preferred_element_type=F32)
        back = (back * slope[:, cols].astype(F32)).astype(BF)
        total = total + lax.dot_general(back, emb[:, cols], NT, preferred_element_type=F32)
    out[...] = total


def sum_kernel(received, ahead, payload):
    total = jnp.sum(received[...], axis=0)
    payload[...] = jnp.broadcast_to(total[None], payload.shape)


def final_kernel(
    received, partner, embedded, slope, weight, gate_term, emb_hbm,
    loss_out, vector_out, grad_out, sums_ref, emb, sem,
):
    fetch = pltpu.make_async_copy(emb_hbm, emb, sem)
    fetch.start()
    position = lax.axis_index("set")
    slides = sums_ref.shape[0]
    groups = slides // S
    for g in range(groups):
        gathered = received[g]
        for part in range(1, received.shape[0] // groups):
            gathered = gathered + received[part * groups + g]
        sums_ref[g * S : g * S + S, :] = gathered
    totals = sums_ref[:, A:]
    pooled = sums_ref[:, :A] / totals[:, :1]
    radius = jnp.sqrt(jnp.sum(pooled * pooled, axis=-1, keepdims=True) + 1e-06)
    vector = pooled / radius
    table = (
        lax.dot_general(vector, vector, NT, precision=HI, preferred_element_type=F32) * INV_T
    )
    row = lax.broadcasted_iota(jnp.int32, (slides, slides), 0)
    col = lax.broadcasted_iota(jnp.int32, (slides, slides), 1)
    positive = jnp.where(row == partner[...], 1.0, 0.0)
    exps = jnp.where(row != col, jnp.exp(table), 0.0)
    normaliser = jnp.sum(exps, axis=-1, keepdims=True)
    losses = jnp.log(normaliser) - jnp.sum(positive * table, axis=-1, keepdims=True)
    coefficients = exps / normaliser - positive
    both = coefficients + coefficients.T
    embed_grad = jnp.dot(both, vector, precision=HI, preferred_element_type=F32) * INV_T
    projection = jnp.sum(pooled * embed_grad, axis=-1, keepdims=True)
    pooled_grad = SCALE * (
        embed_grad / radius - pooled * (projection / (radius * radius * radius))
    )
    dots = jnp.sum(pooled_grad * pooled, axis=-1, keepdims=True)
    index = lax.broadcasted_iota(jnp.int32, (slides, 1), 0)
    fetch.wait()
    for s in range(S):
        mine = index == position * S + s

        def pick(values):
            return jnp.sum(jnp.where(mine, values, 0.0), axis=0, keepdims=True)

        vector_out[s : s + 1, :] = pick(vector)
        loss_out[s] = jnp.sum(jnp.where(mine, losses, 0.0))
        grad = pick(pooled_grad)
        dot = pick(dots)
        total = pick(totals)
        rows = slice(s * HALF, s * HALF + HALF)
        aligned = jnp.sum(embedded[rows, :].astype(F32) * grad, axis=-1, keepdims=True)
        share = weight[rows, :] / total
        score = share * (aligned - dot)
        moved = (slope[rows, :].astype(F32) * grad).astype(BF)
        back = lax.dot_general(moved, emb[...], NT, preferred_element_type=F32)
        share = jnp.concatenate([share] * (C // LANES), axis=1)
        score = jnp.concatenate([score] * (C // LANES), axis=1)
        fresh = share * back + score * gate_term[rows, :]
        grad_out[s] = fresh.astype(BF).reshape(R, W, C)


HBM = pl.BlockSpec(memory_space=pltpu.HBM)
VM = pl.BlockSpec(memory_space=pltpu.VMEM)
SM = pl.BlockSpec(memory_space=pltpu.SMEM)
PAY = A + LANES


def params(mib):
    return pltpu.CompilerParams(vmem_limit_bytes=mib * 1024 * 1024)


def shards(
    features, tissue, partner, dw_kernel, dw_bias, ln_gain, ln_bias, w_up,
    narrowing_projection_kernel, layer_scale, w_embed, embed_bias, attn_v, attn_u, attn_w,
):
    block = (S, R, W, C)
    strip = (S, R, 8, C)
    masked_shapes = (
        jax.ShapeDtypeStruct(block, BF),
        jax.ShapeDtypeStruct(strip, BF),
        jax.ShapeDtypeStruct((N, LANES), F32),
    )
    masked, edge, flags = pl.pallas_call(
        mask_kernel,
        out_shape=masked_shapes,
        in_specs=[HBM, VM],
        out_specs=(HBM, HBM, HBM),
        scratch_shapes=[pltpu.VMEM(block, BF)]
        + [pltpu.VMEM(x.shape, x.dtype) for x in masked_shapes]
        + [pltpu.SemaphoreType.DMA((2 * S * R + 2,))],
        compiler_params=params(60),
        name="mask",
    )(features, tissue.transpose(1, 0, 2))
    tile = ("z", "xl")
    count = lax.axis_size(tile)
    upward = [(i, i + 1) for i in range(count - 1)]
    downward = [(i + 1, i) for i in range(count - 1)]
    above = lax.ppermute(masked, tile, upward)
    below = lax.ppermute(masked, tile, downward)
    edge_own = lax.ppermute(edge, "section", [(0, 1), (1, 0)])
    every = ("section",) + tile
    edge_above = lax.ppermute(
        edge, every, [(c * count + i, (1 - c) * count + i + 1) for c in range(2) for i in range(count - 1)]
    )
    edge_below = lax.ppermute(
        edge, every, [(c * count + i + 1, (1 - c) * count + i) for c in range(2) for i in range(count - 1)]
    )
    depth = lax.axis_size("z")

    operands = (
        masked, above, below, edge_own, edge_above, edge_below, flags,
        dw_kernel, dw_bias, ln_gain, ln_bias, layer_scale, embed_bias, attn_w,
        w_up, narrowing_projection_kernel, w_embed, attn_v, attn_u,
    )
    forward_shapes = (
        jax.ShapeDtypeStruct((depth, S, PAY), F32),
        jax.ShapeDtypeStruct((N, A), BF),
        jax.ShapeDtypeStruct((N, A), BF),
        jax.ShapeDtypeStruct((N, LANES), F32),
        jax.ShapeDtypeStruct((N, AH), BF),
        jax.ShapeDtypeStruct((N, AH), BF),
    )
    payload, embedded, slope, weight, gate_v, gate_u = pl.pallas_call(
        forward_kernel,
        out_shape=forward_shapes,
        in_specs=[HBM] * len(operands),
        out_specs=[HBM] * len(forward_shapes),
        scratch_shapes=[pltpu.VMEM(x.shape, x.dtype) for x in operands + forward_shapes]
        + [
            pltpu.VMEM((S, 3 * R, PW, C), F32),
            pltpu.VMEM((R, 7, PW, LANES), F32),
            pltpu.VMEM((N, C), F32),
            pltpu.VMEM((S, PAY), F32),
            pltpu.SemaphoreType.DMA((len(operands) + len(forward_shapes),)),
        ],
        compiler_params=params(60),
        cost_estimate=pl.CostEstimate(flops=2 * 10**9, bytes_accessed=8 * 10**6, transcendentals=10**6),
        name="forward",
    )(*operands)
    gate_term = pl.pallas_call(
        slope_kernel,
        out_shape=jax.ShapeDtypeStruct((N, C), F32),
        in_specs=[VM] * 3 + [HBM] * 3,
        out_specs=VM,
        scratch_shapes=[
            pltpu.VMEM((C, A), BF),
            pltpu.VMEM((A, AH), BF),
            pltpu.VMEM((A, AH), BF),
            pltpu.SemaphoreType.DMA((3,)),
        ],
        compiler_params=params(24),
        cost_estimate=pl.CostEstimate(flops=10**9, bytes_accessed=4 * 10**6, transcendentals=0),
        name="gate_term",
    )(gate_v, gate_u, slope, w_embed, attn_v, attn_u)

    plane = ("section", "xl", "set")
    received = lax.all_to_all(payload, "z", 0, 0, tiled=True)
    payload = pl.pallas_call(
        sum_kernel,
        out_shape=jax.ShapeDtypeStruct((lax.axis_size(plane), S, PAY), F32),
        in_specs=[VM, HBM],
        out_specs=VM,
        compiler_params=params(24),
        name="add_up",
    )(received, gate_term)
    received = lax.all_to_all(payload, plane, 0, 0, tiled=True)
    slides = partner.shape[0]
    return pl.pallas_call(
        final_kernel,
        out_shape=(
            jax.ShapeDtypeStruct((S,), F32),
            jax.ShapeDtypeStruct((S, A), F32),
            jax.ShapeDtypeStruct((S, R, W, C), BF),
        ),
        in_specs=[VM] * 6 + [HBM],
        out_specs=(SM, VM, VM),
        scratch_shapes=[
            pltpu.VMEM((slides, PAY), F32),
            pltpu.VMEM((C, A), BF),
            pltpu.SemaphoreType.DMA(()),
        ],
        compiler_params=params(24),
        name="final",
    )(received, partner.reshape(1, slides), embedded, slope, weight, gate_term, w_embed)


def solution(mesh):
    section, tile, groups = mesh.devices.shape
    fine = Mesh(
        mesh.devices.reshape(section, tile // 2, 2, groups), ("section", "z", "xl", "set")
    )
    tiles = ("z", "xl")
    placed = (P("set", tiles, "section", None), P("set", tiles, "section")) + (P(),) * 13
    return jax.shard_map(
        shards,
        mesh=fine,
        in_specs=placed,
        out_specs=(P("set"), P("set", None), P("set", tiles, "section", None)),
        check_vma=False,
    )
```

time: 362 us -> 84.1 us (0.23); the launches traced: 356 us -> 83.6 us
  blocking collectives: 155 us -> 20.5 us
  waiting for transfers between devices: 113 us -> 8.57 us
  matrix products: 38.3 us -> 0 us
  starting transfers between devices: 12.7 us -> 33.6 us
  Pallas kernels: 0 us -> 16.2 us
  between operations: 15 us -> 0.84 us
  other arithmetic: 10 us -> 0 us
  local copies, waits for them, and re-layouts: 12.7 us -> 3.79 us
    psum x1 -> x0, blocking collectives: 126 us -> none  [shards(): weighted_sum, totals = lax.psum((weighted_sum, totals), ('section', 'tile'))]
    unnamed x2 -> x0, waiting for transfers between devices: 100 us -> none
    dot_general x31 -> x0, matrix products: 38.3 us -> none  [the longest x3 9.76 us: back_rows(): lax.dot_general(pre_grad, w_embed, contract, preferred_element_type=jnp.f...]
    all_gather x1 -> x0, blocking collectives: 28.4 us -> none  [shards(): lax.all_gather(specimen_normalised_vector, 'set', axis=0, tiled=True)]
    all_to_all x0 -> x1, blocking collectives: none -> 20.5 us  [shards(): received = lax.all_to_all(payload, plane, 0, 0, tiled=True)]
    pallas_call x0 -> x5, Pallas kernels: none -> 16.2 us  [the longest x1 9.28 us: shards(): pl.pallas_call(forward_kernel, out_shape=forward_shapes, in_specs=[HBM] *...]
    all_to_all x0 -> x1, starting transfers between devices: none -> 13.4 us  [shards(): received = lax.all_to_all(payload, 'z', 0, 0, tiled=True)]
    ppermute x4 -> x5, waiting for transfers between devices: 12.9 us -> 1.02 us  [the longest x1 1.01 us: shards(): edge_own = lax.ppermute(edge, 'section', [(0, 1), (1, 0)])]
  transfers between devices with their start and end apart: 5 -> 6, of which waited for: 2 -> 2; matrix products, arithmetic and copies ran while one was open for 2% -> 0% of each run, Pallas kernels for 0% -> 2%
where the time goes in v1:
time: 84.1 us; the launch traced here: 83.6 us
  starting transfers between devices  33.6 us (40%)
  blocking collectives  20.5 us (24%)
  Pallas kernels  16.2 us (19%)
  waiting for transfers between devices  8.57 us (10%)
  local copies, waits for them, and re-layouts  3.79 us (5%)
    all_to_all x1, blocking collectives, shards(): received = lax.all_to_all(payload, plane, 0, 0, tiled=True)  20.5 us
    all_to_all x1, starting transfers between devices, shards(): received = lax.all_to_all(payload, 'z', 0, 0, tiled=True)  13.4 us
    pallas_call x1, Pallas kernels, shards(): pl.pallas_call(forward_kernel, out_shape=forward_shapes, in_specs=[HBM] *...  9.28 us
    ppermute x1, starting transfers between devices, shards(): lax.ppermute(edge, every, [(c * count + i, (1 - c) * count + i + 1) for c...  8.99 us
    all_to_all x1, waiting for transfers between devices, shards(): received = lax.all_to_all(payload, 'z', 0, 0, tiled=True)  7.55 us
    ppermute x1, starting transfers between devices, shards(): above = lax.ppermute(masked, tile, upward)  4.59 us
    ppermute x1, starting transfers between devices, shards(): edge_own = lax.ppermute(edge, 'section', [(0, 1), (1, 0)])  4.04 us
    unnamed x30, local copies, waits for them, and re-layouts  3.79 us
  transfers between devices with their start and end apart: 6, of which 2 were waited for; matrix products, arithmetic and copies ran while one was open for 0% of the time, Pallas kernels for 2%

profile of v1, /device:TPU:1, one launch (start us, length us, event | category | flops | bytes accessed | tf_op | source)
XLA Modules:
  0.0 83.6 jit_solution(10760596964008434715)
XLA Ops:
  0.6 2.7 %mask.1 = (bf16[2,3,64,384]{3,2,1,0:T(8,128)(2,1)}, bf16[2,3,8,384]{3,2,1,0:T(8,128)(2,1)}, f32[384,128]{1,0:T(8,128)}) custom-call(bf16[2,3,64,384]{3,2,1,0:T(8,128)(2,1)} %features_hbm.1, s32[3,2,64]{2,1,0:T(2,128)} %bitcast.3), custom_call_target="tpu_custom_call" | custom-call | tf_op jit(solution)/shard_map/mask/pallas_call | solution.py:306
  3.4 1.3 %collective-permute-start.1 = (bf16[2,3,64,384]{3,2,1,0:T(8,128)(2,1)}, bf16[2,3,64,384]{3,2,1,0:T(8,128)(2,1)S(1)}, u32[]{:S(2)}, u32[]{:S(2)}) collective-permute-start(bf16[2,3,64,384]{3,2,1,0:T(8,128)(2,1)} %get-tuple-element.12.own_hbm), channel_id=1, source_target_pairs={{8,0},{16,8},{24,16},{32,24},{40,32},{48,40},{56,48},{64,56},{72,6... | collective-permute-start | bytes 884744 | tf_op jit(solution)/shard_map/ppermute | solution.py:322
  4.7 4.6 %collective-permute-start = (bf16[2,3,64,384]{3,2,1,0:T(8,128)(2,1)}, bf16[2,3,64,384]{3,2,1,0:T(8,128)(2,1)S(1)}, u32[]{:S(2)}, u32[]{:S(2)}) collective-permute-start(bf16[2,3,64,384]{3,2,1,0:T(8,128)(2,1)} %get-tuple-element.12.own_hbm), channel_id=1, source_target_pairs={{0,8},{8,16},{16,24},{24,32},{32,40},{40,48},{48,56},{56,64},{64,7... | collective-permute-start | bytes 884744 | tf_op jit(solution)/shard_map/ppermute | solution.py:321
  9.3 1.3 %collective-permute-start.4 = (bf16[2,3,8,384]{3,2,1,0:T(8,128)(2,1)}, bf16[2,3,8,384]{3,2,1,0:T(8,128)(2,1)S(1)}, u32[]{:S(2)}, u32[]{:S(2)}) collective-permute-start(bf16[2,3,8,384]{3,2,1,0:T(8,128)(2,1)} %get-tuple-element.13), channel_id=1, source_target_pairs={{8,256},{16,264},{24,272},{32,280},{40,288},{48,296},{56,304},{64,... | collective-permute-start | bytes 110600 | tf_op jit(solution)/shard_map/ppermute | solution.py:328
  10.6 9.0 %collective-permute-start.3 = (bf16[2,3,8,384]{3,2,1,0:T(8,128)(2,1)}, bf16[2,3,8,384]{3,2,1,0:T(8,128)(2,1)S(1)}, u32[]{:S(2)}, u32[]{:S(2)}) collective-permute-start(bf16[2,3,8,384]{3,2,1,0:T(8,128)(2,1)} %get-tuple-element.13), channel_id=1, source_target_pairs={{0,264},{8,272},{16,280},{24,288},{32,296},{40,304},{48,312},{56,3... | collective-permute-start | bytes 110600 | tf_op jit(solution)/shard_map/ppermute | solution.py:325
  19.6 4.0 %collective-permute-start.2 = (bf16[2,3,8,384]{3,2,1,0:T(8,128)(2,1)}, bf16[2,3,8,384]{3,2,1,0:T(8,128)(2,1)S(1)}, u32[]{:S(2)}, u32[]{:S(2)}) collective-permute-start(bf16[2,3,8,384]{3,2,1,0:T(8,128)(2,1)} %get-tuple-element.13), channel_id=1, source_target_pairs={{0,256},{256,0},{1,257},{257,1},{2,258},{258,2},{3,259},{259,3},{4... | collective-permute-start | bytes 110600 | tf_op jit(solution)/shard_map/ppermute | solution.py:323
  23.6 0.0 collective-permute-done.4.edge_below_hbm
  23.6 0.0 copy-start.12
  23.6 0.0 collective-permute-done.3.edge_above_hbm
  23.7 0.0 copy-start.13
  23.7 1.0 %collective-permute-done.2.edge_own_hbm = bf16[2,3,8,384]{3,2,1,0:T(8,128)(2,1)S(1)} collective-permute-done((bf16[2,3,8,384]{3,2,1,0:T(8,128)(2,1)}, bf16[2,3,8,384]{3,2,1,0:T(8,128)(2,1)S(1)}, u32[]{:S(2)}, u32[]{:S(2)}) %collective-permute-start.2) | collective-permute-done | bytes 36896 | tf_op jit(solution)/shard_map/ppermute | solution.py:323
  24.7 0.0 copy-start.14
  24.7 0.0 collective-permute-done.1.below_hbm
  24.7 0.0 copy-start.10
  24.7 0.0 collective-permute-done.above_hbm
  24.7 0.0 copy-start.11
  24.7 0.0 copy-done.12
  24.7 0.0 copy-done.13
  24.7 0.6 copy-done.14
  25.3 0.1 copy-done.10
  25.4 0.1 copy-done.11
  25.5 0.0 copy-start
  25.5 0.0 copy-start.6
  25.5 0.0 copy-start.7
  25.5 9.3 %forward.1 = (f32[16,2,1152]{2,1,0:T(2,128)}, bf16[384,1024]{1,0:T(8,128)(2,1)}, bf16[384,1024]{1,0:T(8,128)(2,1)}, f32[384,128]{1,0:T(8,128)}, bf16[384,256]{1,0:T(8,128)(2,1)}, /*index=5*/bf16[384,256]{1,0:T(8,128)(2,1)}) custom-call(bf16[2,3,64,384]{3,2,1,0:T(8,128)(2,1)} %get-tuple-element.12.own_hbm, bf16[2,3,64,384]{3,2,1,0:T(8,128)(2,1)} %copy-done.11, ...), custom_call_target="tpu_custom_call" | custom-call | flops 2000000000 | bytes 8000000 | tf_op jit(solution)/shard_map/forward/pallas_call | solution.py:346
  34.8 13.4 %all-to-all-start = ((f32[16,2,1152]{2,1,0:T(2,128)}), f32[16,2,1152]{2,1,0:T(2,128)S(1)}, u32[]{:S(2)}, u32[]{:S(2)}) async-start(f32[16,2,1152]{2,1,0:T(2,128)} %get-tuple-element.15), calls=%async_computation | async-start | bytes 294912 | tf_op jit(solution)/shard_map/all_to_all | solution.py:380
  48.2 0.0 copy-done
  48.2 0.0 copy-done.6
  48.2 0.0 copy-done.7
  48.2 0.0 copy-start.2
  48.3 1.1 %copy-done.2 = bf16[384,1024]{1,0:T(8,128)(2,1)S(1)} copy-done((bf16[384,1024]{1,0:T(8,128)(2,1)S(1)}, bf16[384,1024]{1,0:T(8,128)(2,1)}, u32[]{:S(2)}) %copy-start.2) | copy-done | bytes 786456
  49.4 0.0 copy-start.8
  49.4 0.9 %copy-done.8 = bf16[384,256]{1,0:T(8,128)(2,1)S(1)} copy-done((bf16[384,256]{1,0:T(8,128)(2,1)S(1)}, bf16[384,256]{1,0:T(8,128)(2,1)}, u32[]{:S(2)}) %copy-start.8) | copy-done | bytes 196632
  50.3 0.0 copy-start.9
  50.3 0.9 %copy-done.9 = bf16[384,256]{1,0:T(8,128)(2,1)S(1)} copy-done((bf16[384,256]{1,0:T(8,128)(2,1)S(1)}, bf16[384,256]{1,0:T(8,128)(2,1)}, u32[]{:S(2)}) %copy-start.9) | copy-done | bytes 196632
  51.2 0.0 copy-start.4
  51.2 1.5 %gate_term.1.ahead = f32[384,384]{1,0:T(8,128)S(1)} custom-call(bf16[384,256]{1,0:T(8,128)(2,1)S(1)} %copy-done.8, bf16[384,256]{1,0:T(8,128)(2,1)S(1)} %copy-done.9, bf16[384,1024]{1,0:T(8,128)(2,1)S(1)} %copy-done.2, bf16[384,1024]{1,0:T(8,128)(2,1)S(1)} %copy-done, bf16[1024,256]{1,0:T(8,128)(2,1)S(1)} %copy-done.6, bf16[1024,256]{1,0:T(8,128)(2,1)S(1)} %copy-done.7), custom_call_target="tpu_custom_call" | custom-call | flops 1000000000 | bytes 4000000 | tf_op jit(solution)/shard_map/gate_term/pallas_call | solution.py:363
  52.8 0.0 copy-start.1
  52.8 0.0 copy-start.3
  52.8 0.0 copy-start.5
  52.8 7.6 %all-to-all-done.received = f32[16,2,1152]{2,1,0:T(2,128)S(1)} async-done(((f32[16,2,1152]{2,1,0:T(2,128)}), f32[16,2,1152]{2,1,0:T(2,128)S(1)}, u32[]{:S(2)}, u32[]{:S(2)}) %all-to-all-start) | async-done | bytes 147488 | tf_op jit(solution)/shard_map/all_to_all | solution.py:380
  60.3 0.1 add_up.1
  60.4 20.5 %all_to_all.10.received = f32[32,2,1152]{2,1,0:T(2,128)S(1)} all-to-all(f32[32,2,1152]{2,1,0:T(2,128)S(1)} %add_up.1), channel_id=1, replica_groups=mesh['section'=2,'z'=16,'xl'=2,'set'=8] {'section','xl','set'}, dimensions={0} | all-to-all | bytes 589824 | tf_op jit(solution)/shard_map/all_to_all | solution.py:389
  81.0 0.0 copy-done.4
  81.0 0.0 copy-done.1
  81.0 0.0 copy-done.3
  81.0 0.0 copy-done.5
  81.0 2.6 %final.1 = (f32[2]{0:T(128)}, f32[2,1024]{1,0:T(2,128)}, bf16[2,3,64,384]{3,2,1,0:T(8,128)(2,1)}) custom-call(f32[32,2,1152]{2,1,0:T(2,128)S(1)} %all_to_all.10.received, s32[1,16]{1,0:T(1,128)S(1)} %bitcast.2, bf16[384,1024]{1,0:T(8,128)(2,1)S(1)} %copy-done.1, bf16[384,1024]{1,0:T(8,128)(2,1)S(1)} %copy-done.3, f32[384,128]{1,0:T(8,128)S(1)} %copy-done.4, ...), custom_call_target="tpu_custom_call" | custom-call | tf_op jit(solution)/shard_map/final/pallas_call | solution.py:391
Async XLA Ops:
  3.4 21.3 %collective-permute-start.1 = (bf16[2,3,64,384]{3,2,1,0:T(8,128)(2,1)}, bf16[2,3,64,384]{3,2,1,0:T(8,128)(2,1)S(1)}, u32[]{:S(2)}, u32[]{:S(2)}) collective-permute-start(bf16[2,3,64,384]{3,2,1,0:T(8,128)(2,1)} %get-tuple-element.12.own_hbm), channel_id=1, source_target_pairs={{8,0},{16,8},{24,16},{32,24},{40,32},{48,40},{56,48},{64,56},{72,6... | collective-permute-start | bytes 884744 | tf_op jit(solution)/shard_map/ppermute | solution.py:322
  4.7 20.0 %collective-permute-start = (bf16[2,3,64,384]{3,2,1,0:T(8,128)(2,1)}, bf16[2,3,64,384]{3,2,1,0:T(8,128)(2,1)S(1)}, u32[]{:S(2)}, u32[]{:S(2)}) collective-permute-start(bf16[2,3,64,384]{3,2,1,0:T(8,128)(2,1)} %get-tuple-element.12.own_hbm), channel_id=1, source_target_pairs={{0,8},{8,16},{16,24},{24,32},{32,40},{40,48},{48,56},{56,64},{64,7... | collective-permute-start | bytes 884744 | tf_op jit(solution)/shard_map/ppermute | solution.py:321
  9.3 14.3 %collective-permute-start.4 = (bf16[2,3,8,384]{3,2,1,0:T(8,128)(2,1)}, bf16[2,3,8,384]{3,2,1,0:T(8,128)(2,1)S(1)}, u32[]{:S(2)}, u32[]{:S(2)}) collective-permute-start(bf16[2,3,8,384]{3,2,1,0:T(8,128)(2,1)} %get-tuple-element.13), channel_id=1, source_target_pairs={{8,256},{16,264},{24,272},{32,280},{40,288},{48,296},{56,304},{64,... | collective-permute-start | bytes 110600 | tf_op jit(solution)/shard_map/ppermute | solution.py:328
  10.6 13.1 %collective-permute-start.3 = (bf16[2,3,8,384]{3,2,1,0:T(8,128)(2,1)}, bf16[2,3,8,384]{3,2,1,0:T(8,128)(2,1)S(1)}, u32[]{:S(2)}, u32[]{:S(2)}) collective-permute-start(bf16[2,3,8,384]{3,2,1,0:T(8,128)(2,1)} %get-tuple-element.13), channel_id=1, source_target_pairs={{0,264},{8,272},{16,280},{24,288},{32,296},{40,304},{48,312},{56,3... | collective-permute-start | bytes 110600 | tf_op jit(solution)/shard_map/ppermute | solution.py:325
  19.6 5.1 %collective-permute-start.2 = (bf16[2,3,8,384]{3,2,1,0:T(8,128)(2,1)}, bf16[2,3,8,384]{3,2,1,0:T(8,128)(2,1)S(1)}, u32[]{:S(2)}, u32[]{:S(2)}) collective-permute-start(bf16[2,3,8,384]{3,2,1,0:T(8,128)(2,1)} %get-tuple-element.13), channel_id=1, source_target_pairs={{0,256},{256,0},{1,257},{257,1},{2,258},{258,2},{3,259},{259,3},{4... | collective-permute-start | bytes 110600 | tf_op jit(solution)/shard_map/ppermute | solution.py:323
  23.6 1.1 %copy-start.12 = (bf16[2,3,8,384]{3,2,1,0:T(8,128)(2,1)}, bf16[2,3,8,384]{3,2,1,0:T(8,128)(2,1)S(1)}, u32[]{:S(2)}) copy-start(bf16[2,3,8,384]{3,2,1,0:T(8,128)(2,1)S(1)} %collective-permute-done.4.edge_below_hbm) | copy-start | bytes 110596
  23.7 1.1 %copy-start.13 = (bf16[2,3,8,384]{3,2,1,0:T(8,128)(2,1)}, bf16[2,3,8,384]{3,2,1,0:T(8,128)(2,1)S(1)}, u32[]{:S(2)}) copy-start(bf16[2,3,8,384]{3,2,1,0:T(8,128)(2,1)S(1)} %collective-permute-done.3.edge_above_hbm) | copy-start | bytes 110596
  24.7 0.6 copy-start.14
  24.7 0.7 copy-start.10
  24.7 0.8 copy-start.11
  25.5 22.7 %copy-start = (bf16[384,1024]{1,0:T(8,128)(2,1)S(1)}, bf16[384,1024]{1,0:T(8,128)(2,1)}, u32[]{:S(2)}) copy-start(bf16[384,1024]{1,0:T(8,128)(2,1)} %emb_hbm.5) | copy-start | bytes 2359300
  25.5 22.7 %copy-start.6 = (bf16[1024,256]{1,0:T(8,128)(2,1)S(1)}, bf16[1024,256]{1,0:T(8,128)(2,1)}, u32[]{:S(2)}) copy-start(bf16[1024,256]{1,0:T(8,128)(2,1)} %v_hbm.3) | copy-start | bytes 1572868
  25.5 22.7 %copy-start.7 = (bf16[1024,256]{1,0:T(8,128)(2,1)S(1)}, bf16[1024,256]{1,0:T(8,128)(2,1)}, u32[]{:S(2)}) copy-start(bf16[1024,256]{1,0:T(8,128)(2,1)} %u_hbm.3) | copy-start | bytes 1572868
  34.8 25.6 %all-to-all-start = ((f32[16,2,1152]{2,1,0:T(2,128)}), f32[16,2,1152]{2,1,0:T(2,128)S(1)}, u32[]{:S(2)}, u32[]{:S(2)}) async-start(f32[16,2,1152]{2,1,0:T(2,128)} %get-tuple-element.15), calls=%async_computation | async-start | bytes 294912 | tf_op jit(solution)/shard_map/all_to_all | solution.py:380
  48.2 1.1 %copy-start.2 = (bf16[384,1024]{1,0:T(8,128)(2,1)S(1)}, bf16[384,1024]{1,0:T(8,128)(2,1)}, u32[]{:S(2)}) copy-start(bf16[384,1024]{1,0:T(8,128)(2,1)} %get-tuple-element.18.slope) | copy-start | bytes 2359300
  49.4 0.9 %copy-start.8 = (bf16[384,256]{1,0:T(8,128)(2,1)S(1)}, bf16[384,256]{1,0:T(8,128)(2,1)}, u32[]{:S(2)}) copy-start(bf16[384,256]{1,0:T(8,128)(2,1)} %get-tuple-element.16.gate_v) | copy-start | bytes 589828
  50.3 0.9 %copy-start.9 = (bf16[384,256]{1,0:T(8,128)(2,1)S(1)}, bf16[384,256]{1,0:T(8,128)(2,1)}, u32[]{:S(2)}) copy-start(bf16[384,256]{1,0:T(8,128)(2,1)} %get-tuple-element.17.gate_u) | copy-start | bytes 589828
  51.2 29.7 %copy-start.4 = (f32[384,128]{1,0:T(8,128)S(1)}, f32[384,128]{1,0:T(8,128)}, u32[]{:S(2)}) copy-start(f32[384,128]{1,0:T(8,128)} %get-tuple-element.20.weight) | copy-start | bytes 589828
  52.8 28.2 %copy-start.1 = (bf16[384,1024]{1,0:T(8,128)(2,1)S(1)}, bf16[384,1024]{1,0:T(8,128)(2,1)}, u32[]{:S(2)}) copy-start(bf16[384,1024]{1,0:T(8,128)(2,1)} %get-tuple-element.19.embedded) | copy-start | bytes 2359300
  52.8 28.2 %copy-start.3 = (bf16[384,1024]{1,0:T(8,128)(2,1)S(1)}, bf16[384,1024]{1,0:T(8,128)(2,1)}, u32[]{:S(2)}) copy-start(bf16[384,1024]{1,0:T(8,128)(2,1)} %get-tuple-element.18.slope) | copy-start | bytes 2359300
  52.8 28.2 %copy-start.5 = (s32[16]{0:T(128)S(1)}, s32[16]{0:T(128)}, u32[]{:S(2)}) copy-start(s32[16]{0:T(128)} %param.17) | copy-start | bytes 196

commit v2 on v1

--- a/solution.py
+++ b/solution.py
@@ -46,9 +46,10 @@
     place = lax.broadcasted_iota(jnp.int32, (8, C), 0)
     first = jnp.where((place < 3) & (side == 1), 1.0, 0.0)
     last = jnp.where((place >= 5) & (side == 0), 1.0, 0.0)
+    rows = [tissue[r, s : s + 1, :].astype(F32) for s, r in where]
+    turned = jnp.concatenate(rows + rows[:2], axis=0).T
     for i, (s, r) in enumerate(where):
-        row = tissue[r, s : s + 1, :].astype(F32)
-        here = jnp.broadcast_to(row, (LANES, W)).T
+        here = jnp.broadcast_to(turned[:, i : i + 1], (W, LANES))
         flags[i * W : i * W + W, :] = here
         wide = jnp.concatenate([here] * (C // LANES), axis=1)
         arrive[i].wait()
@@ -62,33 +63,103 @@
         c.wait()
 
 
+def fill(grid_ref, at, block, edge):
+    for s in range(S):
+        for r in range(R):
+            grid_ref[s, at + r, 0:W, :] = block[s, r].astype(F32)
+            grid_ref[s, at + r, W:PW, :] = edge[s, r].astype(F32)
+
+
+def convolve(grid_ref, acc_ref, conv_ref, dw_k, first, count, seed):
+    odd = lax.axis_index("xl") == 1
+
+    def turn(i, last):
+        return jnp.where(odd, last - i, i)
+
+    def conv_lane(step, carry):
+        s = step // (C // LANES)
+        lane = pl.multiple_of(lax.rem(step, C // LANES) * LANES, LANES)
+        for col in range(PW // 8):
+            cols = slice(col * 8, col * 8 + 8)
+            rows = [
+                grid_ref[s, base + turn(m, R - 1), cols, pl.ds(lane, LANES)]
+                for base in range(0, count, R)
+                for m in range(R)
+            ]
+            for b in range(7):
+                sums = [None] * R
+                for a in range(7):
+                    pairs = [(a + n - first, n) for n in range(R) if 0 <= a + n - first < count]
+                    if not pairs:
+                        continue
+                    k = dw_k[turn(a, 6), b, pl.ds(lane, LANES)].reshape(1, LANES)
+                    for row, n in pairs:
+                        term = rows[row] * k
+                        sums[n] = term if sums[n] is None else sums[n] + term
+                for n in range(R):
+                    acc_ref[n, b, cols, :] = sums[n]
+        for n in range(R):
+            total = acc_ref[n, 3]
+            for b in (0, 1, 2, 4, 5, 6):
+                total = total + pltpu.roll(acc_ref[n, b], (3 - b) % PW, 0)
+            at = pl.multiple_of(s * R * W + turn(n, R - 1) * W, W)
+            where = (pl.ds(at, W), pl.ds(lane, LANES))
+            total = total[0:W]
+            conv_ref[where] = total if seed is None else total + seed[where]
+        return carry
+
+    lax.fori_loop(0, S * (C // LANES), conv_lane, 0)
+
+
+def near_kernel(
+    own_hbm, edge_own_hbm, near_hbm, edge_near_hbm, dw_k_hbm, partial_hbm,
+    own, edge_own, near, edge_near, dw_k, partial, grid_ref, acc_ref, sems,
+):
+    arrive = copies_between(
+        (
+            (own_hbm, own), (edge_own_hbm, edge_own), (near_hbm, near),
+            (edge_near_hbm, edge_near), (dw_k_hbm, dw_k),
+        ),
+        sems,
+    )
+    for c in arrive:
+        c.start()
+    for c in arrive:
+        c.wait()
+    fill(grid_ref, 0, own, edge_own)
+    fill(grid_ref, R, near, edge_near)
+    convolve(grid_ref, acc_ref, partial, dw_k, R, 2 * R, None)
+    leave = pltpu.make_async_copy(partial, partial_hbm, sems.at[5])
+    leave.start()
+    leave.wait()
+
+
 def forward_kernel(
-    own_hbm, above_hbm, below_hbm, edge_own_hbm, edge_above_hbm, edge_below_hbm, flags_hbm,
+    far_hbm, edge_far_hbm, partial_hbm, own_hbm, flags_hbm,
     dw_k_hbm, dw_b_hbm, ln_g_hbm, ln_b_hbm, scale_hbm, e_bias_hbm, a_w_hbm,
     up_hbm, down_hbm, emb_hbm, v_hbm, u_hbm,
     payload_hbm, embedded_hbm, slope_hbm, weight_hbm, gate_v_hbm, gate_u_hbm,
-    own, above, below, edge_own, edge_above, edge_below, flags,
+    far, edge_far, partial, own, flags,
     dw_k, dw_b, ln_g, ln_b, scale, e_bias, a_w, up, down, emb, att_v, att_u,
     payload, embedded_out, slope_out, weight_out, gate_v_out, gate_u_out,
     grid_ref, acc_ref, conv_ref, sums_ref, sems,
 ):
     blocks = copies_between(
         (
-            (own_hbm, own), (edge_own_hbm, edge_own), (above_hbm, above),
-            (edge_above_hbm, edge_above), (below_hbm, below), (edge_below_hbm, edge_below),
+            (far_hbm, far), (edge_far_hbm, edge_far), (dw_k_hbm, dw_k), (partial_hbm, partial),
         ),
         sems,
     )
     small = copies_between(
         (
-            (dw_k_hbm, dw_k), (dw_b_hbm, dw_b), (ln_g_hbm, ln_g), (ln_b_hbm, ln_b),
+            (own_hbm, own), (dw_b_hbm, dw_b), (ln_g_hbm, ln_g), (ln_b_hbm, ln_b),
             (scale_hbm, scale), (e_bias_hbm, e_bias), (a_w_hbm, a_w), (flags_hbm, flags),
         ),
         sems,
-        6,
+        4,
     )
     copies = copies_between(
-        ((up_hbm, up), (down_hbm, down), (emb_hbm, emb), (v_hbm, att_v), (u_hbm, att_u)), sems, 14
+        ((up_hbm, up), (down_hbm, down), (emb_hbm, emb), (v_hbm, att_v), (u_hbm, att_u)), sems, 12
     )
     results = copies_between(
         (
@@ -96,44 +167,16 @@
             (weight_out, weight_hbm), (gate_v_out, gate_v_hbm), (gate_u_out, gate_u_hbm),
         ),
         sems,
-        19,
+        17,
     )
     for c in blocks + small + copies:
         c.start()
-    for c in blocks + small:
-        c.wait()
-    for s in range(S):
-        for r in range(R):
-            for base, (block, edge) in enumerate(
-                ((above, edge_above), (own, edge_own), (below, edge_below))
-            ):
-                grid_ref[s, base * R + r, 0:W, :] = block[s, r].astype(F32)
-                grid_ref[s, base * R + r, W:PW, :] = edge[s, r].astype(F32)
-
-    def conv_lane(step, carry):
-        s = step // (C // LANES)
-        lane = pl.multiple_of(lax.rem(step, C // LANES) * LANES, LANES)
-        for col in range(PW // 8):
-            cols = slice(col * 8, col * 8 + 8)
-            rows = [grid_ref[s, r, cols, pl.ds(lane, LANES)] for r in range(3 * R)]
-            for b in range(7):
-                sums = [None] * R
-                for a in range(7):
-                    k = dw_k[a, b, pl.ds(lane, LANES)].reshape(1, LANES)
-                    for i in range(R):
-                        term = rows[i + a] * k
-                        sums[i] = term if sums[i] is None else sums[i] + term
-                for i in range(R):
-                    acc_ref[i, b, cols, :] = sums[i]
-        for i in range(R):
-            total = acc_ref[i, 3]
-            for b in (0, 1, 2, 4, 5, 6):
-                total = total + pltpu.roll(acc_ref[i, b], (3 - b) % PW, 0)
-            at = pl.multiple_of(s * R * W + i * W, W)
-            conv_ref[pl.ds(at, W), pl.ds(lane, LANES)] = total[0:W]
-        return carry
-
-    lax.fori_loop(0, S * (C // LANES), conv_lane, 0)
+    for c in blocks:
+        c.wait()
+    fill(grid_ref, 0, far, edge_far)
+    convolve(grid_ref, acc_ref, conv_ref, dw_k, 0, R, partial)
+    for c in small:
+        c.wait()
     conv = conv_ref[...] + dw_b[...].reshape(1, -1)
     centre = jnp.mean(conv, axis=-1, keepdims=True)
     moved = conv - centre
@@ -224,9 +267,10 @@
 
 def final_kernel(
     received, partner, embedded, slope, weight, gate_term, emb_hbm,
-    loss_out, vector_out, grad_out, sums_ref, emb, sem,
-):
-    fetch = pltpu.make_async_copy(emb_hbm, emb, sem)
+    loss_out, vector_out, grad_hbm, grad_out, sums_ref, emb, sems,
+):
+    fetch = pltpu.make_async_copy(emb_hbm, emb, sems.at[S])
+    leave = copies_between([(grad_out.at[s], grad_hbm.at[s]) for s in range(S)], sems)
     fetch.start()
     position = lax.axis_index("set")
     slides = sums_ref.shape[0]
@@ -280,6 +324,9 @@
         score = jnp.concatenate([score] * (C // LANES), axis=1)
         fresh = share * back + score * gate_term[rows, :]
         grad_out[s] = fresh.astype(BF).reshape(R, W, C)
+        leave[s].start()
+    for c in leave:
+        c.wait()
 
 
 HBM = pl.BlockSpec(memory_space=pltpu.HBM)
@@ -316,22 +363,39 @@
     )(features, tissue.transpose(1, 0, 2))
     tile = ("z", "xl")
     count = lax.axis_size(tile)
-    upward = [(i, i + 1) for i in range(count - 1)]
-    downward = [(i + 1, i) for i in range(count - 1)]
-    above = lax.ppermute(masked, tile, upward)
-    below = lax.ppermute(masked, tile, downward)
+    nearby = [(i, i ^ 1) for i in range(count)]
+    away = [(i, i + 1 if i % 2 else i - 1) for i in range(1, count - 1)]
+    every = ("section",) + tile
+
+    def crossed(moves):
+        return [(c * count + i, (1 - c) * count + j) for c in range(2) for i, j in moves]
+
+    far = lax.ppermute(masked, tile, away)
+    near = lax.ppermute(masked, tile, nearby)
+    edge_far = lax.ppermute(edge, every, crossed(away))
+    edge_near = lax.ppermute(edge, every, crossed(nearby))
     edge_own = lax.ppermute(edge, "section", [(0, 1), (1, 0)])
-    every = ("section",) + tile
-    edge_above = lax.ppermute(
-        edge, every, [(c * count + i, (1 - c) * count + i + 1) for c in range(2) for i in range(count - 1)]
-    )
-    edge_below = lax.ppermute(
-        edge, every, [(c * count + i + 1, (1 - c) * count + i) for c in range(2) for i in range(count - 1)]
-    )
     depth = lax.axis_size("z")
 
+    sources = (masked, edge_own, near, edge_near, dw_kernel)
+    partial = jax.ShapeDtypeStruct((N, C), F32)
+    partial = pl.pallas_call(
+        near_kernel,
+        out_shape=partial,
+        in_specs=[HBM] * len(sources),
+        out_specs=HBM,
+        scratch_shapes=[pltpu.VMEM(x.shape, x.dtype) for x in sources + (partial,)]
+        + [
+            pltpu.VMEM((S, 2 * R, PW, C), F32),
+            pltpu.VMEM((R, 7, PW, LANES), F32),
+            pltpu.SemaphoreType.DMA((6,)),
+        ],
+        compiler_params=params(64),
+        cost_estimate=pl.CostEstimate(flops=10**8, bytes_accessed=2 * 10**6, transcendentals=0),
+        name="near",
+    )(*sources)
     operands = (
-        masked, above, below, edge_own, edge_above, edge_below, flags,
+        far, edge_far, partial, masked, flags,
         dw_kernel, dw_bias, ln_gain, ln_bias, layer_scale, embed_bias, attn_w,
         w_up, narrowing_projection_kernel, w_embed, attn_v, attn_u,
     )
@@ -350,7 +414,7 @@
         out_specs=[HBM] * len(forward_shapes),
         scratch_shapes=[pltpu.VMEM(x.shape, x.dtype) for x in operands + forward_shapes]
         + [
-            pltpu.VMEM((S, 3 * R, PW, C), F32),
+            pltpu.VMEM((S, R, PW, C), F32),
             pltpu.VMEM((R, 7, PW, LANES), F32),
             pltpu.VMEM((N, C), F32),
             pltpu.VMEM((S, PAY), F32),
@@ -396,11 +460,12 @@
             jax.ShapeDtypeStruct((S, R, W, C), BF),
         ),
         in_specs=[VM] * 6 + [HBM],
-        out_specs=(SM, VM, VM),
+        out_specs=(SM, VM, HBM),
         scratch_shapes=[
+            pltpu.VMEM(block, BF),
             pltpu.VMEM((slides, PAY), F32),
             pltpu.VMEM((C, A), BF),
-            pltpu.SemaphoreType.DMA(()),
+            pltpu.SemaphoreType.DMA((S + 1,)),
         ],
         compiler_params=params(24),
         name="final",

time: 84.1 us -> 84.4 us (level)
  Pallas kernels: 16.2 us -> 19.1 us
  blocking collectives: 20.5 us -> 18.9 us
    pallas_call x0 -> x1, Pallas kernels: none -> 3.98 us  [shards(): pl.pallas_call(near_kernel, out_shape=partial, in_specs=[HBM] * len(sourc...]
    all_to_all x1, starting transfers between devices: 13.4 us -> 15.8 us  [shards(): received = lax.all_to_all(payload, 'z', 0, 0, tiled=True)]
    ppermute x1, starting transfers between devices: 4.04 us -> 1.92 us  [shards(): edge_own = lax.ppermute(edge, 'section', [(0, 1), (1, 0)])]
    all_to_all x1, blocking collectives: 20.5 us -> 18.9 us  [shards(): received = lax.all_to_all(payload, plane, 0, 0, tiled=True)]
    pallas_call x1, Pallas kernels: 9.28 us -> 7.68 us  [shards(): pl.pallas_call(forward_kernel, out_shape=forward_shapes, in_specs=[HBM] *...]
    ppermute x1, waiting for transfers between devices: 1.01 us -> 0.01 us  [shards(): edge_own = lax.ppermute(edge, 'section', [(0, 1), (1, 0)])]
    ppermute x4, waiting for transfers between devices: 0.01 us -> 0.88 us  [the longest x1 0.87 us: shards(): edge_near = lax.ppermute(edge, every, crossed(nearby))]
    unnamed x30 -> x20, local copies, waits for them, and re-layouts: 3.79 us -> 3.02 us
  transfers between devices with their start and end apart: 6 -> 6, of which waited for: 2 -> 2; matrix products, arithmetic and copies ran while one was open for 0% -> 0% of each run, Pallas kernels for 2% -> 7%
where the time goes in v2:
time: 84.4 us; the launch traced here: 83.9 us
  starting transfers between devices  33.3 us (39%)
  Pallas kernels  19.1 us (23%)
  blocking collectives  18.9 us (22%)
  waiting for transfers between devices  8.83 us (10%)
  local copies, waits for them, and re-layouts  3.02 us (4%)
    all_to_all x1, blocking collectives, shards(): received = lax.all_to_all(payload, plane, 0, 0, tiled=True)  18.9 us
    all_to_all x1, starting transfers between devices, shards(): received = lax.all_to_all(payload, 'z', 0, 0, tiled=True)  15.8 us
    ppermute x1, starting transfers between devices, shards(): edge_near = lax.ppermute(edge, every, crossed(nearby))  8.93 us
    all_to_all x1, waiting for transfers between devices, shards(): received = lax.all_to_all(payload, 'z', 0, 0, tiled=True)  7.95 us
    pallas_call x1, Pallas kernels, shards(): pl.pallas_call(forward_kernel, out_shape=forward_shapes, in_specs=[HBM] *...  7.68 us
    pallas_call x1, Pallas kernels, shards(): pl.pallas_call(near_kernel, out_shape=partial, in_specs=[HBM] * len(sourc...  3.98 us
    ppermute x1, starting transfers between devices, shards(): near = lax.ppermute(masked, tile, nearby)  3.95 us
    pallas_call x1, Pallas kernels, shards(): pl.pallas_call(final_kernel, out_shape=(jax.ShapeDtypeStruct((S,), F32),...  3.14 us
  transfers between devices with their start and end apart: 6, of which 2 were waited for; matrix products, arithmetic and copies ran while one was open for 0% of the time, Pallas kernels for 7%

profile of v2, /device:TPU:1, one launch (start us, length us, event | category | flops | bytes accessed | tf_op | source)
XLA Modules:
  0.0 83.9 jit_solution(8151983667267741698)
XLA Ops:
  0.6 2.7 %mask.1 = (bf16[2,3,64,384]{3,2,1,0:T(8,128)(2,1)}, bf16[2,3,8,384]{3,2,1,0:T(8,128)(2,1)}, f32[384,128]{1,0:T(8,128)}) custom-call(bf16[2,3,64,384]{3,2,1,0:T(8,128)(2,1)} %features_hbm.1, s32[3,2,64]{2,1,0:T(2,128)} %bitcast.3), custom_call_target="tpu_custom_call" | custom-call | tf_op jit(solution)/shard_map/mask/pallas_call | solution.py:353
  3.3 4.0 %collective-permute-start.3 = (bf16[2,3,64,384]{3,2,1,0:T(8,128)(2,1)}, bf16[2,3,64,384]{3,2,1,0:T(8,128)(2,1)}, u32[]{:S(2)}, u32[]{:S(2)}) collective-permute-start(bf16[2,3,64,384]{3,2,1,0:T(8,128)(2,1)} %get-tuple-element.12.own_hbm), channel_id=1, source_target_pairs={{0,8},{8,0},{16,24},{24,16},{32,40},{40,32},{48,56},{56,48},{64,72... | collective-permute-start | bytes 884744 | tf_op jit(solution)/shard_map/ppermute | solution.py:374
  7.3 1.4 %collective-permute-start = (bf16[2,3,64,384]{3,2,1,0:T(8,128)(2,1)}, bf16[2,3,64,384]{3,2,1,0:T(8,128)(2,1)}, u32[]{:S(2)}, u32[]{:S(2)}) collective-permute-start(bf16[2,3,64,384]{3,2,1,0:T(8,128)(2,1)} %get-tuple-element.12.own_hbm), channel_id=1, source_target_pairs={{8,16},{16,8},{24,32},{32,24},{40,48},{48,40},{56,64},{64,56},{72,... | collective-permute-start | bytes 884744 | tf_op jit(solution)/shard_map/ppermute | solution.py:373
  8.7 8.9 %collective-permute-start.4 = (bf16[2,3,8,384]{3,2,1,0:T(8,128)(2,1)}, bf16[2,3,8,384]{3,2,1,0:T(8,128)(2,1)}, u32[]{:S(2)}, u32[]{:S(2)}) collective-permute-start(bf16[2,3,8,384]{3,2,1,0:T(8,128)(2,1)} %get-tuple-element.13), channel_id=1, source_target_pairs={{0,264},{8,256},{16,280},{24,272},{32,296},{40,288},{48,312},{56,3... | collective-permute-start | bytes 110600 | tf_op jit(solution)/shard_map/ppermute | solution.py:376
  17.6 1.9 %collective-permute-start.2 = (bf16[2,3,8,384]{3,2,1,0:T(8,128)(2,1)}, bf16[2,3,8,384]{3,2,1,0:T(8,128)(2,1)}, u32[]{:S(2)}, u32[]{:S(2)}) collective-permute-start(bf16[2,3,8,384]{3,2,1,0:T(8,128)(2,1)} %get-tuple-element.13), channel_id=1, source_target_pairs={{0,256},{256,0},{1,257},{257,1},{2,258},{258,2},{3,259},{259,3},{4... | collective-permute-start | bytes 110600 | tf_op jit(solution)/shard_map/ppermute | solution.py:377
  19.5 1.3 %collective-permute-start.1 = (bf16[2,3,8,384]{3,2,1,0:T(8,128)(2,1)}, bf16[2,3,8,384]{3,2,1,0:T(8,128)(2,1)}, u32[]{:S(2)}, u32[]{:S(2)}) collective-permute-start(bf16[2,3,8,384]{3,2,1,0:T(8,128)(2,1)} %get-tuple-element.13), channel_id=1, source_target_pairs={{8,272},{16,264},{24,288},{32,280},{40,304},{48,296},{56,320},{64,... | collective-permute-start | bytes 110600 | tf_op jit(solution)/shard_map/ppermute | solution.py:375
  20.8 0.9 %collective-permute-done.4.edge_near_hbm = bf16[2,3,8,384]{3,2,1,0:T(8,128)(2,1)} collective-permute-done((bf16[2,3,8,384]{3,2,1,0:T(8,128)(2,1)}, bf16[2,3,8,384]{3,2,1,0:T(8,128)(2,1)}, u32[]{:S(2)}, u32[]{:S(2)}) %collective-permute-start.4) | collective-permute-done | bytes 36896 | tf_op jit(solution)/shard_map/ppermute | solution.py:376
  21.7 0.0 collective-permute-done.2.edge_own_hbm
  21.7 0.0 collective-permute-done.3.near_hbm
  21.7 4.0 %near.1.partial_hbm = f32[384,384]{1,0:T(8,128)} custom-call(bf16[2,3,64,384]{3,2,1,0:T(8,128)(2,1)} %get-tuple-element.12.own_hbm, bf16[2,3,8,384]{3,2,1,0:T(8,128)(2,1)} %collective-permute-done.2.edge_own_hbm, bf16[2,3,64,384]{3,2,1,0:T(8,128)(2,1)} %collective-permute-done.3.near_hbm, bf16[2,3,8,384]{3,2,1,0:T(8,128)(2,1)} %collective-permute-done.4.edge_near_hbm, ...), custom_call_target="tpu_custom_call" | custom-call | flops 100000000 | bytes 2000000 | tf_op jit(solution)/shard_map/near/pallas_call | solution.py:382
  25.7 0.0 collective-permute-done.1.edge_far_hbm
  25.7 0.0 collective-permute-done.far_hbm
  25.7 0.0 copy-start
  25.7 0.0 copy-start.6
  25.7 0.0 copy-start.7
  25.7 7.7 %forward.1 = (f32[16,2,1152]{2,1,0:T(2,128)}, bf16[384,1024]{1,0:T(8,128)(2,1)}, bf16[384,1024]{1,0:T(8,128)(2,1)}, f32[384,128]{1,0:T(8,128)}, bf16[384,256]{1,0:T(8,128)(2,1)}, /*index=5*/bf16[384,256]{1,0:T(8,128)(2,1)}) custom-call(bf16[2,3,64,384]{3,2,1,0:T(8,128)(2,1)} %collective-permute-done.far_hbm, ...), custom_call_target="tpu_custom_call" | custom-call | flops 2000000000 | bytes 8000000 | tf_op jit(solution)/shard_map/forward/pallas_call | solution.py:410
  33.4 15.8 %all-to-all-start = ((f32[16,2,1152]{2,1,0:T(2,128)}), f32[16,2,1152]{2,1,0:T(2,128)S(1)}, u32[]{:S(2)}, u32[]{:S(2)}) async-start(f32[16,2,1152]{2,1,0:T(2,128)} %get-tuple-element.15), calls=%async_computation | async-start | bytes 294912 | tf_op jit(solution)/shard_map/all_to_all | solution.py:444
  49.2 0.0 copy-done
  49.3 0.0 copy-done.6
  49.3 0.0 copy-done.7
  49.3 0.0 copy-start.2
  49.3 1.1 %copy-done.2 = bf16[384,1024]{1,0:T(8,128)(2,1)S(1)} copy-done((bf16[384,1024]{1,0:T(8,128)(2,1)S(1)}, bf16[384,1024]{1,0:T(8,128)(2,1)}, u32[]{:S(2)}) %copy-start.2) | copy-done | bytes 786456
  50.4 0.0 copy-start.8
  50.4 0.9 %copy-done.8 = bf16[384,256]{1,0:T(8,128)(2,1)S(1)} copy-done((bf16[384,256]{1,0:T(8,128)(2,1)S(1)}, bf16[384,256]{1,0:T(8,128)(2,1)}, u32[]{:S(2)}) %copy-start.8) | copy-done | bytes 196632
  51.3 0.0 copy-start.9
  51.3 0.9 %copy-done.9 = bf16[384,256]{1,0:T(8,128)(2,1)S(1)} copy-done((bf16[384,256]{1,0:T(8,128)(2,1)S(1)}, bf16[384,256]{1,0:T(8,128)(2,1)}, u32[]{:S(2)}) %copy-start.9) | copy-done | bytes 196632
  52.3 0.0 copy-start.4
  52.3 1.5 %gate_term.1.ahead = f32[384,384]{1,0:T(8,128)S(1)} custom-call(bf16[384,256]{1,0:T(8,128)(2,1)S(1)} %copy-done.8, bf16[384,256]{1,0:T(8,128)(2,1)S(1)} %copy-done.9, bf16[384,1024]{1,0:T(8,128)(2,1)S(1)} %copy-done.2, bf16[384,1024]{1,0:T(8,128)(2,1)S(1)} %copy-done, bf16[1024,256]{1,0:T(8,128)(2,1)S(1)} %copy-done.6, bf16[1024,256]{1,0:T(8,128)(2,1)S(1)} %copy-done.7), custom_call_target="tpu_custom_call" | custom-call | flops 1000000000 | bytes 4000000 | tf_op jit(solution)/shard_map/gate_term/pallas_call | solution.py:427
  53.8 0.0 copy-start.1
  53.8 0.0 copy-start.3
  53.8 0.0 copy-start.5
  53.8 8.0 %all-to-all-done.received = f32[16,2,1152]{2,1,0:T(2,128)S(1)} async-done(((f32[16,2,1152]{2,1,0:T(2,128)}), f32[16,2,1152]{2,1,0:T(2,128)S(1)}, u32[]{:S(2)}, u32[]{:S(2)}) %all-to-all-start) | async-done | bytes 147488 | tf_op jit(solution)/shard_map/all_to_all | solution.py:444
  61.8 0.1 add_up.1
  61.9 18.9 %all_to_all.10.received = f32[32,2,1152]{2,1,0:T(2,128)S(1)} all-to-all(f32[32,2,1152]{2,1,0:T(2,128)S(1)} %add_up.1), channel_id=1, replica_groups=mesh['section'=2,'z'=16,'xl'=2,'set'=8] {'section','xl','set'}, dimensions={0} | all-to-all | bytes 589824 | tf_op jit(solution)/shard_map/all_to_all | solution.py:453
  80.7 0.0 copy-done.4
  80.8 0.0 copy-done.1
  80.8 0.0 copy-done.3
  80.8 0.0 copy-done.5
  80.8 3.1 %final.1 = (f32[2]{0:T(128)}, f32[2,1024]{1,0:T(2,128)}, bf16[2,3,64,384]{3,2,1,0:T(8,128)(2,1)}) custom-call(f32[32,2,1152]{2,1,0:T(2,128)S(1)} %all_to_all.10.received, s32[1,16]{1,0:T(1,128)S(1)} %bitcast.2, bf16[384,1024]{1,0:T(8,128)(2,1)S(1)} %copy-done.1, bf16[384,1024]{1,0:T(8,128)(2,1)S(1)} %copy-done.3, f32[384,128]{1,0:T(8,128)S(1)} %copy-done.4, ...), custom_call_target="tpu_custom_call" | custom-call | tf_op jit(solution)/shard_map/final/pallas_call | solution.py:455
Async XLA Ops:
  3.3 18.4 %collective-permute-start.3 = (bf16[2,3,64,384]{3,2,1,0:T(8,128)(2,1)}, bf16[2,3,64,384]{3,2,1,0:T(8,128)(2,1)}, u32[]{:S(2)}, u32[]{:S(2)}) collective-permute-start(bf16[2,3,64,384]{3,2,1,0:T(8,128)(2,1)} %get-tuple-element.12.own_hbm), channel_id=1, source_target_pairs={{0,8},{8,0},{16,24},{24,16},{32,40},{40,32},{48,56},{56,48},{64,72... | collective-permute-start | bytes 884744 | tf_op jit(solution)/shard_map/ppermute | solution.py:374
  7.3 18.4 %collective-permute-start = (bf16[2,3,64,384]{3,2,1,0:T(8,128)(2,1)}, bf16[2,3,64,384]{3,2,1,0:T(8,128)(2,1)}, u32[]{:S(2)}, u32[]{:S(2)}) collective-permute-start(bf16[2,3,64,384]{3,2,1,0:T(8,128)(2,1)} %get-tuple-element.12.own_hbm), channel_id=1, source_target_pairs={{8,16},{16,8},{24,32},{32,24},{40,48},{48,40},{56,64},{64,56},{72,... | collective-permute-start | bytes 884744 | tf_op jit(solution)/shard_map/ppermute | solution.py:373
  8.7 13.0 %collective-permute-start.4 = (bf16[2,3,8,384]{3,2,1,0:T(8,128)(2,1)}, bf16[2,3,8,384]{3,2,1,0:T(8,128)(2,1)}, u32[]{:S(2)}, u32[]{:S(2)}) collective-permute-start(bf16[2,3,8,384]{3,2,1,0:T(8,128)(2,1)} %get-tuple-element.13), channel_id=1, source_target_pairs={{0,264},{8,256},{16,280},{24,272},{32,296},{40,288},{48,312},{56,3... | collective-permute-start | bytes 110600 | tf_op jit(solution)/shard_map/ppermute | solution.py:376
  17.6 4.1 %collective-permute-start.2 = (bf16[2,3,8,384]{3,2,1,0:T(8,128)(2,1)}, bf16[2,3,8,384]{3,2,1,0:T(8,128)(2,1)}, u32[]{:S(2)}, u32[]{:S(2)}) collective-permute-start(bf16[2,3,8,384]{3,2,1,0:T(8,128)(2,1)} %get-tuple-element.13), channel_id=1, source_target_pairs={{0,256},{256,0},{1,257},{257,1},{2,258},{258,2},{3,259},{259,3},{4... | collective-permute-start | bytes 110600 | tf_op jit(solution)/shard_map/ppermute | solution.py:377
  19.5 6.1 %collective-permute-start.1 = (bf16[2,3,8,384]{3,2,1,0:T(8,128)(2,1)}, bf16[2,3,8,384]{3,2,1,0:T(8,128)(2,1)}, u32[]{:S(2)}, u32[]{:S(2)}) collective-permute-start(bf16[2,3,8,384]{3,2,1,0:T(8,128)(2,1)} %get-tuple-element.13), channel_id=1, source_target_pairs={{8,272},{16,264},{24,288},{32,280},{40,304},{48,296},{56,320},{64,... | collective-permute-start | bytes 110600 | tf_op jit(solution)/shard_map/ppermute | solution.py:375
  25.7 23.5 %copy-start = (bf16[384,1024]{1,0:T(8,128)(2,1)S(1)}, bf16[384,1024]{1,0:T(8,128)(2,1)}, u32[]{:S(2)}) copy-start(bf16[384,1024]{1,0:T(8,128)(2,1)} %emb_hbm.5) | copy-start | bytes 2359300
  25.7 23.5 %copy-start.6 = (bf16[1024,256]{1,0:T(8,128)(2,1)S(1)}, bf16[1024,256]{1,0:T(8,128)(2,1)}, u32[]{:S(2)}) copy-start(bf16[1024,256]{1,0:T(8,128)(2,1)} %v_hbm.3) | copy-start | bytes 1572868
  25.7 23.5 %copy-start.7 = (bf16[1024,256]{1,0:T(8,128)(2,1)S(1)}, bf16[1024,256]{1,0:T(8,128)(2,1)}, u32[]{:S(2)}) copy-start(bf16[1024,256]{1,0:T(8,128)(2,1)} %u_hbm.3) | copy-start | bytes 1572868
  33.4 28.3 %all-to-all-start = ((f32[16,2,1152]{2,1,0:T(2,128)}), f32[16,2,1152]{2,1,0:T(2,128)S(1)}, u32[]{:S(2)}, u32[]{:S(2)}) async-start(f32[16,2,1152]{2,1,0:T(2,128)} %get-tuple-element.15), calls=%async_computation | async-start | bytes 294912 | tf_op jit(solution)/shard_map/all_to_all | solution.py:444
  49.3 1.1 %copy-start.2 = (bf16[384,1024]{1,0:T(8,128)(2,1)S(1)}, bf16[384,1024]{1,0:T(8,128)(2,1)}, u32[]{:S(2)}) copy-start(bf16[384,1024]{1,0:T(8,128)(2,1)} %get-tuple-element.18.slope) | copy-start | bytes 2359300
  50.4 0.9 %copy-start.8 = (bf16[384,256]{1,0:T(8,128)(2,1)S(1)}, bf16[384,256]{1,0:T(8,128)(2,1)}, u32[]{:S(2)}) copy-start(bf16[384,256]{1,0:T(8,128)(2,1)} %get-tuple-element.16.gate_v) | copy-start | bytes 589828
  51.3 0.9 %copy-start.9 = (bf16[384,256]{1,0:T(8,128)(2,1)S(1)}, bf16[384,256]{1,0:T(8,128)(2,1)}, u32[]{:S(2)}) copy-start(bf16[384,256]{1,0:T(8,128)(2,1)} %get-tuple-element.17.gate_u) | copy-start | bytes 589828
  52.3 28.5 %copy-start.4 = (f32[384,128]{1,0:T(8,128)S(1)}, f32[384,128]{1,0:T(8,128)}, u32[]{:S(2)}) copy-start(f32[384,128]{1,0:T(8,128)} %get-tuple-element.20.weight) | copy-start | bytes 589828
  53.8 27.0 %copy-start.1 = (bf16[384,1024]{1,0:T(8,128)(2,1)S(1)}, bf16[384,1024]{1,0:T(8,128)(2,1)}, u32[]{:S(2)}) copy-start(bf16[384,1024]{1,0:T(8,128)(2,1)} %get-tuple-element.19.embedded) | copy-start | bytes 2359300
  53.8 27.0 %copy-start.3 = (bf16[384,1024]{1,0:T(8,128)(2,1)S(1)}, bf16[384,1024]{1,0:T(8,128)(2,1)}, u32[]{:S(2)}) copy-start(bf16[384,1024]{1,0:T(8,128)(2,1)} %get-tuple-element.18.slope) | copy-start | bytes 2359300
  53.8 27.0 %copy-start.5 = (s32[16]{0:T(128)S(1)}, s32[16]{0:T(128)}, u32[]{:S(2)}) copy-start(s32[16]{0:T(128)} %param.17) | copy-start | bytes 196

commit v3 on v2

--- a/solution.py
+++ b/solution.py
@@ -34,29 +34,34 @@
 
 
 def mask_kernel(
-    features_hbm, tissue, masked_hbm, edge_hbm, flags_hbm, features, masked, edge, flags, sems
-):
-    where = [(s, r) for s in range(S) for r in range(R)]
-    arrive = copies_between([(features_hbm.at[p], features.at[p]) for p in where], sems)
-    leave = copies_between([(masked.at[p], masked_hbm.at[p]) for p in where], sems, S * R)
-    last_out = copies_between([(edge, edge_hbm), (flags, flags_hbm)], sems, 2 * S * R)
+    features_hbm, tissue_hbm, masked_hbm, edge_hbm, flags_hbm,
+    features, tissue, masked, edge, flags, sems,
+):
+    first_in = pltpu.make_async_copy(tissue_hbm, tissue, sems.at[2 * S])
+    arrive = copies_between([(features_hbm.at[s], features.at[s]) for s in range(S)], sems)
+    leave = copies_between([(masked.at[s], masked_hbm.at[s]) for s in range(S)], sems, S)
+    last_out = copies_between([(edge, edge_hbm), (flags, flags_hbm)], sems, 2 * S + 1)
+    first_in.start()
     for c in arrive:
         c.start()
     side = lax.axis_index("section")
     place = lax.broadcasted_iota(jnp.int32, (8, C), 0)
     first = jnp.where((place < 3) & (side == 1), 1.0, 0.0)
     last = jnp.where((place >= 5) & (side == 0), 1.0, 0.0)
-    rows = [tissue[r, s : s + 1, :].astype(F32) for s, r in where]
+    first_in.wait()
+    rows = [tissue[r, s : s + 1, :].astype(F32) for s in range(S) for r in range(R)]
     turned = jnp.concatenate(rows + rows[:2], axis=0).T
-    for i, (s, r) in enumerate(where):
-        here = jnp.broadcast_to(turned[:, i : i + 1], (W, LANES))
-        flags[i * W : i * W + W, :] = here
-        wide = jnp.concatenate([here] * (C // LANES), axis=1)
-        arrive[i].wait()
-        values = features[s, r].astype(F32) * wide
-        masked[s, r] = values.astype(BF)
-        leave[i].start()
-        edge[s, r] = (values[:8] * first + values[W - 8 :] * last).astype(BF)
+    for s in range(S):
+        arrive[s].wait()
+        for r in range(R):
+            i = s * R + r
+            here = jnp.broadcast_to(turned[:, i : i + 1], (W, LANES))
+            flags[i * W : i * W + W, :] = here
+            wide = jnp.concatenate([here] * (C // LANES), axis=1)
+            values = features[s, r].astype(F32) * wide
+            masked[s, r] = values.astype(BF)
+            edge[s, r] = (values[:8] * first + values[W - 8 :] * last).astype(BF)
+        leave[s].start()
     for c in last_out:
         c.start()
     for c in leave + last_out:
@@ -70,39 +75,30 @@
             grid_ref[s, at + r, W:PW, :] = edge[s, r].astype(F32)
 
 
-def convolve(grid_ref, acc_ref, conv_ref, dw_k, first, count, seed):
-    odd = lax.axis_index("xl") == 1
-
-    def turn(i, last):
-        return jnp.where(odd, last - i, i)
-
+def convolve(grid_ref, acc_ref, conv_ref, dw_k, places, seed):
     def conv_lane(step, carry):
         s = step // (C // LANES)
         lane = pl.multiple_of(lax.rem(step, C // LANES) * LANES, LANES)
         for col in range(PW // 8):
             cols = slice(col * 8, col * 8 + 8)
-            rows = [
-                grid_ref[s, base + turn(m, R - 1), cols, pl.ds(lane, LANES)]
-                for base in range(0, count, R)
-                for m in range(R)
-            ]
+            rows = [grid_ref[s, r, cols, pl.ds(lane, LANES)] for r in range(len(places))]
             for b in range(7):
                 sums = [None] * R
                 for a in range(7):
-                    pairs = [(a + n - first, n) for n in range(R) if 0 <= a + n - first < count]
+                    pairs = [(places.index(a + i), i) for i in range(R) if a + i in places]
                     if not pairs:
                         continue
-                    k = dw_k[turn(a, 6), b, pl.ds(lane, LANES)].reshape(1, LANES)
-                    for row, n in pairs:
+                    k = dw_k[a, b, pl.ds(lane, LANES)].reshape(1, LANES)
+                    for row, i in pairs:
                         term = rows[row] * k
-                        sums[n] = term if sums[n] is None else sums[n] + term
-                for n in range(R):
-                    acc_ref[n, b, cols, :] = sums[n]
-        for n in range(R):
-            total = acc_ref[n, 3]
+                        sums[i] = term if sums[i] is None else sums[i] + term
+                for i in range(R):
+                    acc_ref[i, b, cols, :] = sums[i]
+        for i in range(R):
+            total = acc_ref[i, 3]
             for b in (0, 1, 2, 4, 5, 6):
-                total = total + pltpu.roll(acc_ref[n, b], (3 - b) % PW, 0)
-            at = pl.multiple_of(s * R * W + turn(n, R - 1) * W, W)
+                total = total + pltpu.roll(acc_ref[i, b], (3 - b) % PW, 0)
+            at = pl.multiple_of(s * R * W + i * W, W)
             where = (pl.ds(at, W), pl.ds(lane, LANES))
             total = total[0:W]
             conv_ref[where] = total if seed is None else total + seed[where]
@@ -111,42 +107,35 @@
     lax.fori_loop(0, S * (C // LANES), conv_lane, 0)
 
 
-def near_kernel(
-    own_hbm, edge_own_hbm, near_hbm, edge_near_hbm, dw_k_hbm, partial_hbm,
-    own, edge_own, near, edge_near, dw_k, partial, grid_ref, acc_ref, sems,
-):
-    arrive = copies_between(
-        (
-            (own_hbm, own), (edge_own_hbm, edge_own), (near_hbm, near),
-            (edge_near_hbm, edge_near), (dw_k_hbm, dw_k),
-        ),
-        sems,
-    )
+def own_kernel(
+    own_hbm, edge_hbm, dw_k_hbm, partial_hbm, own, edge, dw_k, partial, grid_ref, acc_ref, sems
+):
+    arrive = copies_between(((own_hbm, own), (edge_hbm, edge), (dw_k_hbm, dw_k)), sems)
     for c in arrive:
         c.start()
     for c in arrive:
         c.wait()
-    fill(grid_ref, 0, own, edge_own)
-    fill(grid_ref, R, near, edge_near)
-    convolve(grid_ref, acc_ref, partial, dw_k, R, 2 * R, None)
-    leave = pltpu.make_async_copy(partial, partial_hbm, sems.at[5])
+    fill(grid_ref, 0, own, edge)
+    convolve(grid_ref, acc_ref, partial, dw_k, (3, 4, 5), None)
+    leave = pltpu.make_async_copy(partial, partial_hbm, sems.at[3])
     leave.start()
     leave.wait()
 
 
 def forward_kernel(
-    far_hbm, edge_far_hbm, partial_hbm, own_hbm, flags_hbm,
-    dw_k_hbm, dw_b_hbm, ln_g_hbm, ln_b_hbm, scale_hbm, e_bias_hbm, a_w_hbm,
+    above_hbm, edge_above_hbm, below_hbm, edge_below_hbm, dw_k_hbm, partial_hbm, own_hbm,
+    flags_hbm, dw_b_hbm, ln_g_hbm, ln_b_hbm, scale_hbm, e_bias_hbm, a_w_hbm,
     up_hbm, down_hbm, emb_hbm, v_hbm, u_hbm,
     payload_hbm, embedded_hbm, slope_hbm, weight_hbm, gate_v_hbm, gate_u_hbm,
-    far, edge_far, partial, own, flags,
-    dw_k, dw_b, ln_g, ln_b, scale, e_bias, a_w, up, down, emb, att_v, att_u,
+    above, edge_above, below, edge_below, dw_k, partial, own,
+    flags, dw_b, ln_g, ln_b, scale, e_bias, a_w, up, down, emb, att_v, att_u,
     payload, embedded_out, slope_out, weight_out, gate_v_out, gate_u_out,
     grid_ref, acc_ref, conv_ref, sums_ref, sems,
 ):
     blocks = copies_between(
         (
-            (far_hbm, far), (edge_far_hbm, edge_far), (dw_k_hbm, dw_k), (partial_hbm, partial),
+            (above_hbm, above), (edge_above_hbm, edge_above), (below_hbm, below),
+            (edge_below_hbm, edge_below), (dw_k_hbm, dw_k), (partial_hbm, partial),
         ),
         sems,
     )
@@ -156,25 +145,39 @@
             (scale_hbm, scale), (e_bias_hbm, e_bias), (a_w_hbm, a_w), (flags_hbm, flags),
         ),
         sems,
-        4,
+        6,
     )
     copies = copies_between(
-        ((up_hbm, up), (down_hbm, down), (emb_hbm, emb), (v_hbm, att_v), (u_hbm, att_u)), sems, 12
+        ((up_hbm, up), (down_hbm, down), (emb_hbm, emb), (v_hbm, att_v), (u_hbm, att_u)), sems, 14
+    )
+    embed_step = 512
+    halves = [slice(h, h + embed_step) for h in range(0, A, embed_step)]
+    early = copies_between(
+        [
+            (vm.at[:, cols], hbm.at[:, cols])
+            for cols in halves
+            for vm, hbm in ((embedded_out, embedded_hbm), (slope_out, slope_hbm))
+        ],
+        sems,
+        19,
     )
     results = copies_between(
         (
-            (embedded_out, embedded_hbm), (slope_out, slope_hbm), (payload, payload_hbm),
-            (weight_out, weight_hbm), (gate_v_out, gate_v_hbm), (gate_u_out, gate_u_hbm),
+            (weight_out, weight_hbm), (payload, payload_hbm), (gate_v_out, gate_v_hbm),
+            (gate_u_out, gate_u_hbm),
         ),
         sems,
-        17,
-    )
-    for c in blocks + small + copies:
-        c.start()
+        23,
+    )
     for c in blocks:
-        c.wait()
-    fill(grid_ref, 0, far, edge_far)
-    convolve(grid_ref, acc_ref, conv_ref, dw_k, 0, R, partial)
+        c.start()
+    for c in blocks:
+        c.wait()
+    for c in small + copies:
+        c.start()
+    fill(grid_ref, 0, above, edge_above)
+    fill(grid_ref, R, below, edge_below)
+    convolve(grid_ref, acc_ref, conv_ref, dw_k, (0, 1, 2, 6, 7, 8), partial)
     for c in small:
         c.wait()
     conv = conv_ref[...] + dw_b[...].reshape(1, -1)
@@ -185,7 +188,7 @@
     copies[0].wait()
     copies[1].wait()
     branch = jnp.zeros((N, C), F32)
-    step = 384
+    step = 768
     for h in range(0, HID, step):
         raised = jnp.dot(normed, up[:, h : h + step], preferred_element_type=F32)
         hidden = (0.5 * raised * (1.0 + lax.erf(raised * RSQRT2))).astype(BF)
@@ -199,19 +202,17 @@
     copies[4].wait()
     logits_v = jnp.zeros((N, AH), F32)
     logits_u = jnp.zeros((N, AH), F32)
-    step = 256
-    for h in range(0, A, step):
-        cols = slice(h, h + step)
+    for h, cols in enumerate(halves):
         pre = jnp.dot(trunk, emb[:, cols], preferred_element_type=F32) + e_bias[cols].reshape(1, -1)
         cdf = 0.5 * (1.0 + lax.erf(pre * RSQRT2))
         slope = cdf + pre * (RSQRT2PI * jnp.exp(-0.5 * pre * pre))
         out = (pre * cdf).astype(BF)
         embedded_out[:, cols] = out
         slope_out[:, cols] = slope.astype(BF)
+        early[2 * h].start()
+        early[2 * h + 1].start()
         logits_v = logits_v + jnp.dot(out, att_v[cols, :], preferred_element_type=F32)
         logits_u = logits_u + jnp.dot(out, att_u[cols, :], preferred_element_type=F32)
-    results[0].start()
-    results[1].start()
     tangent = jnp.tanh(logits_v)
     opening = jax.nn.sigmoid(logits_u)
     aw = a_w[...].reshape(1, -1)
@@ -219,7 +220,7 @@
     scores = jnp.sum(product, axis=-1, keepdims=True)
     weight = tissue * jnp.exp(scores)
     weight_out[...] = weight
-    results[3].start()
+    results[0].start()
     for s in range(S):
         rows = slice(s * HALF, s * HALF + HALF)
         w_here = weight[rows, :]
@@ -229,12 +230,12 @@
             sums_ref[s : s + 1, cols] = part
         sums_ref[s : s + 1, A:] = jnp.sum(w_here, axis=0, keepdims=True)
     payload[...] = jnp.broadcast_to(sums_ref[...][None], payload.shape)
-    results[2].start()
+    results[1].start()
     gate_v_out[...] = (aw * opening * (1.0 - tangent * tangent)).astype(BF)
     gate_u_out[...] = (product * (1.0 - opening)).astype(BF)
-    results[4].start()
-    results[5].start()
-    for c in results:
+    results[2].start()
+    results[3].start()
+    for c in early + results:
         c.wait()
 
 
@@ -267,10 +268,9 @@
 
 def final_kernel(
     received, partner, embedded, slope, weight, gate_term, emb_hbm,
-    loss_out, vector_out, grad_hbm, grad_out, sums_ref, emb, sems,
-):
-    fetch = pltpu.make_async_copy(emb_hbm, emb, sems.at[S])
-    leave = copies_between([(grad_out.at[s], grad_hbm.at[s]) for s in range(S)], sems)
+    loss_out, vector_out, grad_out, sums_ref, emb, sem,
+):
+    fetch = pltpu.make_async_copy(emb_hbm, emb, sem)
     fetch.start()
     position = lax.axis_index("set")
     slides = sums_ref.shape[0]
@@ -324,9 +324,6 @@
         score = jnp.concatenate([score] * (C // LANES), axis=1)
         fresh = share * back + score * gate_term[rows, :]
         grad_out[s] = fresh.astype(BF).reshape(R, W, C)
-        leave[s].start()
-    for c in leave:
-        c.wait()
 
 
 HBM = pl.BlockSpec(memory_space=pltpu.HBM)
@@ -353,51 +350,50 @@
     masked, edge, flags = pl.pallas_call(
         mask_kernel,
         out_shape=masked_shapes,
-        in_specs=[HBM, VM],
+        in_specs=[HBM, HBM],
         out_specs=(HBM, HBM, HBM),
-        scratch_shapes=[pltpu.VMEM(block, BF)]
+        scratch_shapes=[pltpu.VMEM(block, BF), pltpu.VMEM((R, S, W), jnp.int32)]
         + [pltpu.VMEM(x.shape, x.dtype) for x in masked_shapes]
-        + [pltpu.SemaphoreType.DMA((2 * S * R + 2,))],
+        + [pltpu.SemaphoreType.DMA((2 * S + 3,))],
         compiler_params=params(60),
         name="mask",
     )(features, tissue.transpose(1, 0, 2))
     tile = ("z", "xl")
     count = lax.axis_size(tile)
-    nearby = [(i, i ^ 1) for i in range(count)]
-    away = [(i, i + 1 if i % 2 else i - 1) for i in range(1, count - 1)]
+    upward = [(i, i + 1) for i in range(count - 1)]
+    downward = [(i + 1, i) for i in range(count - 1)]
+    above = lax.ppermute(masked, tile, upward)
+    below = lax.ppermute(masked, tile, downward)
+    edge_own = lax.ppermute(edge, "section", [(0, 1), (1, 0)])
     every = ("section",) + tile
-
-    def crossed(moves):
-        return [(c * count + i, (1 - c) * count + j) for c in range(2) for i, j in moves]
-
-    far = lax.ppermute(masked, tile, away)
-    near = lax.ppermute(masked, tile, nearby)
-    edge_far = lax.ppermute(edge, every, crossed(away))
-    edge_near = lax.ppermute(edge, every, crossed(nearby))
-    edge_own = lax.ppermute(edge, "section", [(0, 1), (1, 0)])
+    edge_above = lax.ppermute(
+        edge, every, [(c * count + i, (1 - c) * count + i + 1) for c in range(2) for i in range(count - 1)]
+    )
+    edge_below = lax.ppermute(
+        edge, every, [(c * count + i + 1, (1 - c) * count + i) for c in range(2) for i in range(count - 1)]
+    )
     depth = lax.axis_size("z")
 
-    sources = (masked, edge_own, near, edge_near, dw_kernel)
+    sources = (masked, edge_own, dw_kernel)
     partial = jax.ShapeDtypeStruct((N, C), F32)
     partial = pl.pallas_call(
-        near_kernel,
+        own_kernel,
         out_shape=partial,
         in_specs=[HBM] * len(sources),
         out_specs=HBM,
         scratch_shapes=[pltpu.VMEM(x.shape, x.dtype) for x in sources + (partial,)]
         + [
-            pltpu.VMEM((S, 2 * R, PW, C), F32),
+            pltpu.VMEM((S, R, PW, C), F32),
             pltpu.VMEM((R, 7, PW, LANES), F32),
-            pltpu.SemaphoreType.DMA((6,)),
+            pltpu.SemaphoreType.DMA((4,)),
         ],
         compiler_params=params(64),
         cost_estimate=pl.CostEstimate(flops=10**8, bytes_accessed=2 * 10**6, transcendentals=0),
-        name="near",
+        name="own_rows",
     )(*sources)
     operands = (
-        far, edge_far, partial, masked, flags,
-        dw_kernel, dw_bias, ln_gain, ln_bias, layer_scale, embed_bias, attn_w,
-        w_up, narrowing_projection_kernel, w_embed, attn_v, attn_u,
+        above, edge_above, below, edge_below, dw_kernel, partial, masked, flags, dw_bias, ln_gain,
+        ln_bias, layer_scale, embed_bias, attn_w, w_up, narrowing_projection_kernel, w_embed, attn_v, attn_u,
     )
     forward_shapes = (
         jax.ShapeDtypeStruct((depth, S, PAY), F32),
@@ -414,11 +410,11 @@
         out_specs=[HBM] * len(forward_shapes),
         scratch_shapes=[pltpu.VMEM(x.shape, x.dtype) for x in operands + forward_shapes]
         + [
-            pltpu.VMEM((S, R, PW, C), F32),
+            pltpu.VMEM((S, 2 * R, PW, C), F32),
             pltpu.VMEM((R, 7, PW, LANES), F32),
             pltpu.VMEM((N, C), F32),
             pltpu.VMEM((S, PAY), F32),
-            pltpu.SemaphoreType.DMA((len(operands) + len(forward_shapes),)),
+            pltpu.SemaphoreType.DMA((27,)),
         ],
         compiler_params=params(60),
         cost_estimate=pl.CostEstimate(flops=2 * 10**9, bytes_accessed=8 * 10**6, transcendentals=10**6),
@@ -460,12 +456,11 @@
             jax.ShapeDtypeStruct((S, R, W, C), BF),
         ),
         in_specs=[VM] * 6 + [HBM],
-        out_specs=(SM, VM, HBM),
+        out_specs=(SM, VM, VM),
         scratch_shapes=[
-            pltpu.VMEM(block, BF),
             pltpu.VMEM((slides, PAY), F32),
             pltpu.VMEM((C, A), BF),
-            pltpu.SemaphoreType.DMA((S + 1,)),
+            pltpu.SemaphoreType.DMA(()),
         ],
         compiler_params=params(24),
         name="final",

time: 84.4 us -> 82.1 us (0.973)
  Pallas kernels: 19.1 us -> 17 us
  waiting for transfers between devices: 8.83 us -> 7.72 us
    ppermute x1, starting transfers between devices: 1.92 us -> 8.75 us  [shards(): edge_own = lax.ppermute(edge, 'section', [(0, 1), (1, 0)])]
    all_to_all x1, starting transfers between devices: 15.8 us -> 12.1 us  [shards(): received = lax.all_to_all(payload, 'z', 0, 0, tiled=True)]
    ppermute x4, starting transfers between devices: 15.5 us -> 12.8 us  [the longest x1 5.29 us: shards(): above = lax.ppermute(masked, tile, upward)]
    pallas_call x2, Pallas kernels: 6.68 us -> 5.14 us  [the longest x1 3.2 us: shards(): pl.pallas_call(own_kernel, out_shape=partial, in_specs=[HBM] * len(source...]
    ppermute x4, waiting for transfers between devices: 0.88 us -> 0.01 us  [the longest x1 0.01 us: shards(): lax.ppermute(edge, every, [(c * count + i, (1 - c) * count + i + 1) for c...]
  transfers between devices with their start and end apart: 6 -> 6, of which waited for: 2 -> 1; matrix products, arithmetic and copies ran while one was open for 0% -> 0% of each run, Pallas kernels for 7% -> 6%
where the time goes in v3:
time: 82.1 us; the launch traced here: 81.7 us
  starting transfers between devices  33.6 us (41%)
  blocking collectives  19.5 us (24%)
  Pallas kernels  17 us (21%)
  waiting for transfers between devices  7.72 us (9%)
  local copies, waits for them, and re-layouts  3.02 us (4%)
  between operations  0.83 us (1%)
    all_to_all x1, blocking collectives, shards(): received = lax.all_to_all(payload, plane, 0, 0, tiled=True)  19.5 us
    all_to_all x1, starting transfers between devices, shards(): received = lax.all_to_all(payload, 'z', 0, 0, tiled=True)  12.1 us
    ppermute x1, starting transfers between devices, shards(): edge_own = lax.ppermute(edge, 'section', [(0, 1), (1, 0)])  8.75 us
    all_to_all x1, waiting for transfers between devices, shards(): received = lax.all_to_all(payload, 'z', 0, 0, tiled=True)  7.71 us
    pallas_call x1, Pallas kernels, shards(): pl.pallas_call(forward_kernel, out_shape=forward_shapes, in_specs=[HBM] *...  7.69 us
    ppermute x1, starting transfers between devices, shards(): above = lax.ppermute(masked, tile, upward)  5.29 us
    ppermute x1, starting transfers between devices, shards(): lax.ppermute(edge, every, [(c * count + i, (1 - c) * count + i + 1) for c...  4.87 us
    pallas_call x1, Pallas kernels, shards(): pl.pallas_call(own_kernel, out_shape=partial, in_specs=[HBM] * len(source...  3.2 us
  transfers between devices with their start and end apart: 6, of which 1 were waited for; matrix products, arithmetic and copies ran while one was open for 0% of the time, Pallas kernels for 6%

profile of v3, /device:TPU:1, one launch (start us, length us, event | category | flops | bytes accessed | tf_op | source)
XLA Modules:
  0.0 81.7 jit_solution(8808736010784679355)
XLA Ops:
  0.6 1.9 %mask.1 = (bf16[2,3,64,384]{3,2,1,0:T(8,128)(2,1)}, bf16[2,3,8,384]{3,2,1,0:T(8,128)(2,1)}, f32[384,128]{1,0:T(8,128)}) custom-call(bf16[2,3,64,384]{3,2,1,0:T(8,128)(2,1)} %features_hbm.1, s32[3,2,64]{2,1,0:T(2,128)} %bitcast.3), custom_call_target="tpu_custom_call" | custom-call | tf_op jit(solution)/shard_map/mask/pallas_call | solution.py:350
  2.6 1.3 %collective-permute-start.2 = (bf16[2,3,64,384]{3,2,1,0:T(8,128)(2,1)}, bf16[2,3,64,384]{3,2,1,0:T(8,128)(2,1)}, u32[]{:S(2)}, u32[]{:S(2)}) collective-permute-start(bf16[2,3,64,384]{3,2,1,0:T(8,128)(2,1)} %get-tuple-element.12.own_hbm), channel_id=1, source_target_pairs={{8,0},{16,8},{24,16},{32,24},{40,32},{48,40},{56,48},{64,56},{72,6... | collective-permute-start | bytes 884744 | tf_op jit(solution)/shard_map/ppermute | solution.py:366
  3.9 5.3 %collective-permute-start = (bf16[2,3,64,384]{3,2,1,0:T(8,128)(2,1)}, bf16[2,3,64,384]{3,2,1,0:T(8,128)(2,1)}, u32[]{:S(2)}, u32[]{:S(2)}) collective-permute-start(bf16[2,3,64,384]{3,2,1,0:T(8,128)(2,1)} %get-tuple-element.12.own_hbm), channel_id=1, source_target_pairs={{0,8},{8,16},{16,24},{24,32},{32,40},{40,48},{48,56},{56,64},{64,7... | collective-permute-start | bytes 884744 | tf_op jit(solution)/shard_map/ppermute | solution.py:365
  9.2 8.7 %collective-permute-start.4 = (bf16[2,3,8,384]{3,2,1,0:T(8,128)(2,1)}, bf16[2,3,8,384]{3,2,1,0:T(8,128)(2,1)}, u32[]{:S(2)}, u32[]{:S(2)}) collective-permute-start(bf16[2,3,8,384]{3,2,1,0:T(8,128)(2,1)} %get-tuple-element.13), channel_id=1, source_target_pairs={{0,256},{256,0},{1,257},{257,1},{2,258},{258,2},{3,259},{259,3},{4... | collective-permute-start | bytes 110600 | tf_op jit(solution)/shard_map/ppermute | solution.py:367
  17.9 1.3 %collective-permute-start.3 = (bf16[2,3,8,384]{3,2,1,0:T(8,128)(2,1)}, bf16[2,3,8,384]{3,2,1,0:T(8,128)(2,1)}, u32[]{:S(2)}, u32[]{:S(2)}) collective-permute-start(bf16[2,3,8,384]{3,2,1,0:T(8,128)(2,1)} %get-tuple-element.13), channel_id=1, source_target_pairs={{8,256},{16,264},{24,272},{32,280},{40,288},{48,296},{56,304},{64,... | collective-permute-start | bytes 110600 | tf_op jit(solution)/shard_map/ppermute | solution.py:372
  19.2 4.9 %collective-permute-start.1 = (bf16[2,3,8,384]{3,2,1,0:T(8,128)(2,1)}, bf16[2,3,8,384]{3,2,1,0:T(8,128)(2,1)}, u32[]{:S(2)}, u32[]{:S(2)}) collective-permute-start(bf16[2,3,8,384]{3,2,1,0:T(8,128)(2,1)} %get-tuple-element.13), channel_id=1, source_target_pairs={{0,264},{8,272},{16,280},{24,288},{32,296},{40,304},{48,312},{56,3... | collective-permute-start | bytes 110600 | tf_op jit(solution)/shard_map/ppermute | solution.py:369
  24.1 0.0 collective-permute-done.4.edge_hbm
  24.1 3.2 %own_rows.1.partial_hbm = f32[384,384]{1,0:T(8,128)} custom-call(bf16[2,3,64,384]{3,2,1,0:T(8,128)(2,1)} %get-tuple-element.12.own_hbm, bf16[2,3,8,384]{3,2,1,0:T(8,128)(2,1)} %collective-permute-done.4.edge_hbm, f32[7,7,384]{2,1,0:T(8,128)} %dw_k_hbm.3), custom_call_target="tpu_custom_call" | custom-call | flops 100000000 | bytes 2000000 | tf_op jit(solution)/shard_map/own_rows/pallas_call | solution.py:379
  27.3 0.0 collective-permute-done.3.edge_below_hbm
  27.3 0.0 collective-permute-done.1.edge_above_hbm
  27.3 0.0 collective-permute-done.2.below_hbm
  27.3 0.0 collective-permute-done.above_hbm
  27.4 0.0 copy-start
  27.4 0.0 copy-start.6
  27.4 0.0 copy-start.7
  27.4 7.7 %forward.1 = (f32[16,2,1152]{2,1,0:T(2,128)}, bf16[384,1024]{1,0:T(8,128)(2,1)}, bf16[384,1024]{1,0:T(8,128)(2,1)}, f32[384,128]{1,0:T(8,128)}, bf16[384,256]{1,0:T(8,128)(2,1)}, /*index=5*/bf16[384,256]{1,0:T(8,128)(2,1)}) custom-call(bf16[2,3,64,384]{3,2,1,0:T(8,128)(2,1)} %collective-permute-done.above_hbm, ...), custom_call_target="tpu_custom_call" | custom-call | flops 2000000000 | bytes 8000000 | tf_op jit(solution)/shard_map/forward/pallas_call | solution.py:406
  35.1 12.1 %all-to-all-start = ((f32[16,2,1152]{2,1,0:T(2,128)}), f32[16,2,1152]{2,1,0:T(2,128)S(1)}, u32[]{:S(2)}, u32[]{:S(2)}) async-start(f32[16,2,1152]{2,1,0:T(2,128)} %get-tuple-element.15), calls=%async_computation | async-start | bytes 294912 | tf_op jit(solution)/shard_map/all_to_all | solution.py:440
  47.2 0.0 copy-done
  47.2 0.0 copy-done.6
  47.2 0.0 copy-done.7
  47.2 0.0 copy-start.2
  47.3 1.1 %copy-done.2 = bf16[384,1024]{1,0:T(8,128)(2,1)S(1)} copy-done((bf16[384,1024]{1,0:T(8,128)(2,1)S(1)}, bf16[384,1024]{1,0:T(8,128)(2,1)}, u32[]{:S(2)}) %copy-start.2) | copy-done | bytes 786456
  48.4 0.0 copy-start.8
  48.4 0.9 %copy-done.8 = bf16[384,256]{1,0:T(8,128)(2,1)S(1)} copy-done((bf16[384,256]{1,0:T(8,128)(2,1)S(1)}, bf16[384,256]{1,0:T(8,128)(2,1)}, u32[]{:S(2)}) %copy-start.8) | copy-done | bytes 196632
  49.3 0.0 copy-start.9
  49.3 0.9 %copy-done.9 = bf16[384,256]{1,0:T(8,128)(2,1)S(1)} copy-done((bf16[384,256]{1,0:T(8,128)(2,1)S(1)}, bf16[384,256]{1,0:T(8,128)(2,1)}, u32[]{:S(2)}) %copy-start.9) | copy-done | bytes 196632
  50.2 0.0 copy-start.4
  50.2 1.5 %gate_term.1.ahead = f32[384,384]{1,0:T(8,128)S(1)} custom-call(bf16[384,256]{1,0:T(8,128)(2,1)S(1)} %copy-done.8, bf16[384,256]{1,0:T(8,128)(2,1)S(1)} %copy-done.9, bf16[384,1024]{1,0:T(8,128)(2,1)S(1)} %copy-done.2, bf16[384,1024]{1,0:T(8,128)(2,1)S(1)} %copy-done, bf16[1024,256]{1,0:T(8,128)(2,1)S(1)} %copy-done.6, bf16[1024,256]{1,0:T(8,128)(2,1)S(1)} %copy-done.7), custom_call_target="tpu_custom_call" | custom-call | flops 1000000000 | bytes 4000000 | tf_op jit(solution)/shard_map/gate_term/pallas_call | solution.py:423
  51.8 0.0 copy-start.1
  51.8 0.0 copy-start.3
  51.8 0.0 copy-start.5
  51.8 7.7 %all-to-all-done.received = f32[16,2,1152]{2,1,0:T(2,128)S(1)} async-done(((f32[16,2,1152]{2,1,0:T(2,128)}), f32[16,2,1152]{2,1,0:T(2,128)S(1)}, u32[]{:S(2)}, u32[]{:S(2)}) %all-to-all-start) | async-done | bytes 147488 | tf_op jit(solution)/shard_map/all_to_all | solution.py:440
  59.5 0.1 add_up.1
  59.6 19.5 %all_to_all.10.received = f32[32,2,1152]{2,1,0:T(2,128)S(1)} all-to-all(f32[32,2,1152]{2,1,0:T(2,128)S(1)} %add_up.1), channel_id=1, replica_groups=mesh['section'=2,'z'=16,'xl'=2,'set'=8] {'section','xl','set'}, dimensions={0} | all-to-all | bytes 589824 | tf_op jit(solution)/shard_map/all_to_all | solution.py:449
  79.1 0.0 copy-done.4
  79.1 0.0 copy-done.1
  79.1 0.0 copy-done.3
  79.1 0.0 copy-done.5
  79.1 2.6 %final.1 = (f32[2]{0:T(128)}, f32[2,1024]{1,0:T(2,128)}, bf16[2,3,64,384]{3,2,1,0:T(8,128)(2,1)}) custom-call(f32[32,2,1152]{2,1,0:T(2,128)S(1)} %all_to_all.10.received, s32[1,16]{1,0:T(1,128)S(1)} %bitcast.2, bf16[384,1024]{1,0:T(8,128)(2,1)S(1)} %copy-done.1, bf16[384,1024]{1,0:T(8,128)(2,1)S(1)} %copy-done.3, f32[384,128]{1,0:T(8,128)S(1)} %copy-done.4, ...), custom_call_target="tpu_custom_call" | custom-call | tf_op jit(solution)/shard_map/final/pallas_call | solution.py:451
Async XLA Ops:
  2.6 24.8 %collective-permute-start.2 = (bf16[2,3,64,384]{3,2,1,0:T(8,128)(2,1)}, bf16[2,3,64,384]{3,2,1,0:T(8,128)(2,1)}, u32[]{:S(2)}, u32[]{:S(2)}) collective-permute-start(bf16[2,3,64,384]{3,2,1,0:T(8,128)(2,1)} %get-tuple-element.12.own_hbm), channel_id=1, source_target_pairs={{8,0},{16,8},{24,16},{32,24},{40,32},{48,40},{56,48},{64,56},{72,6... | collective-permute-start | bytes 884744 | tf_op jit(solution)/shard_map/ppermute | solution.py:366
  3.9 23.5 %collective-permute-start = (bf16[2,3,64,384]{3,2,1,0:T(8,128)(2,1)}, bf16[2,3,64,384]{3,2,1,0:T(8,128)(2,1)}, u32[]{:S(2)}, u32[]{:S(2)}) collective-permute-start(bf16[2,3,64,384]{3,2,1,0:T(8,128)(2,1)} %get-tuple-element.12.own_hbm), channel_id=1, source_target_pairs={{0,8},{8,16},{16,24},{24,32},{32,40},{40,48},{48,56},{56,64},{64,7... | collective-permute-start | bytes 884744 | tf_op jit(solution)/shard_map/ppermute | solution.py:365
  9.2 14.9 %collective-permute-start.4 = (bf16[2,3,8,384]{3,2,1,0:T(8,128)(2,1)}, bf16[2,3,8,384]{3,2,1,0:T(8,128)(2,1)}, u32[]{:S(2)}, u32[]{:S(2)}) collective-permute-start(bf16[2,3,8,384]{3,2,1,0:T(8,128)(2,1)} %get-tuple-element.13), channel_id=1, source_target_pairs={{0,256},{256,0},{1,257},{257,1},{2,258},{258,2},{3,259},{259,3},{4... | collective-permute-start | bytes 110600 | tf_op jit(solution)/shard_map/ppermute | solution.py:367
  17.9 9.4 %collective-permute-start.3 = (bf16[2,3,8,384]{3,2,1,0:T(8,128)(2,1)}, bf16[2,3,8,384]{3,2,1,0:T(8,128)(2,1)}, u32[]{:S(2)}, u32[]{:S(2)}) collective-permute-start(bf16[2,3,8,384]{3,2,1,0:T(8,128)(2,1)} %get-tuple-element.13), channel_id=1, source_target_pairs={{8,256},{16,264},{24,272},{32,280},{40,288},{48,296},{56,304},{64,... | collective-permute-start | bytes 110600 | tf_op jit(solution)/shard_map/ppermute | solution.py:372
  19.2 8.1 %collective-permute-start.1 = (bf16[2,3,8,384]{3,2,1,0:T(8,128)(2,1)}, bf16[2,3,8,384]{3,2,1,0:T(8,128)(2,1)}, u32[]{:S(2)}, u32[]{:S(2)}) collective-permute-start(bf16[2,3,8,384]{3,2,1,0:T(8,128)(2,1)} %get-tuple-element.13), channel_id=1, source_target_pairs={{0,264},{8,272},{16,280},{24,288},{32,296},{40,304},{48,312},{56,3... | collective-permute-start | bytes 110600 | tf_op jit(solution)/shard_map/ppermute | solution.py:369
  27.4 19.9 %copy-start = (bf16[384,1024]{1,0:T(8,128)(2,1)S(1)}, bf16[384,1024]{1,0:T(8,128)(2,1)}, u32[]{:S(2)}) copy-start(bf16[384,1024]{1,0:T(8,128)(2,1)} %emb_hbm.5) | copy-start | bytes 2359300
  27.4 19.9 %copy-start.6 = (bf16[1024,256]{1,0:T(8,128)(2,1)S(1)}, bf16[1024,256]{1,0:T(8,128)(2,1)}, u32[]{:S(2)}) copy-start(bf16[1024,256]{1,0:T(8,128)(2,1)} %v_hbm.3) | copy-start | bytes 1572868
  27.4 19.9 %copy-start.7 = (bf16[1024,256]{1,0:T(8,128)(2,1)S(1)}, bf16[1024,256]{1,0:T(8,128)(2,1)}, u32[]{:S(2)}) copy-start(bf16[1024,256]{1,0:T(8,128)(2,1)} %u_hbm.3) | copy-start | bytes 1572868
  35.1 24.4 %all-to-all-start = ((f32[16,2,1152]{2,1,0:T(2,128)}), f32[16,2,1152]{2,1,0:T(2,128)S(1)}, u32[]{:S(2)}, u32[]{:S(2)}) async-start(f32[16,2,1152]{2,1,0:T(2,128)} %get-tuple-element.15), calls=%async_computation | async-start | bytes 294912 | tf_op jit(solution)/shard_map/all_to_all | solution.py:440
  47.2 1.1 %copy-start.2 = (bf16[384,1024]{1,0:T(8,128)(2,1)S(1)}, bf16[384,1024]{1,0:T(8,128)(2,1)}, u32[]{:S(2)}) copy-start(bf16[384,1024]{1,0:T(8,128)(2,1)} %get-tuple-element.18.slope) | copy-start | bytes 2359300
  48.4 0.9 %copy-start.8 = (bf16[384,256]{1,0:T(8,128)(2,1)S(1)}, bf16[384,256]{1,0:T(8,128)(2,1)}, u32[]{:S(2)}) copy-start(bf16[384,256]{1,0:T(8,128)(2,1)} %get-tuple-element.16.gate_v) | copy-start | bytes 589828
  49.3 0.9 %copy-start.9 = (bf16[384,256]{1,0:T(8,128)(2,1)S(1)}, bf16[384,256]{1,0:T(8,128)(2,1)}, u32[]{:S(2)}) copy-start(bf16[384,256]{1,0:T(8,128)(2,1)} %get-tuple-element.17.gate_u) | copy-start | bytes 589828
  50.2 28.8 %copy-start.4 = (f32[384,128]{1,0:T(8,128)S(1)}, f32[384,128]{1,0:T(8,128)}, u32[]{:S(2)}) copy-start(f32[384,128]{1,0:T(8,128)} %get-tuple-element.20.weight) | copy-start | bytes 589828
  51.8 27.3 %copy-start.1 = (bf16[384,1024]{1,0:T(8,128)(2,1)S(1)}, bf16[384,1024]{1,0:T(8,128)(2,1)}, u32[]{:S(2)}) copy-start(bf16[384,1024]{1,0:T(8,128)(2,1)} %get-tuple-element.19.embedded) | copy-start | bytes 2359300
  51.8 27.3 %copy-start.3 = (bf16[384,1024]{1,0:T(8,128)(2,1)S(1)}, bf16[384,1024]{1,0:T(8,128)(2,1)}, u32[]{:S(2)}) copy-start(bf16[384,1024]{1,0:T(8,128)(2,1)} %get-tuple-element.18.slope) | copy-start | bytes 2359300
  51.8 27.3 %copy-start.5 = (s32[16]{0:T(128)S(1)}, s32[16]{0:T(128)}, u32[]{:S(2)}) copy-start(s32[16]{0:T(128)} %param.17) | copy-start | bytes 196

commit v4 on v3

--- a/solution.py
+++ b/solution.py
@@ -71,17 +71,20 @@
 def fill(grid_ref, at, block, edge):
     for s in range(S):
         for r in range(R):
-            grid_ref[s, at + r, 0:W, :] = block[s, r].astype(F32)
-            grid_ref[s, at + r, W:PW, :] = edge[s, r].astype(F32)
-
-
-def convolve(grid_ref, acc_ref, conv_ref, dw_k, places, seed):
+            if block is not None:
+                grid_ref[s, at + r, 0:W, :] = block[s, r].astype(F32)
+            if edge is not None:
+                grid_ref[s, at + r, W:PW, :] = edge[s, r].astype(F32)
+
+
+def convolve(grid_ref, acc_ref, conv_ref, dw_k, inner, outer, seed):
     def conv_lane(step, carry):
         s = step // (C // LANES)
         lane = pl.multiple_of(lax.rem(step, C // LANES) * LANES, LANES)
         for col in range(PW // 8):
             cols = slice(col * 8, col * 8 + 8)
-            rows = [grid_ref[s, r, cols, pl.ds(lane, LANES)] for r in range(len(places))]
+            places = inner if col < W // 8 else outer
+            rows = [grid_ref[s, r, cols, pl.ds(lane, LANES)] for r in places]
             for b in range(7):
                 sums = [None] * R
                 for a in range(7):
@@ -93,7 +96,8 @@
                         term = rows[row] * k
                         sums[i] = term if sums[i] is None else sums[i] + term
                 for i in range(R):
-                    acc_ref[i, b, cols, :] = sums[i]
+                    empty = sums[i] is None
+                    acc_ref[i, b, cols, :] = jnp.zeros((8, LANES), F32) if empty else sums[i]
         for i in range(R):
             total = acc_ref[i, 3]
             for b in (0, 1, 2, 4, 5, 6):
@@ -108,26 +112,26 @@
 
 
 def own_kernel(
-    own_hbm, edge_hbm, dw_k_hbm, partial_hbm, own, edge, dw_k, partial, grid_ref, acc_ref, sems
-):
-    arrive = copies_between(((own_hbm, own), (edge_hbm, edge), (dw_k_hbm, dw_k)), sems)
+    own_hbm, dw_k_hbm, partial_hbm, own, dw_k, partial, grid_ref, acc_ref, sems
+):
+    arrive = copies_between(((own_hbm, own), (dw_k_hbm, dw_k)), sems)
     for c in arrive:
         c.start()
     for c in arrive:
         c.wait()
-    fill(grid_ref, 0, own, edge)
-    convolve(grid_ref, acc_ref, partial, dw_k, (3, 4, 5), None)
-    leave = pltpu.make_async_copy(partial, partial_hbm, sems.at[3])
+    fill(grid_ref, R, own, None)
+    convolve(grid_ref, acc_ref, partial, dw_k, (3, 4, 5), (), None)
+    leave = pltpu.make_async_copy(partial, partial_hbm, sems.at[2])
     leave.start()
     leave.wait()
 
 
 def forward_kernel(
-    above_hbm, edge_above_hbm, below_hbm, edge_below_hbm, dw_k_hbm, partial_hbm, own_hbm,
+    edge_own_hbm, above_hbm, edge_above_hbm, below_hbm, edge_below_hbm, dw_k_hbm, partial_hbm, own_hbm,
     flags_hbm, dw_b_hbm, ln_g_hbm, ln_b_hbm, scale_hbm, e_bias_hbm, a_w_hbm,
     up_hbm, down_hbm, emb_hbm, v_hbm, u_hbm,
     payload_hbm, embedded_hbm, slope_hbm, weight_hbm, gate_v_hbm, gate_u_hbm,
-    above, edge_above, below, edge_below, dw_k, partial, own,
+    edge_own, above, edge_above, below, edge_below, dw_k, partial, own,
     flags, dw_b, ln_g, ln_b, scale, e_bias, a_w, up, down, emb, att_v, att_u,
     payload, embedded_out, slope_out, weight_out, gate_v_out, gate_u_out,
     grid_ref, acc_ref, conv_ref, sums_ref, sems,
@@ -135,7 +139,8 @@
     blocks = copies_between(
         (
             (above_hbm, above), (edge_above_hbm, edge_above), (below_hbm, below),
-            (edge_below_hbm, edge_below), (dw_k_hbm, dw_k), (partial_hbm, partial),
+            (edge_below_hbm, edge_below), (edge_own_hbm, edge_own), (dw_k_hbm, dw_k),
+            (partial_hbm, partial),
         ),
         sems,
     )
@@ -145,10 +150,10 @@
             (scale_hbm, scale), (e_bias_hbm, e_bias), (a_w_hbm, a_w), (flags_hbm, flags),
         ),
         sems,
-        6,
+        7,
     )
     copies = copies_between(
-        ((up_hbm, up), (down_hbm, down), (emb_hbm, emb), (v_hbm, att_v), (u_hbm, att_u)), sems, 14
+        ((up_hbm, up), (down_hbm, down), (emb_hbm, emb), (v_hbm, att_v), (u_hbm, att_u)), sems, 15
     )
     embed_step = 512
     halves = [slice(h, h + embed_step) for h in range(0, A, embed_step)]
@@ -159,7 +164,7 @@
             for vm, hbm in ((embedded_out, embedded_hbm), (slope_out, slope_hbm))
         ],
         sems,
-        19,
+        20,
     )
     results = copies_between(
         (
@@ -167,7 +172,7 @@
             (gate_u_out, gate_u_hbm),
         ),
         sems,
-        23,
+        24,
     )
     for c in blocks:
         c.start()
@@ -176,8 +181,11 @@
     for c in small + copies:
         c.start()
     fill(grid_ref, 0, above, edge_above)
-    fill(grid_ref, R, below, edge_below)
-    convolve(grid_ref, acc_ref, conv_ref, dw_k, (0, 1, 2, 6, 7, 8), partial)
+    fill(grid_ref, R, None, edge_own)
+    fill(grid_ref, 2 * R, below, edge_below)
+    convolve(
+        grid_ref, acc_ref, conv_ref, dw_k, (0, 1, 2, 6, 7, 8), tuple(range(3 * R)), partial
+    )
     for c in small:
         c.wait()
     conv = conv_ref[...] + dw_b[...].reshape(1, -1)
@@ -374,7 +382,7 @@
     )
     depth = lax.axis_size("z")
 
-    sources = (masked, edge_own, dw_kernel)
+    sources = (masked, dw_kernel)
     partial = jax.ShapeDtypeStruct((N, C), F32)
     partial = pl.pallas_call(
         own_kernel,
@@ -383,16 +391,16 @@
         out_specs=HBM,
         scratch_shapes=[pltpu.VMEM(x.shape, x.dtype) for x in sources + (partial,)]
         + [
-            pltpu.VMEM((S, R, PW, C), F32),
+            pltpu.VMEM((S, 3 * R, PW, C), F32),
             pltpu.VMEM((R, 7, PW, LANES), F32),
-            pltpu.SemaphoreType.DMA((4,)),
+            pltpu.SemaphoreType.DMA((3,)),
         ],
         compiler_params=params(64),
         cost_estimate=pl.CostEstimate(flops=10**8, bytes_accessed=2 * 10**6, transcendentals=0),
         name="own_rows",
     )(*sources)
     operands = (
-        above, edge_above, below, edge_below, dw_kernel, partial, masked, flags, dw_bias, ln_gain,
+        edge_own, above, edge_above, below, edge_below, dw_kernel, partial, masked, flags, dw_bias, ln_gain,
         ln_bias, layer_scale, embed_bias, attn_w, w_up, narrowing_projection_kernel, w_embed, attn_v, attn_u,
     )
     forward_shapes = (
@@ -410,11 +418,11 @@
         out_specs=[HBM] * len(forward_shapes),
         scratch_shapes=[pltpu.VMEM(x.shape, x.dtype) for x in operands + forward_shapes]
         + [
-            pltpu.VMEM((S, 2 * R, PW, C), F32),
+            pltpu.VMEM((S, 3 * R, PW, C), F32),
             pltpu.VMEM((R, 7, PW, LANES), F32),
             pltpu.VMEM((N, C), F32),
             pltpu.VMEM((S, PAY), F32),
-            pltpu.SemaphoreType.DMA((27,)),
+            pltpu.SemaphoreType.DMA((28,)),
         ],
         compiler_params=params(60),
         cost_estimate=pl.CostEstimate(flops=2 * 10**9, bytes_accessed=8 * 10**6, transcendentals=10**6),

time: 82.1 us -> 80.4 us (0.979)
  starting transfers between devices: 33.6 us -> 31.6 us
    ppermute x1, starting transfers between devices: 4.87 us -> 8.92 us  [shards(): lax.ppermute(edge, every, [(c * count + i, (1 - c) * count + i + 1) for c...]
    ppermute x1, starting transfers between devices: 8.75 us -> 4.71 us  [shards(): edge_own = lax.ppermute(edge, 'section', [(0, 1), (1, 0)])]
    all_to_all x1, starting transfers between devices: 12.1 us -> 10.1 us  [shards(): received = lax.all_to_all(payload, 'z', 0, 0, tiled=True)]
where the time goes in v4:
time: 80.4 us; the launch traced here: 79.9 us
  starting transfers between devices  31.6 us (39%)
  blocking collectives  19.9 us (25%)
  Pallas kernels  17 us (21%)
  waiting for transfers between devices  7.56 us (9%)
  local copies, waits for them, and re-layouts  3.02 us (4%)
  between operations  0.83 us (1%)
    all_to_all x1, blocking collectives, shards(): received = lax.all_to_all(payload, plane, 0, 0, tiled=True)  19.9 us
    all_to_all x1, starting transfers between devices, shards(): received = lax.all_to_all(payload, 'z', 0, 0, tiled=True)  10.1 us
    ppermute x1, starting transfers between devices, shards(): lax.ppermute(edge, every, [(c * count + i, (1 - c) * count + i + 1) for c...  8.92 us
    pallas_call x1, Pallas kernels, shards(): pl.pallas_call(forward_kernel, out_shape=forward_shapes, in_specs=[HBM] *...  7.81 us
    all_to_all x1, waiting for transfers between devices, shards(): received = lax.all_to_all(payload, 'z', 0, 0, tiled=True)  7.54 us
    ppermute x1, starting transfers between devices, shards(): above = lax.ppermute(masked, tile, upward)  5.29 us
    ppermute x1, starting transfers between devices, shards(): edge_own = lax.ppermute(edge, 'section', [(0, 1), (1, 0)])  4.71 us
    pallas_call x1, Pallas kernels, shards(): pl.pallas_call(own_kernel, out_shape=partial, in_specs=[HBM] * len(source...  3.06 us
  transfers between devices with their start and end apart: 6, of which 1 were waited for; matrix products, arithmetic and copies ran while one was open for 0% of the time, Pallas kernels for 6%

profile of v4, /device:TPU:1, one launch (start us, length us, event | category | flops | bytes accessed | tf_op | source)
XLA Modules:
  0.0 79.9 jit_solution(11216436931375017682)
XLA Ops:
  0.6 1.9 %mask.1 = (bf16[2,3,64,384]{3,2,1,0:T(8,128)(2,1)}, bf16[2,3,8,384]{3,2,1,0:T(8,128)(2,1)}, f32[384,128]{1,0:T(8,128)}) custom-call(bf16[2,3,64,384]{3,2,1,0:T(8,128)(2,1)} %features_hbm.1, s32[3,2,64]{2,1,0:T(2,128)} %bitcast.3), custom_call_target="tpu_custom_call" | custom-call | tf_op jit(solution)/shard_map/mask/pallas_call | solution.py:358
  2.6 1.3 %collective-permute-start.3 = (bf16[2,3,64,384]{3,2,1,0:T(8,128)(2,1)}, bf16[2,3,64,384]{3,2,1,0:T(8,128)(2,1)}, u32[]{:S(2)}, u32[]{:S(2)}) collective-permute-start(bf16[2,3,64,384]{3,2,1,0:T(8,128)(2,1)} %get-tuple-element.13.own_hbm), channel_id=1, source_target_pairs={{8,0},{16,8},{24,16},{32,24},{40,32},{48,40},{56,48},{64,56},{72,6... | collective-permute-start | bytes 884744 | tf_op jit(solution)/shard_map/ppermute | solution.py:374
  3.9 5.3 %collective-permute-start.1 = (bf16[2,3,64,384]{3,2,1,0:T(8,128)(2,1)}, bf16[2,3,64,384]{3,2,1,0:T(8,128)(2,1)}, u32[]{:S(2)}, u32[]{:S(2)}) collective-permute-start(bf16[2,3,64,384]{3,2,1,0:T(8,128)(2,1)} %get-tuple-element.13.own_hbm), channel_id=1, source_target_pairs={{0,8},{8,16},{16,24},{24,32},{32,40},{40,48},{48,56},{56,64},{64,7... | collective-permute-start | bytes 884744 | tf_op jit(solution)/shard_map/ppermute | solution.py:373
  9.2 1.3 %collective-permute-start.4 = (bf16[2,3,8,384]{3,2,1,0:T(8,128)(2,1)}, bf16[2,3,8,384]{3,2,1,0:T(8,128)(2,1)}, u32[]{:S(2)}, u32[]{:S(2)}) collective-permute-start(bf16[2,3,8,384]{3,2,1,0:T(8,128)(2,1)} %get-tuple-element.12), channel_id=1, source_target_pairs={{8,256},{16,264},{24,272},{32,280},{40,288},{48,296},{56,304},{64,... | collective-permute-start | bytes 110600 | tf_op jit(solution)/shard_map/ppermute | solution.py:380
  10.5 8.9 %collective-permute-start.2 = (bf16[2,3,8,384]{3,2,1,0:T(8,128)(2,1)}, bf16[2,3,8,384]{3,2,1,0:T(8,128)(2,1)}, u32[]{:S(2)}, u32[]{:S(2)}) collective-permute-start(bf16[2,3,8,384]{3,2,1,0:T(8,128)(2,1)} %get-tuple-element.12), channel_id=1, source_target_pairs={{0,264},{8,272},{16,280},{24,288},{32,296},{40,304},{48,312},{56,3... | collective-permute-start | bytes 110600 | tf_op jit(solution)/shard_map/ppermute | solution.py:377
  19.4 4.7 %collective-permute-start = (bf16[2,3,8,384]{3,2,1,0:T(8,128)(2,1)}, bf16[2,3,8,384]{3,2,1,0:T(8,128)(2,1)}, u32[]{:S(2)}, u32[]{:S(2)}) collective-permute-start(bf16[2,3,8,384]{3,2,1,0:T(8,128)(2,1)} %get-tuple-element.12), channel_id=1, source_target_pairs={{0,256},{256,0},{1,257},{257,1},{2,258},{258,2},{3,259},{259,3},{4... | collective-permute-start | bytes 110600 | tf_op jit(solution)/shard_map/ppermute | solution.py:375
  24.1 3.1 %own_rows.1.partial_hbm = f32[384,384]{1,0:T(8,128)} custom-call(bf16[2,3,64,384]{3,2,1,0:T(8,128)(2,1)} %get-tuple-element.13.own_hbm, f32[7,7,384]{2,1,0:T(8,128)} %dw_k_hbm.3), custom_call_target="tpu_custom_call" | custom-call | flops 100000000 | bytes 2000000 | tf_op jit(solution)/shard_map/own_rows/pallas_call | solution.py:387
  27.2 0.0 collective-permute-done.4.edge_below_hbm
  27.2 0.0 collective-permute-done.2.edge_above_hbm
  27.2 0.0 collective-permute-done.edge_own_hbm
  27.2 0.0 collective-permute-done.3.below_hbm
  27.2 0.0 collective-permute-done.1.above_hbm
  27.2 0.0 copy-start
  27.2 0.0 copy-start.6
  27.2 0.0 copy-start.7
  27.3 7.8 %forward.1 = (f32[16,2,1152]{2,1,0:T(2,128)}, bf16[384,1024]{1,0:T(8,128)(2,1)}, bf16[384,1024]{1,0:T(8,128)(2,1)}, f32[384,128]{1,0:T(8,128)}, bf16[384,256]{1,0:T(8,128)(2,1)}, /*index=5*/bf16[384,256]{1,0:T(8,128)(2,1)}) custom-call(bf16[2,3,8,384]{3,2,1,0:T(8,128)(2,1)} %collective-permute-done.edge_own_hbm, ...), custom_call_target="tpu_custom_call" | custom-call | flops 2000000000 | bytes 8000000 | tf_op jit(solution)/shard_map/forward/pallas_call | solution.py:414
  35.1 10.1 %all-to-all-start = ((f32[16,2,1152]{2,1,0:T(2,128)}), f32[16,2,1152]{2,1,0:T(2,128)S(1)}, u32[]{:S(2)}, u32[]{:S(2)}) async-start(f32[16,2,1152]{2,1,0:T(2,128)} %get-tuple-element.15), calls=%async_computation | async-start | bytes 294912 | tf_op jit(solution)/shard_map/all_to_all | solution.py:448
  45.1 0.0 copy-done
  45.2 0.0 copy-done.6
  45.2 0.0 copy-done.7
  45.2 0.0 copy-start.2
  45.2 1.1 %copy-done.2 = bf16[384,1024]{1,0:T(8,128)(2,1)S(1)} copy-done((bf16[384,1024]{1,0:T(8,128)(2,1)S(1)}, bf16[384,1024]{1,0:T(8,128)(2,1)}, u32[]{:S(2)}) %copy-start.2) | copy-done | bytes 786456
  46.3 0.0 copy-start.8
  46.3 0.9 %copy-done.8 = bf16[384,256]{1,0:T(8,128)(2,1)S(1)} copy-done((bf16[384,256]{1,0:T(8,128)(2,1)S(1)}, bf16[384,256]{1,0:T(8,128)(2,1)}, u32[]{:S(2)}) %copy-start.8) | copy-done | bytes 196632
  47.2 0.0 copy-start.9
  47.2 0.9 %copy-done.9 = bf16[384,256]{1,0:T(8,128)(2,1)S(1)} copy-done((bf16[384,256]{1,0:T(8,128)(2,1)S(1)}, bf16[384,256]{1,0:T(8,128)(2,1)}, u32[]{:S(2)}) %copy-start.9) | copy-done | bytes 196632
  48.2 0.0 copy-start.4
  48.2 1.5 %gate_term.1.ahead = f32[384,384]{1,0:T(8,128)S(1)} custom-call(bf16[384,256]{1,0:T(8,128)(2,1)S(1)} %copy-done.8, bf16[384,256]{1,0:T(8,128)(2,1)S(1)} %copy-done.9, bf16[384,1024]{1,0:T(8,128)(2,1)S(1)} %copy-done.2, bf16[384,1024]{1,0:T(8,128)(2,1)S(1)} %copy-done, bf16[1024,256]{1,0:T(8,128)(2,1)S(1)} %copy-done.6, bf16[1024,256]{1,0:T(8,128)(2,1)S(1)} %copy-done.7), custom_call_target="tpu_custom_call" | custom-call | flops 1000000000 | bytes 4000000 | tf_op jit(solution)/shard_map/gate_term/pallas_call | solution.py:431
  49.7 0.0 copy-start.1
  49.7 0.0 copy-start.3
  49.7 0.0 copy-start.5
  49.7 7.5 %all-to-all-done.received = f32[16,2,1152]{2,1,0:T(2,128)S(1)} async-done(((f32[16,2,1152]{2,1,0:T(2,128)}), f32[16,2,1152]{2,1,0:T(2,128)S(1)}, u32[]{:S(2)}, u32[]{:S(2)}) %all-to-all-start) | async-done | bytes 147488 | tf_op jit(solution)/shard_map/all_to_all | solution.py:448
  57.3 0.1 add_up.1
  57.4 19.9 %all_to_all.10.received = f32[32,2,1152]{2,1,0:T(2,128)S(1)} all-to-all(f32[32,2,1152]{2,1,0:T(2,128)S(1)} %add_up.1), channel_id=1, replica_groups=mesh['section'=2,'z'=16,'xl'=2,'set'=8] {'section','xl','set'}, dimensions={0} | all-to-all | bytes 589824 | tf_op jit(solution)/shard_map/all_to_all | solution.py:457
  77.3 0.0 copy-done.4
  77.3 0.0 copy-done.1
  77.3 0.0 copy-done.3
  77.3 0.0 copy-done.5
  77.3 2.6 %final.1 = (f32[2]{0:T(128)}, f32[2,1024]{1,0:T(2,128)}, bf16[2,3,64,384]{3,2,1,0:T(8,128)(2,1)}) custom-call(f32[32,2,1152]{2,1,0:T(2,128)S(1)} %all_to_all.10.received, s32[1,16]{1,0:T(1,128)S(1)} %bitcast.2, bf16[384,1024]{1,0:T(8,128)(2,1)S(1)} %copy-done.1, bf16[384,1024]{1,0:T(8,128)(2,1)S(1)} %copy-done.3, f32[384,128]{1,0:T(8,128)S(1)} %copy-done.4, ...), custom_call_target="tpu_custom_call" | custom-call | tf_op jit(solution)/shard_map/final/pallas_call | solution.py:459
Async XLA Ops:
  2.6 24.6 %collective-permute-start.3 = (bf16[2,3,64,384]{3,2,1,0:T(8,128)(2,1)}, bf16[2,3,64,384]{3,2,1,0:T(8,128)(2,1)}, u32[]{:S(2)}, u32[]{:S(2)}) collective-permute-start(bf16[2,3,64,384]{3,2,1,0:T(8,128)(2,1)} %get-tuple-element.13.own_hbm), channel_id=1, source_target_pairs={{8,0},{16,8},{24,16},{32,24},{40,32},{48,40},{56,48},{64,56},{72,6... | collective-permute-start | bytes 884744 | tf_op jit(solution)/shard_map/ppermute | solution.py:374
  3.9 23.3 %collective-permute-start.1 = (bf16[2,3,64,384]{3,2,1,0:T(8,128)(2,1)}, bf16[2,3,64,384]{3,2,1,0:T(8,128)(2,1)}, u32[]{:S(2)}, u32[]{:S(2)}) collective-permute-start(bf16[2,3,64,384]{3,2,1,0:T(8,128)(2,1)} %get-tuple-element.13.own_hbm), channel_id=1, source_target_pairs={{0,8},{8,16},{16,24},{24,32},{32,40},{40,48},{48,56},{56,64},{64,7... | collective-permute-start | bytes 884744 | tf_op jit(solution)/shard_map/ppermute | solution.py:373
  9.2 18.0 %collective-permute-start.4 = (bf16[2,3,8,384]{3,2,1,0:T(8,128)(2,1)}, bf16[2,3,8,384]{3,2,1,0:T(8,128)(2,1)}, u32[]{:S(2)}, u32[]{:S(2)}) collective-permute-start(bf16[2,3,8,384]{3,2,1,0:T(8,128)(2,1)} %get-tuple-element.12), channel_id=1, source_target_pairs={{8,256},{16,264},{24,272},{32,280},{40,288},{48,296},{56,304},{64,... | collective-permute-start | bytes 110600 | tf_op jit(solution)/shard_map/ppermute | solution.py:380
  10.5 16.7 %collective-permute-start.2 = (bf16[2,3,8,384]{3,2,1,0:T(8,128)(2,1)}, bf16[2,3,8,384]{3,2,1,0:T(8,128)(2,1)}, u32[]{:S(2)}, u32[]{:S(2)}) collective-permute-start(bf16[2,3,8,384]{3,2,1,0:T(8,128)(2,1)} %get-tuple-element.12), channel_id=1, source_target_pairs={{0,264},{8,272},{16,280},{24,288},{32,296},{40,304},{48,312},{56,3... | collective-permute-start | bytes 110600 | tf_op jit(solution)/shard_map/ppermute | solution.py:377
  19.4 7.8 %collective-permute-start = (bf16[2,3,8,384]{3,2,1,0:T(8,128)(2,1)}, bf16[2,3,8,384]{3,2,1,0:T(8,128)(2,1)}, u32[]{:S(2)}, u32[]{:S(2)}) collective-permute-start(bf16[2,3,8,384]{3,2,1,0:T(8,128)(2,1)} %get-tuple-element.12), channel_id=1, source_target_pairs={{0,256},{256,0},{1,257},{257,1},{2,258},{258,2},{3,259},{259,3},{4... | collective-permute-start | bytes 110600 | tf_op jit(solution)/shard_map/ppermute | solution.py:375
  27.2 17.9 %copy-start = (bf16[384,1024]{1,0:T(8,128)(2,1)S(1)}, bf16[384,1024]{1,0:T(8,128)(2,1)}, u32[]{:S(2)}) copy-start(bf16[384,1024]{1,0:T(8,128)(2,1)} %emb_hbm.5) | copy-start | bytes 2359300
  27.2 17.9 %copy-start.6 = (bf16[1024,256]{1,0:T(8,128)(2,1)S(1)}, bf16[1024,256]{1,0:T(8,128)(2,1)}, u32[]{:S(2)}) copy-start(bf16[1024,256]{1,0:T(8,128)(2,1)} %v_hbm.3) | copy-start | bytes 1572868
  27.2 17.9 %copy-start.7 = (bf16[1024,256]{1,0:T(8,128)(2,1)S(1)}, bf16[1024,256]{1,0:T(8,128)(2,1)}, u32[]{:S(2)}) copy-start(bf16[1024,256]{1,0:T(8,128)(2,1)} %u_hbm.3) | copy-start | bytes 1572868
  35.1 22.2 %all-to-all-start = ((f32[16,2,1152]{2,1,0:T(2,128)}), f32[16,2,1152]{2,1,0:T(2,128)S(1)}, u32[]{:S(2)}, u32[]{:S(2)}) async-start(f32[16,2,1152]{2,1,0:T(2,128)} %get-tuple-element.15), calls=%async_computation | async-start | bytes 294912 | tf_op jit(solution)/shard_map/all_to_all | solution.py:448
  45.2 1.1 %copy-start.2 = (bf16[384,1024]{1,0:T(8,128)(2,1)S(1)}, bf16[384,1024]{1,0:T(8,128)(2,1)}, u32[]{:S(2)}) copy-start(bf16[384,1024]{1,0:T(8,128)(2,1)} %get-tuple-element.18.slope) | copy-start | bytes 2359300
  46.3 0.9 %copy-start.8 = (bf16[384,256]{1,0:T(8,128)(2,1)S(1)}, bf16[384,256]{1,0:T(8,128)(2,1)}, u32[]{:S(2)}) copy-start(bf16[384,256]{1,0:T(8,128)(2,1)} %get-tuple-element.16.gate_v) | copy-start | bytes 589828
  47.2 0.9 %copy-start.9 = (bf16[384,256]{1,0:T(8,128)(2,1)S(1)}, bf16[384,256]{1,0:T(8,128)(2,1)}, u32[]{:S(2)}) copy-start(bf16[384,256]{1,0:T(8,128)(2,1)} %get-tuple-element.17.gate_u) | copy-start | bytes 589828
  48.2 29.1 %copy-start.4 = (f32[384,128]{1,0:T(8,128)S(1)}, f32[384,128]{1,0:T(8,128)}, u32[]{:S(2)}) copy-start(f32[384,128]{1,0:T(8,128)} %get-tuple-element.20.weight) | copy-start | bytes 589828
  49.7 27.6 %copy-start.1 = (bf16[384,1024]{1,0:T(8,128)(2,1)S(1)}, bf16[384,1024]{1,0:T(8,128)(2,1)}, u32[]{:S(2)}) copy-start(bf16[384,1024]{1,0:T(8,128)(2,1)} %get-tuple-element.19.embedded) | copy-start | bytes 2359300
  49.7 27.6 %copy-start.3 = (bf16[384,1024]{1,0:T(8,128)(2,1)S(1)}, bf16[384,1024]{1,0:T(8,128)(2,1)}, u32[]{:S(2)}) copy-start(bf16[384,1024]{1,0:T(8,128)(2,1)} %get-tuple-element.18.slope) | copy-start | bytes 2359300
  49.7 27.6 %copy-start.5 = (s32[16]{0:T(128)S(1)}, s32[16]{0:T(128)}, u32[]{:S(2)}) copy-start(s32[16]{0:T(128)} %param.17) | copy-start | bytes 196

commit v5 on v4

--- a/solution.py
+++ b/solution.py
@@ -247,39 +247,26 @@
         c.wait()
 
 
-def slope_kernel(
-    gate_v, gate_u, slope, emb_hbm, v_hbm, u_hbm, out, emb, att_v, att_u, sems
-):
-    copies = [
-        pltpu.make_async_copy(src, dst, sems.at[i])
-        for i, (src, dst) in enumerate(((v_hbm, att_v), (u_hbm, att_u), (emb_hbm, emb)))
-    ]
-    for c in copies:
-        c.start()
-    for c in copies:
-        c.wait()
-    total = jnp.zeros((N, C), F32)
-    step = 256
-    for h in range(0, A, step):
-        cols = slice(h, h + step)
-        back = lax.dot_general(gate_v[...], att_v[cols, :], NT, preferred_element_type=F32)
-        back = back + lax.dot_general(gate_u[...], att_u[cols, :], NT, preferred_element_type=F32)
-        back = (back * slope[:, cols].astype(F32)).astype(BF)
-        total = total + lax.dot_general(back, emb[:, cols], NT, preferred_element_type=F32)
-    out[...] = total
-
-
-def sum_kernel(received, ahead, payload):
+def sum_kernel(received, payload):
     total = jnp.sum(received[...], axis=0)
     payload[...] = jnp.broadcast_to(total[None], payload.shape)
 
 
 def final_kernel(
-    received, partner, embedded, slope, weight, gate_term, emb_hbm,
-    loss_out, vector_out, grad_out, sums_ref, emb, sem,
+    received, partner, embedded_hbm, weight_hbm, gate_v_hbm, gate_u_hbm, slope_hbm, v_hbm, u_hbm,
+    emb_hbm, loss_out, vector_out, grad_out,
+    embedded, weight, gate_v, gate_u, slope, att_v, att_u, emb, sums_ref, scaled_v, scaled_u, sems,
 ):
-    fetch = pltpu.make_async_copy(emb_hbm, emb, sem)
-    fetch.start()
+    fetch = copies_between(
+        (
+            (embedded_hbm, embedded), (weight_hbm, weight), (gate_v_hbm, gate_v),
+            (gate_u_hbm, gate_u), (slope_hbm, slope), (v_hbm, att_v), (u_hbm, att_u),
+            (emb_hbm, emb),
+        ),
+        sems,
+    )
+    for c in fetch:
+        c.start()
     position = lax.axis_index("set")
     slides = sums_ref.shape[0]
     groups = slides // S
@@ -310,7 +297,9 @@
     )
     dots = jnp.sum(pooled_grad * pooled, axis=-1, keepdims=True)
     index = lax.broadcasted_iota(jnp.int32, (slides, 1), 0)
-    fetch.wait()
+    leading = []
+    for c in fetch[:4]:
+        c.wait()
     for s in range(S):
         mine = index == position * S + s
 
@@ -326,12 +315,28 @@
         aligned = jnp.sum(embedded[rows, :].astype(F32) * grad, axis=-1, keepdims=True)
         share = weight[rows, :] / total
         score = share * (aligned - dot)
-        moved = (slope[rows, :].astype(F32) * grad).astype(BF)
-        back = lax.dot_general(moved, emb[...], NT, preferred_element_type=F32)
-        share = jnp.concatenate([share] * (C // LANES), axis=1)
-        score = jnp.concatenate([score] * (C // LANES), axis=1)
-        fresh = share * back + score * gate_term[rows, :]
-        grad_out[s] = fresh.astype(BF).reshape(R, W, C)
+        leading.append((share, grad))
+        score = jnp.concatenate([score] * (AH // LANES), axis=1)
+        scaled_v[rows, :] = (score * gate_v[rows, :].astype(F32)).astype(BF)
+        scaled_u[rows, :] = (score * gate_u[rows, :].astype(F32)).astype(BF)
+    for c in fetch[4:]:
+        c.wait()
+    fresh = jnp.zeros((N, C), F32)
+    step = 512
+    for h in range(0, A, step):
+        cols = slice(h, h + step)
+        back = lax.dot_general(scaled_v[...], att_v[cols, :], NT, preferred_element_type=F32)
+        back = back + lax.dot_general(scaled_u[...], att_u[cols, :], NT, preferred_element_type=F32)
+        lead = jnp.concatenate(
+            [
+                jnp.concatenate([share] * (step // LANES), axis=1) * grad[:, cols]
+                for share, grad in leading
+            ],
+            axis=0,
+        )
+        moved = ((lead + back) * slope[:, cols].astype(F32)).astype(BF)
+        fresh = fresh + lax.dot_general(moved, emb[:, cols], NT, preferred_element_type=F32)
+    grad_out[...] = fresh.astype(BF).reshape(S, R, W, C)
 
 
 HBM = pl.BlockSpec(memory_space=pltpu.HBM)
@@ -428,34 +433,19 @@
         cost_estimate=pl.CostEstimate(flops=2 * 10**9, bytes_accessed=8 * 10**6, transcendentals=10**6),
         name="forward",
     )(*operands)
-    gate_term = pl.pallas_call(
-        slope_kernel,
-        out_shape=jax.ShapeDtypeStruct((N, C), F32),
-        in_specs=[VM] * 3 + [HBM] * 3,
-        out_specs=VM,
-        scratch_shapes=[
-            pltpu.VMEM((C, A), BF),
-            pltpu.VMEM((A, AH), BF),
-            pltpu.VMEM((A, AH), BF),
-            pltpu.SemaphoreType.DMA((3,)),
-        ],
-        compiler_params=params(24),
-        cost_estimate=pl.CostEstimate(flops=10**9, bytes_accessed=4 * 10**6, transcendentals=0),
-        name="gate_term",
-    )(gate_v, gate_u, slope, w_embed, attn_v, attn_u)
-
     plane = ("section", "xl", "set")
     received = lax.all_to_all(payload, "z", 0, 0, tiled=True)
     payload = pl.pallas_call(
         sum_kernel,
         out_shape=jax.ShapeDtypeStruct((lax.axis_size(plane), S, PAY), F32),
-        in_specs=[VM, HBM],
+        in_specs=[VM],
         out_specs=VM,
         compiler_params=params(24),
         name="add_up",
-    )(received, gate_term)
+    )(received)
     received = lax.all_to_all(payload, plane, 0, 0, tiled=True)
     slides = partner.shape[0]
+    kept = (embedded, weight, gate_v, gate_u, slope, attn_v, attn_u, w_embed)
     return pl.pallas_call(
         final_kernel,
         out_shape=(
@@ -463,16 +453,18 @@
             jax.ShapeDtypeStruct((S, A), F32),
             jax.ShapeDtypeStruct((S, R, W, C), BF),
         ),
-        in_specs=[VM] * 6 + [HBM],
+        in_specs=[VM, VM] + [HBM] * len(kept),
         out_specs=(SM, VM, VM),
-        scratch_shapes=[
+        scratch_shapes=[pltpu.VMEM(x.shape, x.dtype) for x in kept]
+        + [
             pltpu.VMEM((slides, PAY), F32),
-            pltpu.VMEM((C, A), BF),
-            pltpu.SemaphoreType.DMA(()),
+            pltpu.VMEM((N, AH), BF),
+            pltpu.VMEM((N, AH), BF),
+            pltpu.SemaphoreType.DMA((len(kept),)),
         ],
-        compiler_params=params(24),
+        compiler_params=params(53),
         name="final",
-    )(received, partner.reshape(1, slides), embedded, slope, weight, gate_term, w_embed)
+    )(received, partner.reshape(1, slides), *kept)
 
 
 def solution(mesh):

time: 80.4 us -> 82.7 us (1.029)
  blocking collectives: 19.9 us -> 42.4 us
  starting transfers between devices: 31.6 us -> 21.5 us
  waiting for transfers between devices: 7.56 us -> 0.01 us
  local copies, waits for them, and re-layouts: 3.02 us -> 0.02 us
    all_to_all x0 -> x1, blocking collectives: none -> 22.3 us  [shards(): received = lax.all_to_all(payload, 'z', 0, 0, tiled=True)]
    all_to_all x1 -> x0, starting transfers between devices: 10.1 us -> none  [shards(): received = lax.all_to_all(payload, 'z', 0, 0, tiled=True)]
    all_to_all x1 -> x0, waiting for transfers between devices: 7.54 us -> none  [shards(): received = lax.all_to_all(payload, 'z', 0, 0, tiled=True)]
    unnamed x20 -> x8, local copies, waits for them, and re-layouts: 3.02 us -> 0.02 us
    pallas_call x1, Pallas kernels: 2.57 us -> 4.82 us  [shards(): pl.pallas_call(final_kernel, out_shape=(jax.ShapeDtypeStruct((S,), F32),...]
    pallas_call x1 -> x0, Pallas kernels: 1.51 us -> none  [shards(): pl.pallas_call(slope_kernel, out_shape=jax.ShapeDtypeStruct((N, C), F32),...]
  transfers between devices with their start and end apart: 6 -> 5, of which waited for: 1 -> 0; matrix products, arithmetic and copies ran while one was open for 0% -> 0% of each run, Pallas kernels for 6% -> 4%
where the time goes in v5:
time: 82.7 us; the launch traced here: 82.3 us
  blocking collectives  42.4 us (51%)
  starting transfers between devices  21.5 us (26%)
  Pallas kernels  17.6 us (21%)
    all_to_all x1, blocking collectives, shards(): received = lax.all_to_all(payload, 'z', 0, 0, tiled=True)  22.3 us
    all_to_all x1, blocking collectives, shards(): received = lax.all_to_all(payload, plane, 0, 0, tiled=True)  20.1 us
    ppermute x1, starting transfers between devices, shards(): lax.ppermute(edge, every, [(c * count + i, (1 - c) * count + i + 1) for c...  8.9 us
    pallas_call x1, Pallas kernels, shards(): pl.pallas_call(forward_kernel, out_shape=forward_shapes, in_specs=[HBM] *...  7.71 us
    ppermute x1, starting transfers between devices, shards(): above = lax.ppermute(masked, tile, upward)  5.31 us
    pallas_call x1, Pallas kernels, shards(): pl.pallas_call(final_kernel, out_shape=(jax.ShapeDtypeStruct((S,), F32),...  4.82 us
    ppermute x1, starting transfers between devices, shards(): edge_own = lax.ppermute(edge, 'section', [(0, 1), (1, 0)])  4.72 us
    pallas_call x1, Pallas kernels, shards(): pl.pallas_call(own_kernel, out_shape=partial, in_specs=[HBM] * len(source...  3.05 us
  transfers between devices with their start and end apart: 5, of which 0 were waited for; matrix products, arithmetic and copies ran while one was open for 0% of the time, Pallas kernels for 4%

profile of v5, /device:TPU:1, one launch (start us, length us, event | category | flops | bytes accessed | tf_op | source)
XLA Modules:
  0.0 82.3 jit_solution(17313258741835864171)
XLA Ops:
  0.6 1.9 %mask.1 = (bf16[2,3,64,384]{3,2,1,0:T(8,128)(2,1)}, bf16[2,3,8,384]{3,2,1,0:T(8,128)(2,1)}, f32[384,128]{1,0:T(8,128)}) custom-call(bf16[2,3,64,384]{3,2,1,0:T(8,128)(2,1)} %features_hbm.1, s32[3,2,64]{2,1,0:T(2,128)} %bitcast.3), custom_call_target="tpu_custom_call" | custom-call | tf_op jit(solution)/shard_map/mask/pallas_call | solution.py:363
  2.6 1.3 %collective-permute-start.3 = (bf16[2,3,64,384]{3,2,1,0:T(8,128)(2,1)}, bf16[2,3,64,384]{3,2,1,0:T(8,128)(2,1)}, u32[]{:S(2)}, u32[]{:S(2)}) collective-permute-start(bf16[2,3,64,384]{3,2,1,0:T(8,128)(2,1)} %get-tuple-element.13.own_hbm), channel_id=1, source_target_pairs={{8,0},{16,8},{24,16},{32,24},{40,32},{48,40},{56,48},{64,56},{72,6... | collective-permute-start | bytes 884744 | tf_op jit(solution)/shard_map/ppermute | solution.py:379
  3.9 5.3 %collective-permute-start.1 = (bf16[2,3,64,384]{3,2,1,0:T(8,128)(2,1)}, bf16[2,3,64,384]{3,2,1,0:T(8,128)(2,1)}, u32[]{:S(2)}, u32[]{:S(2)}) collective-permute-start(bf16[2,3,64,384]{3,2,1,0:T(8,128)(2,1)} %get-tuple-element.13.own_hbm), channel_id=1, source_target_pairs={{0,8},{8,16},{16,24},{24,32},{32,40},{40,48},{48,56},{56,64},{64,7... | collective-permute-start | bytes 884744 | tf_op jit(solution)/shard_map/ppermute | solution.py:378
  9.2 1.3 %collective-permute-start.4 = (bf16[2,3,8,384]{3,2,1,0:T(8,128)(2,1)}, bf16[2,3,8,384]{3,2,1,0:T(8,128)(2,1)}, u32[]{:S(2)}, u32[]{:S(2)}) collective-permute-start(bf16[2,3,8,384]{3,2,1,0:T(8,128)(2,1)} %get-tuple-element.12), channel_id=1, source_target_pairs={{8,256},{16,264},{24,272},{32,280},{40,288},{48,296},{56,304},{64,... | collective-permute-start | bytes 110600 | tf_op jit(solution)/shard_map/ppermute | solution.py:385
  10.5 8.9 %collective-permute-start.2 = (bf16[2,3,8,384]{3,2,1,0:T(8,128)(2,1)}, bf16[2,3,8,384]{3,2,1,0:T(8,128)(2,1)}, u32[]{:S(2)}, u32[]{:S(2)}) collective-permute-start(bf16[2,3,8,384]{3,2,1,0:T(8,128)(2,1)} %get-tuple-element.12), channel_id=1, source_target_pairs={{0,264},{8,272},{16,280},{24,288},{32,296},{40,304},{48,312},{56,3... | collective-permute-start | bytes 110600 | tf_op jit(solution)/shard_map/ppermute | solution.py:382
  19.4 4.7 %collective-permute-start = (bf16[2,3,8,384]{3,2,1,0:T(8,128)(2,1)}, bf16[2,3,8,384]{3,2,1,0:T(8,128)(2,1)}, u32[]{:S(2)}, u32[]{:S(2)}) collective-permute-start(bf16[2,3,8,384]{3,2,1,0:T(8,128)(2,1)} %get-tuple-element.12), channel_id=1, source_target_pairs={{0,256},{256,0},{1,257},{257,1},{2,258},{258,2},{3,259},{259,3},{4... | collective-permute-start | bytes 110600 | tf_op jit(solution)/shard_map/ppermute | solution.py:380
  24.1 3.0 %own_rows.1.partial_hbm = f32[384,384]{1,0:T(8,128)} custom-call(bf16[2,3,64,384]{3,2,1,0:T(8,128)(2,1)} %get-tuple-element.13.own_hbm, f32[7,7,384]{2,1,0:T(8,128)} %dw_k_hbm.3), custom_call_target="tpu_custom_call" | custom-call | flops 100000000 | bytes 2000000 | tf_op jit(solution)/shard_map/own_rows/pallas_call | solution.py:392
  27.2 0.0 collective-permute-done.4.edge_below_hbm
  27.2 0.0 collective-permute-done.2.edge_above_hbm
  27.2 0.0 collective-permute-done.edge_own_hbm
  27.2 0.0 collective-permute-done.3.below_hbm
  27.2 0.0 collective-permute-done.1.above_hbm
  27.2 7.7 %forward.1 = (f32[16,2,1152]{2,1,0:T(2,128)}, bf16[384,1024]{1,0:T(8,128)(2,1)}, bf16[384,1024]{1,0:T(8,128)(2,1)}, f32[384,128]{1,0:T(8,128)}, bf16[384,256]{1,0:T(8,128)(2,1)}, /*index=5*/bf16[384,256]{1,0:T(8,128)(2,1)}) custom-call(bf16[2,3,8,384]{3,2,1,0:T(8,128)(2,1)} %collective-permute-done.edge_own_hbm, ...), custom_call_target="tpu_custom_call" | custom-call | flops 2000000000 | bytes 8000000 | tf_op jit(solution)/shard_map/forward/pallas_call | solution.py:419
  34.9 0.0 copy-start
  34.9 0.0 copy-start.1
  34.9 0.0 copy-start.2
  35.0 0.0 copy-start.3
  35.0 22.3 %all_to_all.10.received = f32[16,2,1152]{2,1,0:T(2,128)S(1)} all-to-all(f32[16,2,1152]{2,1,0:T(2,128)} %get-tuple-element.15), channel_id=1, replica_groups=mesh['section'=2,'z'=16,'xl'=2,'set'=8] {'z'}, dimensions={0} | all-to-all | bytes 294912 | tf_op jit(solution)/shard_map/all_to_all | solution.py:437
  57.3 0.1 add_up.1
  57.4 20.1 %all_to_all.11.received = f32[32,2,1152]{2,1,0:T(2,128)S(1)} all-to-all(f32[32,2,1152]{2,1,0:T(2,128)S(1)} %add_up.1), channel_id=1, replica_groups=mesh['section'=2,'z'=16,'xl'=2,'set'=8] {'section','xl','set'}, dimensions={0} | all-to-all | bytes 589824 | tf_op jit(solution)/shard_map/all_to_all | solution.py:446
  77.4 0.0 copy-done
  77.5 0.0 copy-done.1
  77.5 0.0 copy-done.2
  77.5 0.0 copy-done.3
  77.5 4.8 %final.1 = (f32[2]{0:T(128)}, f32[2,1024]{1,0:T(2,128)}, bf16[2,3,64,384]{3,2,1,0:T(8,128)(2,1)}) custom-call(f32[32,2,1152]{2,1,0:T(2,128)S(1)} %all_to_all.11.received, s32[1,16]{1,0:T(1,128)S(1)} %bitcast.2, bf16[384,1024]{1,0:T(8,128)(2,1)} %get-tuple-element.16.embedded_hbm, f32[384,128]{1,0:T(8,128)S(1)} %copy-done, bf16[384,256]{1,0:T(8,128)(2,1)S(1)} %copy-done.1, ...), custom_call_target="tpu_custom_call" | custom-call | tf_op jit(solution)/shard_map/final/pallas_call | solution.py:449
Async XLA Ops:
  2.6 24.6 %collective-permute-start.3 = (bf16[2,3,64,384]{3,2,1,0:T(8,128)(2,1)}, bf16[2,3,64,384]{3,2,1,0:T(8,128)(2,1)}, u32[]{:S(2)}, u32[]{:S(2)}) collective-permute-start(bf16[2,3,64,384]{3,2,1,0:T(8,128)(2,1)} %get-tuple-element.13.own_hbm), channel_id=1, source_target_pairs={{8,0},{16,8},{24,16},{32,24},{40,32},{48,40},{56,48},{64,56},{72,6... | collective-permute-start | bytes 884744 | tf_op jit(solution)/shard_map/ppermute | solution.py:379
  3.9 23.3 %collective-permute-start.1 = (bf16[2,3,64,384]{3,2,1,0:T(8,128)(2,1)}, bf16[2,3,64,384]{3,2,1,0:T(8,128)(2,1)}, u32[]{:S(2)}, u32[]{:S(2)}) collective-permute-start(bf16[2,3,64,384]{3,2,1,0:T(8,128)(2,1)} %get-tuple-element.13.own_hbm), channel_id=1, source_target_pairs={{0,8},{8,16},{16,24},{24,32},{32,40},{40,48},{48,56},{56,64},{64,7... | collective-permute-start | bytes 884744 | tf_op jit(solution)/shard_map/ppermute | solution.py:378
  9.2 18.0 %collective-permute-start.4 = (bf16[2,3,8,384]{3,2,1,0:T(8,128)(2,1)}, bf16[2,3,8,384]{3,2,1,0:T(8,128)(2,1)}, u32[]{:S(2)}, u32[]{:S(2)}) collective-permute-start(bf16[2,3,8,384]{3,2,1,0:T(8,128)(2,1)} %get-tuple-element.12), channel_id=1, source_target_pairs={{8,256},{16,264},{24,272},{32,280},{40,288},{48,296},{56,304},{64,... | collective-permute-start | bytes 110600 | tf_op jit(solution)/shard_map/ppermute | solution.py:385
  10.5 16.7 %collective-permute-start.2 = (bf16[2,3,8,384]{3,2,1,0:T(8,128)(2,1)}, bf16[2,3,8,384]{3,2,1,0:T(8,128)(2,1)}, u32[]{:S(2)}, u32[]{:S(2)}) collective-permute-start(bf16[2,3,8,384]{3,2,1,0:T(8,128)(2,1)} %get-tuple-element.12), channel_id=1, source_target_pairs={{0,264},{8,272},{16,280},{24,288},{32,296},{40,304},{48,312},{56,3... | collective-permute-start | bytes 110600 | tf_op jit(solution)/shard_map/ppermute | solution.py:382
  19.4 7.8 %collective-permute-start = (bf16[2,3,8,384]{3,2,1,0:T(8,128)(2,1)}, bf16[2,3,8,384]{3,2,1,0:T(8,128)(2,1)}, u32[]{:S(2)}, u32[]{:S(2)}) collective-permute-start(bf16[2,3,8,384]{3,2,1,0:T(8,128)(2,1)} %get-tuple-element.12), channel_id=1, source_target_pairs={{0,256},{256,0},{1,257},{257,1},{2,258},{258,2},{3,259},{259,3},{4... | collective-permute-start | bytes 110600 | tf_op jit(solution)/shard_map/ppermute | solution.py:380
  34.9 42.5 %copy-start = (f32[384,128]{1,0:T(8,128)S(1)}, f32[384,128]{1,0:T(8,128)}, u32[]{:S(2)}) copy-start(f32[384,128]{1,0:T(8,128)} %get-tuple-element.17.weight_hbm) | copy-start | bytes 589828
  34.9 42.5 %copy-start.1 = (bf16[384,256]{1,0:T(8,128)(2,1)S(1)}, bf16[384,256]{1,0:T(8,128)(2,1)}, u32[]{:S(2)}) copy-start(bf16[384,256]{1,0:T(8,128)(2,1)} %get-tuple-element.18.gate_v_hbm) | copy-start | bytes 589828
  34.9 42.5 %copy-start.2 = (bf16[384,256]{1,0:T(8,128)(2,1)S(1)}, bf16[384,256]{1,0:T(8,128)(2,1)}, u32[]{:S(2)}) copy-start(bf16[384,256]{1,0:T(8,128)(2,1)} %get-tuple-element.19.gate_u_hbm) | copy-start | bytes 589828
  35.0 42.5 %copy-start.3 = (s32[16]{0:T(128)S(1)}, s32[16]{0:T(128)}, u32[]{:S(2)}) copy-start(s32[16]{0:T(128)} %param.17) | copy-start | bytes 196

commit v6 on v4

--- a/solution.py
+++ b/solution.py
@@ -127,19 +127,19 @@
 
 
 def forward_kernel(
-    edge_own_hbm, above_hbm, edge_above_hbm, below_hbm, edge_below_hbm, dw_k_hbm, partial_hbm, own_hbm,
+    edge_own_hbm, near_hbm, edge_near_hbm, far_hbm, edge_far_hbm, dw_k_hbm, partial_hbm, own_hbm,
     flags_hbm, dw_b_hbm, ln_g_hbm, ln_b_hbm, scale_hbm, e_bias_hbm, a_w_hbm,
     up_hbm, down_hbm, emb_hbm, v_hbm, u_hbm,
     payload_hbm, embedded_hbm, slope_hbm, weight_hbm, gate_v_hbm, gate_u_hbm,
-    edge_own, above, edge_above, below, edge_below, dw_k, partial, own,
+    edge_own, near, edge_near, far, edge_far, dw_k, partial, own,
     flags, dw_b, ln_g, ln_b, scale, e_bias, a_w, up, down, emb, att_v, att_u,
     payload, embedded_out, slope_out, weight_out, gate_v_out, gate_u_out,
     grid_ref, acc_ref, conv_ref, sums_ref, sems,
 ):
     blocks = copies_between(
         (
-            (above_hbm, above), (edge_above_hbm, edge_above), (below_hbm, below),
-            (edge_below_hbm, edge_below), (edge_own_hbm, edge_own), (dw_k_hbm, dw_k),
+            (near_hbm, near), (edge_near_hbm, edge_near), (far_hbm, far),
+            (edge_far_hbm, edge_far), (edge_own_hbm, edge_own), (dw_k_hbm, dw_k),
             (partial_hbm, partial),
         ),
         sems,
@@ -180,9 +180,10 @@
         c.wait()
     for c in small + copies:
         c.start()
-    fill(grid_ref, 0, above, edge_above)
+    odd = lax.axis_index("xl") == 1
+    fill(grid_ref, jnp.where(odd, 2 * R, 0), far, edge_far)
     fill(grid_ref, R, None, edge_own)
-    fill(grid_ref, 2 * R, below, edge_below)
+    fill(grid_ref, jnp.where(odd, 0, 2 * R), near, edge_near)
     convolve(
         grid_ref, acc_ref, conv_ref, dw_k, (0, 1, 2, 6, 7, 8), tuple(range(3 * R)), partial
     )
@@ -368,18 +369,18 @@
     )(features, tissue.transpose(1, 0, 2))
     tile = ("z", "xl")
     count = lax.axis_size(tile)
-    upward = [(i, i + 1) for i in range(count - 1)]
-    downward = [(i + 1, i) for i in range(count - 1)]
-    above = lax.ppermute(masked, tile, upward)
-    below = lax.ppermute(masked, tile, downward)
+    nearby = [(i, i ^ 1) for i in range(count)]
+    away = [(i, i + 1 if i % 2 else i - 1) for i in range(1, count - 1)]
+    every = ("section",) + tile
+
+    def crossed(moves):
+        return [(c * count + i, (1 - c) * count + j) for c in range(2) for i, j in moves]
+
+    far = lax.ppermute(masked, tile, away)
+    near = lax.ppermute(masked, tile, nearby)
     edge_own = lax.ppermute(edge, "section", [(0, 1), (1, 0)])
-    every = ("section",) + tile
-    edge_above = lax.ppermute(
-        edge, every, [(c * count + i, (1 - c) * count + i + 1) for c in range(2) for i in range(count - 1)]
-    )
-    edge_below = lax.ppermute(
-        edge, every, [(c * count + i + 1, (1 - c) * count + i) for c in range(2) for i in range(count - 1)]
-    )
+    edge_near = lax.ppermute(edge, every, crossed(nearby))
+    edge_far = lax.ppermute(edge, every, crossed(away))
     depth = lax.axis_size("z")
 
     sources = (masked, dw_kernel)
@@ -400,7 +401,7 @@
         name="own_rows",
     )(*sources)
     operands = (
-        edge_own, above, edge_above, below, edge_below, dw_kernel, partial, masked, flags, dw_bias, ln_gain,
+        edge_own, near, edge_near, far, edge_far, dw_kernel, partial, masked, flags, dw_bias, ln_gain,
         ln_bias, layer_scale, embed_bias, attn_w, w_up, narrowing_projection_kernel, w_embed, attn_v, attn_u,
     )
     forward_shapes = (

time: 80.4 us -> 82.6 us (1.027)
  starting transfers between devices: 31.6 us -> 33.8 us
    all_to_all x1, starting transfers between devices: 10.1 us -> 16.2 us  [shards(): received = lax.all_to_all(payload, 'z', 0, 0, tiled=True)]
    ppermute x1, starting transfers between devices: 4.71 us -> 1.92 us  [shards(): edge_own = lax.ppermute(edge, 'section', [(0, 1), (1, 0)])]
    ppermute x4, starting transfers between devices: 16.8 us -> 15.6 us  [the longest x1 6.89 us: shards(): edge_near = lax.ppermute(edge, every, crossed(nearby))]
where the time goes in v6:
time: 82.6 us; the launch traced here: 82.1 us
  starting transfers between devices  33.8 us (41%)
  blocking collectives  19.8 us (24%)
  Pallas kernels  17 us (21%)
  waiting for transfers between devices  7.72 us (9%)
  local copies, waits for them, and re-layouts  3.02 us (4%)
  between operations  0.83 us (1%)
    all_to_all x1, blocking collectives, shards(): received = lax.all_to_all(payload, plane, 0, 0, tiled=True)  19.8 us
    all_to_all x1, starting transfers between devices, shards(): received = lax.all_to_all(payload, 'z', 0, 0, tiled=True)  16.2 us
    pallas_call x1, Pallas kernels, shards(): pl.pallas_call(forward_kernel, out_shape=forward_shapes, in_specs=[HBM] *...  7.83 us
    all_to_all x1, waiting for transfers between devices, shards(): received = lax.all_to_all(payload, 'z', 0, 0, tiled=True)  7.71 us
    ppermute x1, starting transfers between devices, shards(): edge_near = lax.ppermute(edge, every, crossed(nearby))  6.89 us
    ppermute x1, starting transfers between devices, shards(): near = lax.ppermute(masked, tile, nearby)  6.09 us
    pallas_call x1, Pallas kernels, shards(): pl.pallas_call(own_kernel, out_shape=partial, in_specs=[HBM] * len(source...  3.06 us
    unnamed x20, local copies, waits for them, and re-layouts  3.02 us
  transfers between devices with their start and end apart: 6, of which 1 were waited for; matrix products, arithmetic and copies ran while one was open for 0% of the time, Pallas kernels for 6%

profile of v6, /device:TPU:1, one launch (start us, length us, event | category | flops | bytes accessed | tf_op | source)
XLA Modules:
  0.0 82.1 jit_solution(9069502619305560050)
XLA Ops:
  0.6 1.9 %mask.1 = (bf16[2,3,64,384]{3,2,1,0:T(8,128)(2,1)}, bf16[2,3,8,384]{3,2,1,0:T(8,128)(2,1)}, f32[384,128]{1,0:T(8,128)}) custom-call(bf16[2,3,64,384]{3,2,1,0:T(8,128)(2,1)} %features_hbm.1, s32[3,2,64]{2,1,0:T(2,128)} %bitcast.3), custom_call_target="tpu_custom_call" | custom-call | tf_op jit(solution)/shard_map/mask/pallas_call | solution.py:359
  2.6 1.4 %collective-permute-start.3 = (bf16[2,3,64,384]{3,2,1,0:T(8,128)(2,1)}, bf16[2,3,64,384]{3,2,1,0:T(8,128)(2,1)}, u32[]{:S(2)}, u32[]{:S(2)}) collective-permute-start(bf16[2,3,64,384]{3,2,1,0:T(8,128)(2,1)} %get-tuple-element.13.own_hbm), channel_id=1, source_target_pairs={{8,16},{16,8},{24,32},{32,24},{40,48},{48,40},{56,64},{64,56},{72,... | collective-permute-start | bytes 884744 | tf_op jit(solution)/shard_map/ppermute | solution.py:379
  4.0 6.1 %collective-permute-start.1 = (bf16[2,3,64,384]{3,2,1,0:T(8,128)(2,1)}, bf16[2,3,64,384]{3,2,1,0:T(8,128)(2,1)}, u32[]{:S(2)}, u32[]{:S(2)}) collective-permute-start(bf16[2,3,64,384]{3,2,1,0:T(8,128)(2,1)} %get-tuple-element.13.own_hbm), channel_id=1, source_target_pairs={{0,8},{8,0},{16,24},{24,16},{32,40},{40,32},{48,56},{56,48},{64,72... | collective-permute-start | bytes 884744 | tf_op jit(solution)/shard_map/ppermute | solution.py:380
  10.1 1.3 %collective-permute-start.4 = (bf16[2,3,8,384]{3,2,1,0:T(8,128)(2,1)}, bf16[2,3,8,384]{3,2,1,0:T(8,128)(2,1)}, u32[]{:S(2)}, u32[]{:S(2)}) collective-permute-start(bf16[2,3,8,384]{3,2,1,0:T(8,128)(2,1)} %get-tuple-element.12), channel_id=1, source_target_pairs={{8,272},{16,264},{24,288},{32,280},{40,304},{48,296},{56,320},{64,... | collective-permute-start | bytes 110600 | tf_op jit(solution)/shard_map/ppermute | solution.py:383
  11.3 6.9 %collective-permute-start.2 = (bf16[2,3,8,384]{3,2,1,0:T(8,128)(2,1)}, bf16[2,3,8,384]{3,2,1,0:T(8,128)(2,1)}, u32[]{:S(2)}, u32[]{:S(2)}) collective-permute-start(bf16[2,3,8,384]{3,2,1,0:T(8,128)(2,1)} %get-tuple-element.12), channel_id=1, source_target_pairs={{0,264},{8,256},{16,280},{24,272},{32,296},{40,288},{48,312},{56,3... | collective-permute-start | bytes 110600 | tf_op jit(solution)/shard_map/ppermute | solution.py:382
  18.2 1.9 %collective-permute-start = (bf16[2,3,8,384]{3,2,1,0:T(8,128)(2,1)}, bf16[2,3,8,384]{3,2,1,0:T(8,128)(2,1)}, u32[]{:S(2)}, u32[]{:S(2)}) collective-permute-start(bf16[2,3,8,384]{3,2,1,0:T(8,128)(2,1)} %get-tuple-element.12), channel_id=1, source_target_pairs={{0,256},{256,0},{1,257},{257,1},{2,258},{258,2},{3,259},{259,3},{4... | collective-permute-start | bytes 110600 | tf_op jit(solution)/shard_map/ppermute | solution.py:381
  20.2 3.1 %own_rows.1.partial_hbm = f32[384,384]{1,0:T(8,128)} custom-call(bf16[2,3,64,384]{3,2,1,0:T(8,128)(2,1)} %get-tuple-element.13.own_hbm, f32[7,7,384]{2,1,0:T(8,128)} %dw_k_hbm.3), custom_call_target="tpu_custom_call" | custom-call | flops 100000000 | bytes 2000000 | tf_op jit(solution)/shard_map/own_rows/pallas_call | solution.py:388
  23.2 0.0 collective-permute-done.4.edge_far_hbm
  23.2 0.0 collective-permute-done.2.edge_near_hbm
  23.2 0.0 collective-permute-done.edge_own_hbm
  23.3 0.0 collective-permute-done.3.far_hbm
  23.3 0.0 collective-permute-done.1.near_hbm
  23.3 0.0 copy-start
  23.3 0.0 copy-start.6
  23.3 0.0 copy-start.7
  23.3 7.8 %forward.1 = (f32[16,2,1152]{2,1,0:T(2,128)}, bf16[384,1024]{1,0:T(8,128)(2,1)}, bf16[384,1024]{1,0:T(8,128)(2,1)}, f32[384,128]{1,0:T(8,128)}, bf16[384,256]{1,0:T(8,128)(2,1)}, /*index=5*/bf16[384,256]{1,0:T(8,128)(2,1)}) custom-call(bf16[2,3,8,384]{3,2,1,0:T(8,128)(2,1)} %collective-permute-done.edge_own_hbm, ...), custom_call_target="tpu_custom_call" | custom-call | flops 2000000000 | bytes 8000000 | tf_op jit(solution)/shard_map/forward/pallas_call | solution.py:415
  31.2 16.2 %all-to-all-start = ((f32[16,2,1152]{2,1,0:T(2,128)}), f32[16,2,1152]{2,1,0:T(2,128)S(1)}, u32[]{:S(2)}, u32[]{:S(2)}) async-start(f32[16,2,1152]{2,1,0:T(2,128)} %get-tuple-element.15), calls=%async_computation | async-start | bytes 294912 | tf_op jit(solution)/shard_map/all_to_all | solution.py:449
  47.4 0.0 copy-done
  47.4 0.0 copy-done.6
  47.4 0.0 copy-done.7
  47.4 0.0 copy-start.2
  47.4 1.1 %copy-done.2 = bf16[384,1024]{1,0:T(8,128)(2,1)S(1)} copy-done((bf16[384,1024]{1,0:T(8,128)(2,1)S(1)}, bf16[384,1024]{1,0:T(8,128)(2,1)}, u32[]{:S(2)}) %copy-start.2) | copy-done | bytes 786456
  48.5 0.0 copy-start.8
  48.5 0.9 %copy-done.8 = bf16[384,256]{1,0:T(8,128)(2,1)S(1)} copy-done((bf16[384,256]{1,0:T(8,128)(2,1)S(1)}, bf16[384,256]{1,0:T(8,128)(2,1)}, u32[]{:S(2)}) %copy-start.8) | copy-done | bytes 196632
  49.5 0.0 copy-start.9
  49.5 0.9 %copy-done.9 = bf16[384,256]{1,0:T(8,128)(2,1)S(1)} copy-done((bf16[384,256]{1,0:T(8,128)(2,1)S(1)}, bf16[384,256]{1,0:T(8,128)(2,1)}, u32[]{:S(2)}) %copy-start.9) | copy-done | bytes 196632
  50.4 0.0 copy-start.4
  50.4 1.5 %gate_term.1.ahead = f32[384,384]{1,0:T(8,128)S(1)} custom-call(bf16[384,256]{1,0:T(8,128)(2,1)S(1)} %copy-done.8, bf16[384,256]{1,0:T(8,128)(2,1)S(1)} %copy-done.9, bf16[384,1024]{1,0:T(8,128)(2,1)S(1)} %copy-done.2, bf16[384,1024]{1,0:T(8,128)(2,1)S(1)} %copy-done, bf16[1024,256]{1,0:T(8,128)(2,1)S(1)} %copy-done.6, bf16[1024,256]{1,0:T(8,128)(2,1)S(1)} %copy-done.7), custom_call_target="tpu_custom_call" | custom-call | flops 1000000000 | bytes 4000000 | tf_op jit(solution)/shard_map/gate_term/pallas_call | solution.py:432
  51.9 0.0 copy-start.1
  51.9 0.0 copy-start.3
  51.9 0.0 copy-start.5
  51.9 7.7 %all-to-all-done.received = f32[16,2,1152]{2,1,0:T(2,128)S(1)} async-done(((f32[16,2,1152]{2,1,0:T(2,128)}), f32[16,2,1152]{2,1,0:T(2,128)S(1)}, u32[]{:S(2)}, u32[]{:S(2)}) %all-to-all-start) | async-done | bytes 147488 | tf_op jit(solution)/shard_map/all_to_all | solution.py:449
  59.7 0.1 add_up.1
  59.8 19.8 %all_to_all.10.received = f32[32,2,1152]{2,1,0:T(2,128)S(1)} all-to-all(f32[32,2,1152]{2,1,0:T(2,128)S(1)} %add_up.1), channel_id=1, replica_groups=mesh['section'=2,'z'=16,'xl'=2,'set'=8] {'section','xl','set'}, dimensions={0} | all-to-all | bytes 589824 | tf_op jit(solution)/shard_map/all_to_all | solution.py:458
  79.5 0.0 copy-done.4
  79.5 0.0 copy-done.1
  79.5 0.0 copy-done.3
  79.5 0.0 copy-done.5
  79.5 2.6 %final.1 = (f32[2]{0:T(128)}, f32[2,1024]{1,0:T(2,128)}, bf16[2,3,64,384]{3,2,1,0:T(8,128)(2,1)}) custom-call(f32[32,2,1152]{2,1,0:T(2,128)S(1)} %all_to_all.10.received, s32[1,16]{1,0:T(1,128)S(1)} %bitcast.2, bf16[384,1024]{1,0:T(8,128)(2,1)S(1)} %copy-done.1, bf16[384,1024]{1,0:T(8,128)(2,1)S(1)} %copy-done.3, f32[384,128]{1,0:T(8,128)S(1)} %copy-done.4, ...), custom_call_target="tpu_custom_call" | custom-call | tf_op jit(solution)/shard_map/final/pallas_call | solution.py:460
Async XLA Ops:
  2.6 20.7 %collective-permute-start.3 = (bf16[2,3,64,384]{3,2,1,0:T(8,128)(2,1)}, bf16[2,3,64,384]{3,2,1,0:T(8,128)(2,1)}, u32[]{:S(2)}, u32[]{:S(2)}) collective-permute-start(bf16[2,3,64,384]{3,2,1,0:T(8,128)(2,1)} %get-tuple-element.13.own_hbm), channel_id=1, source_target_pairs={{8,16},{16,8},{24,32},{32,24},{40,48},{48,40},{56,64},{64,56},{72,... | collective-permute-start | bytes 884744 | tf_op jit(solution)/shard_map/ppermute | solution.py:379
  4.0 19.3 %collective-permute-start.1 = (bf16[2,3,64,384]{3,2,1,0:T(8,128)(2,1)}, bf16[2,3,64,384]{3,2,1,0:T(8,128)(2,1)}, u32[]{:S(2)}, u32[]{:S(2)}) collective-permute-start(bf16[2,3,64,384]{3,2,1,0:T(8,128)(2,1)} %get-tuple-element.13.own_hbm), channel_id=1, source_target_pairs={{0,8},{8,0},{16,24},{24,16},{32,40},{40,32},{48,56},{56,48},{64,72... | collective-permute-start | bytes 884744 | tf_op jit(solution)/shard_map/ppermute | solution.py:380
  10.1 13.2 %collective-permute-start.4 = (bf16[2,3,8,384]{3,2,1,0:T(8,128)(2,1)}, bf16[2,3,8,384]{3,2,1,0:T(8,128)(2,1)}, u32[]{:S(2)}, u32[]{:S(2)}) collective-permute-start(bf16[2,3,8,384]{3,2,1,0:T(8,128)(2,1)} %get-tuple-element.12), channel_id=1, source_target_pairs={{8,272},{16,264},{24,288},{32,280},{40,304},{48,296},{56,320},{64,... | collective-permute-start | bytes 110600 | tf_op jit(solution)/shard_map/ppermute | solution.py:383
  11.3 11.9 %collective-permute-start.2 = (bf16[2,3,8,384]{3,2,1,0:T(8,128)(2,1)}, bf16[2,3,8,384]{3,2,1,0:T(8,128)(2,1)}, u32[]{:S(2)}, u32[]{:S(2)}) collective-permute-start(bf16[2,3,8,384]{3,2,1,0:T(8,128)(2,1)} %get-tuple-element.12), channel_id=1, source_target_pairs={{0,264},{8,256},{16,280},{24,272},{32,296},{40,288},{48,312},{56,3... | collective-permute-start | bytes 110600 | tf_op jit(solution)/shard_map/ppermute | solution.py:382
  18.2 5.0 %collective-permute-start = (bf16[2,3,8,384]{3,2,1,0:T(8,128)(2,1)}, bf16[2,3,8,384]{3,2,1,0:T(8,128)(2,1)}, u32[]{:S(2)}, u32[]{:S(2)}) collective-permute-start(bf16[2,3,8,384]{3,2,1,0:T(8,128)(2,1)} %get-tuple-element.12), channel_id=1, source_target_pairs={{0,256},{256,0},{1,257},{257,1},{2,258},{258,2},{3,259},{259,3},{4... | collective-permute-start | bytes 110600 | tf_op jit(solution)/shard_map/ppermute | solution.py:381
  23.3 24.1 %copy-start = (bf16[384,1024]{1,0:T(8,128)(2,1)S(1)}, bf16[384,1024]{1,0:T(8,128)(2,1)}, u32[]{:S(2)}) copy-start(bf16[384,1024]{1,0:T(8,128)(2,1)} %emb_hbm.5) | copy-start | bytes 2359300
  23.3 24.1 %copy-start.6 = (bf16[1024,256]{1,0:T(8,128)(2,1)S(1)}, bf16[1024,256]{1,0:T(8,128)(2,1)}, u32[]{:S(2)}) copy-start(bf16[1024,256]{1,0:T(8,128)(2,1)} %v_hbm.3) | copy-start | bytes 1572868
  23.3 24.1 %copy-start.7 = (bf16[1024,256]{1,0:T(8,128)(2,1)S(1)}, bf16[1024,256]{1,0:T(8,128)(2,1)}, u32[]{:S(2)}) copy-start(bf16[1024,256]{1,0:T(8,128)(2,1)} %u_hbm.3) | copy-start | bytes 1572868
  31.2 28.5 %all-to-all-start = ((f32[16,2,1152]{2,1,0:T(2,128)}), f32[16,2,1152]{2,1,0:T(2,128)S(1)}, u32[]{:S(2)}, u32[]{:S(2)}) async-start(f32[16,2,1152]{2,1,0:T(2,128)} %get-tuple-element.15), calls=%async_computation | async-start | bytes 294912 | tf_op jit(solution)/shard_map/all_to_all | solution.py:449
  47.4 1.1 %copy-start.2 = (bf16[384,1024]{1,0:T(8,128)(2,1)S(1)}, bf16[384,1024]{1,0:T(8,128)(2,1)}, u32[]{:S(2)}) copy-start(bf16[384,1024]{1,0:T(8,128)(2,1)} %get-tuple-element.18.slope) | copy-start | bytes 2359300
  48.5 0.9 %copy-start.8 = (bf16[384,256]{1,0:T(8,128)(2,1)S(1)}, bf16[384,256]{1,0:T(8,128)(2,1)}, u32[]{:S(2)}) copy-start(bf16[384,256]{1,0:T(8,128)(2,1)} %get-tuple-element.16.gate_v) | copy-start | bytes 589828
  49.5 0.9 %copy-start.9 = (bf16[384,256]{1,0:T(8,128)(2,1)S(1)}, bf16[384,256]{1,0:T(8,128)(2,1)}, u32[]{:S(2)}) copy-start(bf16[384,256]{1,0:T(8,128)(2,1)} %get-tuple-element.17.gate_u) | copy-start | bytes 589828
  50.4 29.1 %copy-start.4 = (f32[384,128]{1,0:T(8,128)S(1)}, f32[384,128]{1,0:T(8,128)}, u32[]{:S(2)}) copy-start(f32[384,128]{1,0:T(8,128)} %get-tuple-element.20.weight) | copy-start | bytes 589828
  51.9 27.6 %copy-start.1 = (bf16[384,1024]{1,0:T(8,128)(2,1)S(1)}, bf16[384,1024]{1,0:T(8,128)(2,1)}, u32[]{:S(2)}) copy-start(bf16[384,1024]{1,0:T(8,128)(2,1)} %get-tuple-element.19.embedded) | copy-start | bytes 2359300
  51.9 27.6 %copy-start.3 = (bf16[384,1024]{1,0:T(8,128)(2,1)S(1)}, bf16[384,1024]{1,0:T(8,128)(2,1)}, u32[]{:S(2)}) copy-start(bf16[384,1024]{1,0:T(8,128)(2,1)} %get-tuple-element.18.slope) | copy-start | bytes 2359300
  51.9 27.6 %copy-start.5 = (s32[16]{0:T(128)S(1)}, s32[16]{0:T(128)}, u32[]{:S(2)}) copy-start(s32[16]{0:T(128)} %param.17) | copy-start | bytes 196
